TPU v7x, 256 devices: a whole 4x4x8 slice. The times are simulated.
256 devices in a mesh: ctx: 32 (over y, z), head: 8 (over x, core).
Axes of the slice: x: 4, y: 4, z: 8, core: 2. Of those that a mesh axis runs over, the one named last changes fastest.
Arguments:
- queries: bfloat16 [32768, 4096], P('ctx', 'head'), may hold values from -6 to 6
- keys: bfloat16 [32768, 4096], P('ctx', 'head'), may hold values from -0.5 to 0.5
- values: bfloat16 [32768, 2048], P('ctx', 'head'), may hold values from -120 to 120
- norm_gain: bfloat16 [2048], P('head'), may hold values from 0.099609375 to 1.8984375
- level_index: int32 [10, 32, 32768], P(None, 'head', 'ctx'), may hold values from 1 to 256
Outputs:
- attended: bfloat16 [32768, 2048], P('ctx', 'head')
All inputs are finite; a program needn't handle non-finite values.
Results may differ from a plain program's by a relative error of at most 0.0049.
Values sent between devices are 32-bit elements; how exact they have to be, the bound alone decides.
No kernel may reach another device: no remote copies, remote signals or barrier semaphores. Data moves between devices by JAX's collectives and lax.ppermute only.
A program may use at most 64 MiB of HBM per device.

v0:
```python
import jax
import jax.numpy as jnp
from jax import lax
from jax.sharding import PartitionSpec as P

H = 32
DK = 128
DV = 64
STRETCH = 64


def level_factor(weights, level_id, span_tokens):
    return (weights[level_id].T * float(span_tokens) ** (-0.5))[:, :, None]


def on_device(queries, keys, values, norm_gain, level_index):
    tokens_here = queries.shape[0]
    head_count = queries.shape[1] // DK
    stretches = tokens_here // STRETCH
    stretch_bits = stretches.bit_length() - 1
    ctx_bits = lax.axis_size("ctx").bit_length() - 1
    query_rows = queries.reshape(tokens_here, head_count, DK)
    query_blocks = queries.reshape(stretches, STRETCH, head_count, DK)
    key_blocks = keys.reshape(stretches, STRETCH, head_count, DK)
    value_blocks = values.reshape(stretches, STRETCH, head_count, DV)
    weights = level_index.astype(jnp.float32) / 256.0
    scores = jnp.einsum(
        "cihd,cjhd->chij", query_blocks, key_blocks, preferred_element_type=jnp.float32
    )
    causal = jnp.arange(STRETCH)[:, None] >= jnp.arange(STRETCH)[None, :]
    scores_low = jnp.where(causal, scores, 0.0).astype(jnp.bfloat16)
    intra = jnp.einsum(
        "chij,cjhe->cihe", scores_low, value_blocks, preferred_element_type=jnp.float32
    )
    mixed = intra.reshape(tokens_here, head_count, DV) * level_factor(weights, 0, STRETCH)
    block_sums = jnp.einsum(
        "cjhd,cjhe->chde", key_blocks, value_blocks, preferred_element_type=jnp.float32
    )
    for bit_pos in range(stretch_bits):
        groups = stretches >> bit_pos + 1
        width_rows = 2**bit_pos * STRETCH
        paired = block_sums.reshape(groups, 2, head_count, DK, DV)
        lower_half = paired[:, 0].astype(jnp.bfloat16)
        upper_rows = query_rows.reshape(groups, 2, width_rows, head_count, DK)[:, 1]
        factor = level_factor(weights, 1 + bit_pos, width_rows).reshape(
            groups, 2, width_rows, head_count, 1
        )[:, 1]
        level_term = (
            jnp.einsum(
                "gthd,ghde->gthe", upper_rows, lower_half, preferred_element_type=jnp.float32
            )
            * factor
        )
        mixed = mixed.reshape(groups, 2, width_rows, head_count, DV).at[:, 1].add(level_term)
        mixed = mixed.reshape(tokens_here, head_count, DV)
        block_sums = jnp.sum(paired, axis=1)
    shard_state = block_sums[0]
    self_rank = lax.axis_index("ctx")
    shard_rows = lax.all_gather(shard_state[None], "ctx", axis=0, tiled=True)
    ranks = jnp.arange(shard_rows.shape[0], dtype=jnp.int32)
    updated = []
    for fold_bit_pos in range(ctx_bits):
        bit_set = self_rank >> fold_bit_pos & 1
        block_base = (self_rank >> fold_bit_pos + 1) * 2
        member = (ranks >> fold_bit_pos == block_base) & (bit_set == 1)
        added = jnp.sum(jnp.where(member[:, None, None, None], shard_rows, 0.0), axis=0)
        updated.append(added)
    states = list(tuple(updated))
    far_states = jnp.stack(states).astype(jnp.bfloat16)
    far_terms = jnp.einsum(
        "thd,bhde->bthe", query_rows, far_states, preferred_element_type=jnp.float32
    )
    for bit_pos in range(ctx_bits):
        span_tokens = tokens_here * 2**bit_pos
        mixed = mixed + far_terms[bit_pos] * level_factor(
            weights, 1 + stretch_bits + bit_pos, span_tokens
        )
    flat = mixed.reshape(tokens_here, head_count * DV)
    square_sum = lax.psum(jnp.sum(flat * flat, axis=1), "head")
    inv_rms = lax.rsqrt(square_sum / (H * DV) + 1e-06)
    return (flat * inv_rms[:, None] * norm_gain.astype(jnp.float32)).astype(jnp.bfloat16)


def solution(mesh):
    in_specs = (
        P("ctx", "head"),
        P("ctx", "head"),
        P("ctx", "head"),
        P("head"),
        P(None, "head", "ctx"),
    )
    out_specs = P("ctx", "head")
    return jax.shard_map(
        on_device, mesh=mesh, in_specs=in_specs, out_specs=out_specs, check_vma=False
    )
```

profile of v0, /device:TPU:1, one launch (start us, length us, event | category | flops | bytes accessed | tf_op | source)
XLA Modules:
  0.0 146.8 jit_solution(5509571672758845506)
XLA Ops:
  6.5 2.1 %reshape.348 = bf16[16,64,4,64]{3,2,1,0:T(4,128)(2,1)S(1)} reshape(bf16[1024,256]{1,0:T(8,128)(2,1)} %param.15) | data formatting | bytes 1048576 | tf_op jit(solution)/shard_map/reshape | solution.py:25
  8.7 1.4 copy.74
  10.0 1.1 reshape.347
  11.1 2.7 %fusion.60 = (f32[4,128,64]{1,2,0:T(8,128)}, f32[16,4,128,64]{2,3,1,0:T(8,128)S(1)}) fusion(bf16[16,64,4,64]{1,3,2,0:T(8,128)(2,1)} %copy.74, bf16[16,64,4,128]{3,2,1,0:T(4,128)(2,1)} %reshape.347), kind=kOutput, calls=%fused_computation.118 | convolution fusion | flops 67600384 | bytes 3801088 | tf_op jit(solution)/shard_map/cjhd,cjhe->chde/dot_general | solution.py:36
  13.9 1.1 reshape.346
  15.0 1.2 reshape_reshape.21
  16.2 1.1 reshape_reshape.23
  17.3 1.1 reshape_reshape.25
  18.4 1.1 reshape_reshape.27
  19.5 1.2 reshape.360
  20.9 4.4 %fusion = f32[16,4,64,64]{3,2,1,0:T(8,128)} fusion(bf16[16,64,4,64]{1,3,2,0:T(8,128)(2,1)} %copy.74, bf16[16,64,4,128]{3,2,1,0:T(4,128)(2,1)} %reshape.346, pred[64,64]{1,0:T(8,128)(4,1)S(1)} %iota_compare_fusion, bf16[16,64,4,128]{3,2,1,0:T(4,128)(2,1)} %reshape.347), kind=kOutput, calls=%fused_computation.7 | convolution fusion | flops 101187584 | bytes 3674112 | tf_op jit(solution)/shard_map/chij,cjhe->cihe/dot_general | solution.py:32
  25.3 2.9 %copy.72 = f32[8,2,64,4,64]{2,4,3,0,1:T(8,128)} copy(f32[8,2,64,4,64]{4,2,3,1,0:T(8,128)} %bitcast.287) | data formatting | bytes 2097152 | tf_op jit(solution)/shard_map/reshape | solution.py:35
  28.4 1.9 %broadcast_multiply_fusion = f32[8,2,64,4,64]{2,4,3,0,1:T(8,128)S(1)} fusion(f32[8,2,64,4,64]{2,4,3,0,1:T(8,128)} %copy.72, f32[8,2,64,4]{2,3,0,1:T(4,128)S(1)} %copy.71), kind=kLoop, calls=%fused_computation.58 | loop fusion | flops 262144 | bytes 2113536 | tf_op jit(solution)/shard_map/mul | solution.py:35
  30.8 3.0 %copy.78 = f32[8,2,64,4,64]{2,1,4,3,0:T(2,128)} copy(f32[8,2,64,4,64]{2,4,3,0,1:T(8,128)S(1)} %fusion.4) | data formatting | bytes 2097152 | tf_op jit(solution)/shard_map/scatter-add | solution.py:54
  33.8 3.3 %reshape_reshape.22 = f32[4,2,128,4,64]{2,4,3,1,0:T(8,128)} reshape(f32[8,2,64,4,64]{2,1,4,3,0:T(2,128)} %copy.78) | data formatting | bytes 2097152 | tf_op jit(solution)/shard_map/reshape;reshape | solution.py:54
  37.4 1.0 copy-done.1
  39.8 0.8 reshape_reshape.24
  42.8 0.8 reshape_reshape.26
  45.2 1.2 copy.121
  46.4 50.6 %all-gather.3.cloned.1.call-done = f32[128,128,64]{1,2,0:T(8,128)} async-done(((f32[4,128,64]{1,2,0:T(8,128)}), f32[128,128,64]{1,2,0:T(8,128)}) %all-gather.3.cloned.1.call-update) | async-done | bytes 4194320 | tf_op jit(solution)/shard_map/all_gather | solution.py:59
  97.0 4.6 %select_reduce_fusion = (bf16[4,128,64]{1,2,0:T(8,128)(2,1)S(1)}, bf16[4,128,64]{1,2,0:T(8,128)(2,1)S(1)}, bf16[4,128,64]{1,2,0:T(8,128)(2,1)S(1)}, bf16[4,128,64]{1,2,0:T(8,128)(2,1)S(1)}, bf16[4,128,64]{1,2,0:T(8,128)(2,1)S(1)}) fusion(f32[32,4,128,64]{2,3,1,0:T(8,128)} %bitcast.291, pred[32]{0:T(512)(128)(4,1)S(1)} %get-tuple-element.80, ...), kind=kLoop, calls=%fused_computation | loop fusion | flops 10321920 | bytes 4522144 | tf_op jit(solution)/shard_map/reduce_sum | solution.py:66
  101.7 0.8 convolution_bitcast_fusion
  102.5 1.9 %fusion.59 = (f32[1,1024,4,64]{1,3,0,2:T(8,128)S(1)}, f32[1,1024,4,64]{1,3,0,2:T(8,128)S(1)}, f32[1,1024,4,64]{1,3,0,2:T(8,128)}, f32[1,1024,4,64]{1,3,0,2:T(8,128)}, f32[1,1024,4,64]{1,3,0,2:T(8,128)}) fusion(f32[5,1024,4,64]{1,3,0,2:T(8,128)S(1)} %convolution_bitcast_fusion), kind=kLoop, calls=%fused_computation.117 | loop fusion | bytes 10485760 | tf_op jit(solution)/shard_map/slice | solution.py:75
  104.4 2.0 %squeeze.61 = f32[1,2,512,4,64]{2,1,4,3,0:T(2,128)} reshape(f32[1,1024,4,64]{1,3,0,2:T(8,128)S(1)} %get-tuple-element.58) | data formatting | bytes 2097152 | tf_op jit(solution)/shard_map/squeeze | solution.py:75
  106.3 3.1 %squeeze.62 = f32[1,2,512,4,64]{2,1,4,3,0:T(2,128)} reshape(f32[1,1024,4,64]{1,3,0,2:T(8,128)} %get-tuple-element.62) | data formatting | bytes 2097152 | tf_op jit(solution)/shard_map/squeeze | solution.py:75
  109.4 3.1 %squeeze.63 = f32[1,2,512,4,64]{2,1,4,3,0:T(2,128)} reshape(f32[1,1024,4,64]{1,3,0,2:T(8,128)} %get-tuple-element.61) | data formatting | bytes 2097152 | tf_op jit(solution)/shard_map/squeeze | solution.py:75
  112.5 3.1 %squeeze.64 = f32[1,2,512,4,64]{2,1,4,3,0:T(2,128)} reshape(f32[1,1024,4,64]{1,3,0,2:T(8,128)} %get-tuple-element.60) | data formatting | bytes 2097152 | tf_op jit(solution)/shard_map/squeeze | solution.py:75
  115.7 1.9 %squeeze.65 = f32[1,2,512,4,64]{2,1,4,3,0:T(2,128)} reshape(f32[1,1024,4,64]{1,3,0,2:T(8,128)S(1)} %get-tuple-element.59) | data formatting | bytes 2097152 | tf_op jit(solution)/shard_map/squeeze | solution.py:75
  117.5 3.4 %fusion.30 = f32[2,512]{1,0:T(2,128)S(1)} fusion(f32[1,2,512,4,64]{2,1,4,3,0:T(2,128)} %squeeze.65, f32[1,2,512,4,64]{2,1,4,3,0:T(2,128)} %squeeze.64, f32[1,2,512,4,64]{2,1,4,3,0:T(2,128)} %squeeze.63, f32[1,2,512,4,64]{2,1,4,3,0:T(2,128)} %squeeze.62, f32[1,2,512,4,64]{2,4,3,1,0:T(8,128)S(1)} %fusion.18, f32[1,2,512,4,64]{2,1,4,3,0:T(2,128)} %squeeze.61, ...), kind=kLoop, calls=%fused_computation.48 | loop fusion | flops 3144704 | bytes 6377472 | tf_op jit(solution)/shard_map/reduce_sum | solution.py:79
  120.9 15.1 %psum.7 = f32[1024]{0:T(1024)S(1)} all-reduce(f32[1024]{0:T(1024)S(1)} %bitcast.304), channel_id=1, replica_groups=mesh['ctx'=32,'head'=8] {'head'}, use_global_device_ids=true, to_apply=%region_10.11 | all-reduce | flops 1024 | bytes 8192 | tf_op jit(solution)/shard_map/psum | solution.py:79
  136.0 2.9 %fusion.22 = bf16[1024,256]{0,1:T(8,128)(2,1)S(1)} fusion(f32[1,1024,4,64]{1,3,0,2:T(8,128)S(1)} %get-tuple-element.59, f32[1,1024,4,64]{1,3,0,2:T(8,128)} %get-tuple-element.60, f32[1,1024,4,64]{1,3,0,2:T(8,128)} %get-tuple-element.61, f32[1,1024,4,64]{1,3,0,2:T(8,128)} %get-tuple-element.62, f32[1024,256]{0,1:T(8,128)} %bitcast.290, ...), kind=kLoop, calls=%fused_computation.35 | loop fusion | flops 3407872 | bytes 6902784 | tf_op jit(solution)/shard_map/convert_element_type | solution.py:81
  138.9 1.0 copy.105
  (63 shorter events, 6.1 us)
Async XLA Ops:
  6.5 3.5 %copy-start.5 = (bf16[1024,512]{1,0:T(8,128)(2,1)S(1)}, bf16[1024,512]{1,0:T(8,128)(2,1)}, u32[]{:S(2)}) copy-start(bf16[1024,512]{1,0:T(8,128)(2,1)} %param.14) | copy-start | bytes 3145732
  6.5 90.5 %all-gather.3.cloned.1.call-start = ((), (), s32[]{:S(2)}) async-start(), calls=%async_computation | async-start | bytes 4325376 | tf_op jit(solution)/shard_map/all_gather | solution.py:59
  11.1 2.7 %copy-start = (bf16[1024,512]{1,0:T(8,128)(2,1)S(1)}, bf16[1024,512]{1,0:T(8,128)(2,1)}, u32[]{:S(2)}) copy-start(bf16[1024,512]{1,0:T(8,128)(2,1)} %param.13) | copy-start | bytes 3145732
  18.4 2.3 %copy-start.6 = (s32[10,4,1024]{2,1,0:T(4,128)S(1)}, s32[10,4,1024]{2,1,0:T(4,128)}, u32[]{:S(2)}) copy-start(s32[10,4,1024]{2,1,0:T(4,128)} %param.17) | copy-start | bytes 491524
  28.4 2.0 %slice-start.3 = ((bf16[8,2,64,4,128]{4,3,2,1,0:T(4,128)(2,1)}), bf16[8,1,64,4,128]{4,3,2,1,0:T(4,128)(2,1)S(1)}, s32[]{:S(2)}) async-start(bf16[8,2,64,4,128]{4,3,2,1,0:T(4,128)(2,1)} %reshape_reshape.21), calls=%async_computation.4 | async-start | bytes 1048576 | tf_op jit(solution)/shard_map/slice | solution.py:44
  37.1 1.2 copy-start.1
  37.2 1.3 slice-start.2
  40.6 1.0 slice-start.1
  40.8 0.8 copy-start.3
  42.8 1.0 copy-start.4
  42.8 1.2 slice-start
  44.3 2.0 %copy-start.7 = (bf16[256]{0:T(256)(128)(2,1)S(1)}, bf16[256]{0:T(256)(128)(2,1)}, u32[]{:S(2)}) copy-start(bf16[256]{0:T(256)(128)(2,1)} %param.16) | copy-start | bytes 1540
  97.0 4.7 %copy-start.2 = (bf16[1024,4,128]{2,1,0:T(4,128)(2,1)S(1)}, bf16[1024,4,128]{2,1,0:T(4,128)(2,1)}, u32[]{:S(2)}) copy-start(bf16[1024,4,128]{2,1,0:T(4,128)(2,1)} %reshape.360) | copy-start | bytes 3145732
Sparse Core Ops, SparseCore 0:
  14.0 82.9 all-gather.2
where the time goes:
time: 147 us
  waiting for transfers between devices  50.6 us (34%)
  local copies, waits for them, and re-layouts  44.6 us (30%)
  blocking collectives  15.1 us (10%)
  between operations  13.8 us (9%)
  other arithmetic  13.2 us (9%)
  matrix products  9.47 us (6%)
    all_gather x1, waiting for transfers between devices, on_device(): shard_rows = lax.all_gather(shard_state[None], 'ctx', axis=0, tiled=True)  50.6 us
    psum x1, blocking collectives, on_device(): square_sum = lax.psum(jnp.sum(flat * flat, axis=1), 'head')  15.1 us
    squeeze x5, local copies, waits for them, and re-layouts, on_device(): far_terms[bit_pos]  13.2 us
    scatter-add x4, local copies, waits for them, and re-layouts, on_device(): mixed.reshape(groups, 2, width_rows, head_count, DV).at[:, 1]  5.41 us
    another operation x3, local copies, waits for them, and re-layouts, on_device(): mixed.reshape(groups, 2, width_rows, head_count, DV).at[:, 1]  5.01 us
    reduce_sum x1, other arithmetic, on_device(): jnp.sum(jnp.where(member[:, None, None, None], shard_rows, 0.0), axis=0)  4.55 us
    another operation x4, local copies, waits for them, and re-layouts, on_device(): upper_rows = query_rows.reshape(groups, 2, width_rows, head_count, DK)[:, 1]  4.48 us
    dot_general x1, matrix products, on_device(): jnp.einsum('chij,cjhe->cihe', scores_low, value_blocks, preferred_element...  4.43 us
  transfers between devices with their start and end apart: 1, of which 1 were waited for; matrix products, arithmetic and copies ran while one was open for 20% of the time, Pallas kernels for 0%

commit v1 on v0

v1 whole, which is shorter than its diff:
```python
import functools

import jax
import jax.numpy as jnp
from jax import lax
from jax.experimental import pallas as pl
from jax.experimental.pallas import tpu as pltpu
from jax.sharding import PartitionSpec as P

H = 32
DK = 128
DV = 64
STRETCH = 64
HEADS = 4
TOK = 1024
BLK = 256
Z = 8
VMEM_LIMIT = 32 * 1024 * 1024

NT = (((1,), (1,)), ((), ()))
NN = (((1,), (0,)), ((), ()))


def dot(a, b, dims):
    return lax.dot_general(a, b, dims, preferred_element_type=jnp.float32)


def weight_scale(level):
    span = STRETCH if level == 0 else STRETCH * 2 ** (level - 1)
    return float(span) ** (-0.5) / 256.0


def weight_row(li_ref, level, head, start, size):
    row = li_ref[level, head : head + 1, start : start + size]
    return row.astype(jnp.float32) * weight_scale(level)


def summary_kernel(k_ref, v_ref, s_ref):
    vt = v_ref[...].T
    for h in range(HEADS):
        s_ref[h * DV : (h + 1) * DV, :] = dot(
            vt[h * DV : (h + 1) * DV, :], k_ref[:, h * DK : (h + 1) * DK], NN
        )


def local_kernel(first_head, heads, q_ref, k_ref, v_ref, li_ref, m_ref):
    lane = lax.broadcasted_iota(jnp.int32, (1, BLK), 1)
    t_stretch = lane // STRETCH
    row = lax.broadcasted_iota(jnp.int32, (BLK, BLK), 0)
    col = lax.broadcasted_iota(jnp.int32, (BLK, BLK), 1)
    causal = (row // STRETCH == col // STRETCH) & (row <= col)
    zero = jnp.zeros((), jnp.bfloat16)
    vt_all = v_ref[...].T
    for h in range(heads):
        wh = first_head + h
        before = None
        first_half = None
        for b in range(TOK // BLK):
            r0 = b * BLK
            q = q_ref[r0 : r0 + BLK, h * DK : (h + 1) * DK]
            k = k_ref[r0 : r0 + BLK, h * DK : (h + 1) * DK]
            vt = vt_all[h * DV : (h + 1) * DV, r0 : r0 + BLK]
            sums = dot(
                jnp.concatenate(
                    [
                        jnp.where(t_stretch == 0, vt, zero),
                        jnp.where(t_stretch == 2, vt, zero),
                        jnp.where(t_stretch < 2, vt, zero),
                        vt,
                    ],
                    axis=0,
                ),
                k,
                NN,
            )
            total = sums[3 * DV :]
            rows = [k, sums[: 3 * DV].astype(jnp.bfloat16)]
            if b % 2 == 1:
                rows.append(before.astype(jnp.bfloat16))
            if b >= 2:
                rows.append(first_half.astype(jnp.bfloat16))
            prod = dot(jnp.concatenate(rows, axis=0), q, NT)
            low = jnp.where(causal, prod[:BLK], 0.0).astype(jnp.bfloat16)
            mix = dot(vt, low, NN) * weight_row(li_ref, 0, wh, r0, BLK)
            part = [prod[BLK + i * DV : BLK + (i + 1) * DV] for i in range(len(rows) + 1)]
            near = jnp.where(
                t_stretch == 1, part[0], jnp.where(t_stretch == 3, part[1], 0.0)
            )
            mix = mix + near * weight_row(li_ref, 1, wh, r0, BLK)
            mix = mix + jnp.where(t_stretch >= 2, part[2], 0.0) * weight_row(
                li_ref, 2, wh, r0, BLK
            )
            at = 3
            if b % 2 == 1:
                mix = mix + part[at] * weight_row(li_ref, 3, wh, r0, BLK)
                at += 1
            if b >= 2:
                mix = mix + part[at] * weight_row(li_ref, 4, wh, r0, BLK)
            m_ref[h * DV : (h + 1) * DV, r0 : r0 + BLK] = mix
            if b == 1:
                first_half = before + total
            before = total


def far_mix(h, rank, bits, states, q_ref, li_ref):
    rows = jnp.concatenate(
        [s[h * DV : (h + 1) * DV, :].astype(jnp.bfloat16) for s in states], axis=0
    )
    prod = dot(rows, q_ref[:, h * DK : (h + 1) * DK], NT)
    mix = None
    for i, bit in enumerate(bits):
        has = (rank >> bit) & 1
        w = jnp.where(has == 1, weight_row(li_ref, 5 + bit, h, 0, TOK), 0.0)
        term = prod[i * DV : (i + 1) * DV] * w
        mix = term if mix is None else mix + term
    return mix


def far_kernel(bits, q_ref, li_ref, *refs):
    state_refs, m_in, m_ref = refs[: len(bits)], refs[len(bits) : -1], refs[-1]
    rank = lax.axis_index("ctx")
    states = [r[...] for r in state_refs]
    per = HEADS // len(m_in)
    for h in range(HEADS):
        at = (h % per) * DV
        mix = far_mix(h, rank, bits, states, q_ref, li_ref)
        m_ref[h * DV : (h + 1) * DV, :] = m_in[h // per][at : at + DV, :] + mix


def last_kernel(q_ref, li_ref, l2_ref, a_ref, b_ref, c_ref, m_in, m_ref, ss_ref):
    rank = lax.axis_index("ctx")
    both = rank // Z == 3
    l4 = b_ref[...] + jnp.where(both, c_ref[...], a_ref[...])
    states = [l2_ref[...], a_ref[...], l4]
    squares = None
    for h in range(HEADS):
        mix = m_in[h * DV : (h + 1) * DV, :] + far_mix(
            h, rank, (2, 3, 4), states, q_ref, li_ref
        )
        m_ref[h * DV : (h + 1) * DV, :] = mix
        sq = jnp.sum(mix * mix, axis=0, keepdims=True)
        squares = sq if squares is None else squares + sq
    for i in range(TOK // 128):
        ss_ref[i : i + 1, :] = squares[:, i * 128 : (i + 1) * 128]


def norm_kernel(m_ref, g_ref, s0, s1, s2, s3, out_ref):
    total = (s0[...] + s1[...]) + (s2[...] + s3[...])
    inv = lax.rsqrt(total / (H * DV) + 1e-06)
    gain = g_ref[...].astype(jnp.float32)
    for i in range(TOK // 128):
        x = m_ref[:, i * 128 : (i + 1) * 128] * inv[i : i + 1, :]
        out_ref[i * 128 : (i + 1) * 128, :] = (x.T * gain).astype(jnp.bfloat16)


def call(kernel, outs, n_in, flops=0, moved=0, in_specs=None, name=None):
    whole = pl.BlockSpec(memory_space=pltpu.VMEM)
    return pl.pallas_call(
        kernel,
        out_shape=outs,
        in_specs=in_specs or [whole] * n_in,
        out_specs=jax.tree.map(lambda _: whole, outs),
        compiler_params=pltpu.CompilerParams(vmem_limit_bytes=VMEM_LIMIT),
        cost_estimate=pl.CostEstimate(flops=flops, bytes_accessed=moved, transcendentals=0),
        name=name,
    )


def f32(*shape):
    return jax.ShapeDtypeStruct(shape, jnp.float32)


def on_device(queries, keys, values, norm_gain, level_index):
    ctx = lax.axis_size("ctx")
    ys = ctx // Z
    state = f32(HEADS * DV, DK)
    mixed = f32(HEADS * DV, TOK)

    def over_ctx(x, move):
        pairs = [(r, move(r // Z, r % Z)) for r in range(ctx)]
        return lax.ppermute(x, "ctx", [(r, y * Z + z) for r, (y, z) in pairs if y < ys])

    own = call(summary_kernel, state, 2, 268_000_000, 1_700_000, name="summary")(keys, values)
    l0 = over_ctx(own, lambda y, z: (y, z ^ 1))
    pair = own + l0
    l1 = over_ctx(pair, lambda y, z: (y, z ^ 2))
    quad = pair + l1
    hop = (6, 7, 4, 5, 2, 3, 0, 1)
    l2 = over_ctx(quad, lambda y, z: (y, hop[z]))
    group = quad + l2
    up1 = over_ctx(group, lambda y, z: (y + 1, z))
    up2 = over_ctx(group, lambda y, z: (y + 2, z))
    up3 = over_ctx(group, lambda y, z: (y + 3, z))

    half = HEADS // 2
    parts = []
    for p in range(2):
        specs = [
            pl.BlockSpec((TOK, half * DK), lambda i, p=p: (0, p)),
            pl.BlockSpec((TOK, half * DK), lambda i, p=p: (0, p)),
            pl.BlockSpec((TOK, half * DV), lambda i, p=p: (0, p)),
            pl.BlockSpec(level_index.shape, lambda i: (0, 0, 0)),
        ]
        parts.append(
            pl.pallas_call(
                functools.partial(local_kernel, p * half, half),
                grid=(1,),
                out_shape=f32(half * DV, TOK),
                in_specs=specs,
                out_specs=pl.BlockSpec((half * DV, TOK), lambda i: (0, 0)),
                compiler_params=pltpu.CompilerParams(vmem_limit_bytes=VMEM_LIMIT),
                cost_estimate=pl.CostEstimate(
                    flops=1_000_000_000, bytes_accessed=2_000_000, transcendentals=0
                ),
                name="local%d" % p,
            )(queries, keys, values, level_index)
        )
    near = call(
        functools.partial(far_kernel, (0, 1)), mixed, 6, 134_000_000, 3_000_000, name="far01"
    )(queries, level_index, l0, l1, *parts)
    flat, squares = call(
        last_kernel, (mixed, f32(8, 128)), 7, 200_000_000, 3_000_000, name="last"
    )(queries, level_index, l2, up1, up2, up3, near)

    squares = squares + lax.ppermute(squares, "head", [(i, i ^ 1) for i in range(8)])
    others = [
        lax.ppermute(squares, "head", [(i, (i + 2 * n) % 8) for i in range(8)]) for n in (1, 3, 2)
    ]
    return call(
        norm_kernel,
        jax.ShapeDtypeStruct((TOK, HEADS * DV), jnp.bfloat16),
        6,
        1_000_000,
        1_500_000,
        name="norm",
    )(flat, norm_gain.reshape(1, HEADS * DV), squares, *others)


def solution(mesh):
    in_specs = (
        P("ctx", "head"),
        P("ctx", "head"),
        P("ctx", "head"),
        P("head"),
        P(None, "head", "ctx"),
    )
    out_specs = P("ctx", "head")
    return jax.shard_map(
        on_device, mesh=mesh, in_specs=in_specs, out_specs=out_specs, check_vma=False
    )
```

time: 147 us -> 52.6 us (0.36)
  the two profiles are of different devices: /device:TPU:1 before, /device:TPU:64 now
where the time goes in v1:
time: 52.6 us; the launch traced here: 52.5 us
  starting transfers between devices  24.4 us (46%)
  waiting for transfers between devices  18.8 us (36%)
  Pallas kernels  6.73 us (13%)
  local copies, waits for them, and re-layouts  2.37 us (5%)
    ppermute x6, starting transfers between devices, over_ctx(): lax.ppermute(x, 'ctx', [(r, y * Z + z) for r, (y, z) in pairs if y < ys])  19.2 us
    ppermute x6, waiting for transfers between devices, over_ctx(): lax.ppermute(x, 'ctx', [(r, y * Z + z) for r, (y, z) in pairs if y < ys])  14.3 us
    ppermute x3, starting transfers between devices, on_device(): lax.ppermute(squares, 'head', [(i, (i + 2 * n) % 8) for i in range(8)])  5.05 us
    pallas_call x2, Pallas kernels, on_device(): pl.pallas_call(functools.partial(local_kernel, p * half, half), grid=(1,)...  4.18 us
    ppermute x3, waiting for transfers between devices, on_device(): lax.ppermute(squares, 'head', [(i, (i + 2 * n) % 8) for i in range(8)])  3.29 us
    unnamed x10, local copies, waits for them, and re-layouts  2.37 us
    ppermute x1, waiting for transfers between devices, on_device(): lax.ppermute(squares, 'head', [(i, i ^ 1) for i in range(8)])  1.15 us
    pallas_call x1, Pallas kernels, on_device(): call(norm_kernel, jax.ShapeDtypeStruct((TOK, HEADS * DV), jnp.bfloat16),...  1.14 us
  transfers between devices with their start and end apart: 10, of which 5 were waited for; matrix products, arithmetic and copies ran while one was open for 0% of the time, Pallas kernels for 9%

profile of v1, /device:TPU:64, one launch (start us, length us, event | category | flops | bytes accessed | tf_op | source)
XLA Modules:
  0.0 52.5 jit_solution(11711623790920468820)
XLA Ops:
  0.0 1.3 %copy-done.1 = bf16[1024,512]{1,0:T(8,128)(2,1)S(1)} copy-done((bf16[1024,512]{1,0:T(8,128)(2,1)S(1)}, bf16[1024,512]{1,0:T(8,128)(2,1)}, u32[]{:S(2)}) %copy-start.1) | copy-done | bytes 1048600
  1.3 1.0 %copy-done.3 = bf16[1024,256]{1,0:T(8,128)(2,1)S(1)} copy-done((bf16[1024,256]{1,0:T(8,128)(2,1)S(1)}, bf16[1024,256]{1,0:T(8,128)(2,1)}, u32[]{:S(2)}) %copy-start.3) | copy-done | bytes 524312
  2.4 0.3 summary.1
  2.7 2.0 %collective-permute-start = (f32[256,128]{1,0:T(8,128)S(1)}, f32[256,128]{1,0:T(8,128)S(1)}, u32[]{:S(2)}, u32[]{:S(2)}) collective-permute-start(f32[256,128]{1,0:T(8,128)S(1)} %summary.1), channel_id=1, source_target_pairs={{0,8},{8,0},{16,24},{24,16},{32,40},{40,32},{48,56},{56,48},{64,72... | collective-permute-start | bytes 393224 | tf_op jit(solution)/shard_map/ppermute | solution.py:181
  4.7 3.5 %collective-permute-done.refs_0_ = f32[256,128]{1,0:T(8,128)S(1)} collective-permute-done((f32[256,128]{1,0:T(8,128)S(1)}, f32[256,128]{1,0:T(8,128)S(1)}, u32[]{:S(2)}, u32[]{:S(2)}) %collective-permute-start) | collective-permute-done | bytes 131104 | tf_op jit(solution)/shard_map/ppermute | solution.py:181
  8.2 1.0 %collective-permute-start.1 = (f32[256,128]{1,0:T(8,128)S(1)}, f32[256,128]{1,0:T(8,128)S(1)}, u32[]{:S(2)}, u32[]{:S(2)}) collective-permute-start(f32[256,128]{1,0:T(8,128)S(1)} %add.12), channel_id=1, source_target_pairs={{0,16},{8,24},{16,0},{24,8},{32,48},{40,56},{48,32},{56,40},{64,80... | collective-permute-start | bytes 393224 | tf_op jit(solution)/shard_map/ppermute | solution.py:181
  9.3 4.9 %collective-permute-done.1.refs_1_ = f32[256,128]{1,0:T(8,128)S(1)} collective-permute-done((f32[256,128]{1,0:T(8,128)S(1)}, f32[256,128]{1,0:T(8,128)S(1)}, u32[]{:S(2)}, u32[]{:S(2)}) %collective-permute-start.1) | collective-permute-done | bytes 131104 | tf_op jit(solution)/shard_map/ppermute | solution.py:181
  14.2 0.0 copy-start.2
  14.2 6.6 %collective-permute-start.2 = (f32[256,128]{1,0:T(8,128)S(1)}, f32[256,128]{1,0:T(8,128)S(1)}, u32[]{:S(2)}, u32[]{:S(2)}) collective-permute-start(f32[256,128]{1,0:T(8,128)S(1)} %add.13), channel_id=1, source_target_pairs={{0,48},{8,56},{16,32},{24,40},{32,16},{40,24},{48,0},{56,8},{64,11... | collective-permute-start | bytes 393224 | tf_op jit(solution)/shard_map/ppermute | solution.py:181
  20.8 5.9 %collective-permute-done.2.l2_ref = f32[256,128]{1,0:T(8,128)S(1)} collective-permute-done((f32[256,128]{1,0:T(8,128)S(1)}, f32[256,128]{1,0:T(8,128)S(1)}, u32[]{:S(2)}, u32[]{:S(2)}) %collective-permute-start.2) | collective-permute-done | bytes 131104 | tf_op jit(solution)/shard_map/ppermute | solution.py:181
  26.7 3.5 %collective-permute-start.3 = (f32[256,128]{1,0:T(8,128)S(1)}, f32[256,128]{1,0:T(8,128)S(1)}, u32[]{:S(2)}, u32[]{:S(2)}) collective-permute-start(f32[256,128]{1,0:T(8,128)S(1)} %add.14), channel_id=1, source_target_pairs={{0,64},{8,72},{16,80},{24,88},{32,96},{40,104},{48,112},{56,120},{... | collective-permute-start | bytes 393224 | tf_op jit(solution)/shard_map/ppermute | solution.py:181
  30.2 4.8 %collective-permute-start.4 = (f32[256,128]{1,0:T(8,128)S(1)}, f32[256,128]{1,0:T(8,128)S(1)}, u32[]{:S(2)}, u32[]{:S(2)}) collective-permute-start(f32[256,128]{1,0:T(8,128)S(1)} %add.14), channel_id=1, source_target_pairs={{0,128},{8,136},{16,144},{24,152},{32,160},{40,168},{48,176},{56,1... | collective-permute-start | bytes 393224 | tf_op jit(solution)/shard_map/ppermute | solution.py:181
  35.1 1.3 %collective-permute-start.5 = (f32[256,128]{1,0:T(8,128)S(1)}, f32[256,128]{1,0:T(8,128)S(1)}, u32[]{:S(2)}, u32[]{:S(2)}) collective-permute-start(f32[256,128]{1,0:T(8,128)S(1)} %add.14), channel_id=1, source_target_pairs={{0,192},{8,200},{16,208},{24,216},{32,224},{40,232},{48,240},{56,2... | collective-permute-start | bytes 393224 | tf_op jit(solution)/shard_map/ppermute | solution.py:181
  36.4 0.0 copy-done
  36.4 0.0 copy-done.2
  36.4 2.1 %local0.1.refs_2_ = f32[128,1024]{1,0:T(8,128)S(1)} custom-call(bf16[1024,512]{1,0:T(8,128)(2,1)S(1)} %copy-done, bf16[1024,512]{1,0:T(8,128)(2,1)S(1)} %copy-done.1, bf16[1024,256]{1,0:T(8,128)(2,1)S(1)} %copy-done.3, s32[10,4,1024]{2,1,0:T(4,128)S(1)} %copy-done.2), custom_call_target="tpu_custom_call" | custom-call | flops 1000000000 | bytes 2000000 | tf_op jit(solution)/shard_map/local0/pallas_call | solution.py:205
  38.5 2.1 %local1.1.refs_3_ = f32[128,1024]{1,0:T(8,128)S(1)} custom-call(bf16[1024,512]{1,0:T(8,128)(2,1)S(1)} %copy-done, bf16[1024,512]{1,0:T(8,128)(2,1)S(1)} %copy-done.1, bf16[1024,256]{1,0:T(8,128)(2,1)S(1)} %copy-done.3, s32[10,4,1024]{2,1,0:T(4,128)S(1)} %copy-done.2), custom_call_target="tpu_custom_call" | custom-call | flops 1000000000 | bytes 2000000 | tf_op jit(solution)/shard_map/local1/pallas_call | solution.py:205
  40.6 0.4 far01.1.m_in
  41.0 0.0 collective-permute-done.3.a_ref
  41.0 0.0 collective-permute-done.4.b_ref
  41.1 0.0 collective-permute-done.5.c_ref
  41.1 0.6 %last.1 = (f32[256,1024]{1,0:T(8,128)S(1)}, f32[8,128]{1,0:T(8,128)S(1)}) custom-call(bf16[1024,512]{1,0:T(8,128)(2,1)S(1)} %copy-done, s32[10,4,1024]{2,1,0:T(4,128)S(1)} %copy-done.2, f32[256,128]{1,0:T(8,128)S(1)} %collective-permute-done.2.l2_ref, f32[256,128]{1,0:T(8,128)S(1)} %collective-permute-done.3.a_ref, ...), custom_call_target="tpu_custom_call" | custom-call | flops 200000000 | bytes 3000000 | tf_op jit(solution)/shard_map/last/pallas_call | solution.py:221
  41.7 0.0 copy-start.4
  41.7 0.1 collective-permute-start.6
  41.8 1.2 %collective-permute-done.6 = f32[8,128]{1,0:T(8,128)S(1)} collective-permute-done((f32[8,128]{1,0:T(8,128)S(1)}, f32[8,128]{1,0:T(8,128)S(1)}, u32[]{:S(2)}, u32[]{:S(2)}) %collective-permute-start.6) | collective-permute-done | bytes 4128 | tf_op jit(solution)/shard_map/ppermute | solution.py:225
  43.0 1.5 %collective-permute-start.7 = (f32[8,128]{1,0:T(8,128)S(1)}, f32[8,128]{1,0:T(8,128)S(1)}, u32[]{:S(2)}, u32[]{:S(2)}) collective-permute-start(f32[8,128]{1,0:T(8,128)S(1)} %add.15.s0), channel_id=1, source_target_pairs={{0,2},{1,3},{2,4},{3,5},{4,6},{5,7},{6,0},{7,1},{8,10},{9,11},{10,... | collective-permute-start | bytes 12296 | tf_op jit(solution)/shard_map/ppermute | solution.py:227
  44.5 1.7 %collective-permute-start.8 = (f32[8,128]{1,0:T(8,128)S(1)}, f32[8,128]{1,0:T(8,128)S(1)}, u32[]{:S(2)}, u32[]{:S(2)}) collective-permute-start(f32[8,128]{1,0:T(8,128)S(1)} %add.15.s0), channel_id=1, source_target_pairs={{0,6},{1,7},{2,0},{3,1},{4,2},{5,3},{6,4},{7,5},{8,14},{9,15},{10,... | collective-permute-start | bytes 12296 | tf_op jit(solution)/shard_map/ppermute | solution.py:227
  46.2 1.8 %collective-permute-start.9 = (f32[8,128]{1,0:T(8,128)S(1)}, f32[8,128]{1,0:T(8,128)S(1)}, u32[]{:S(2)}, u32[]{:S(2)}) collective-permute-start(f32[8,128]{1,0:T(8,128)S(1)} %add.15.s0), channel_id=1, source_target_pairs={{0,4},{1,5},{2,6},{3,7},{4,0},{5,1},{6,2},{7,3},{8,12},{9,13},{10,... | collective-permute-start | bytes 12296 | tf_op jit(solution)/shard_map/ppermute | solution.py:227
  48.0 0.0 collective-permute-done.7.s1
  48.0 0.0 collective-permute-done.8.s2
  48.1 3.2 %collective-permute-done.9.s3 = f32[8,128]{1,0:T(8,128)S(1)} collective-permute-done((f32[8,128]{1,0:T(8,128)S(1)}, f32[8,128]{1,0:T(8,128)S(1)}, u32[]{:S(2)}, u32[]{:S(2)}) %collective-permute-start.9) | collective-permute-done | bytes 4128 | tf_op jit(solution)/shard_map/ppermute | solution.py:227
  51.3 1.1 %norm.1 = bf16[1024,256]{1,0:T(8,128)(2,1)} custom-call(f32[256,1024]{1,0:T(8,128)S(1)} %get-tuple-element.7.m_ref, bf16[1,256]{1,0:T(2,128)(2,1)S(1)} %reshape.3.g_ref, f32[8,128]{1,0:T(8,128)S(1)} %add.15.s0, f32[8,128]{1,0:T(8,128)S(1)} %collective-permute-done.7.s1, f32[8,128]{1,0:T(8,128)S(1)} %collective-permute-done.8.s2, ...), custom_call_target="tpu_custom_call" | custom-call | flops 1000000 | bytes 1500000 | tf_op jit(solution)/shard_map/norm/pallas_call | solution.py:229
  (9 shorter events, 0.1 us)
Async XLA Ops:
  0.0 36.4 %copy-start = (bf16[1024,512]{1,0:T(8,128)(2,1)S(1)}, bf16[1024,512]{1,0:T(8,128)(2,1)}, u32[]{:S(2)}) copy-start(bf16[1024,512]{1,0:T(8,128)(2,1)} %q_ref.7) | copy-start | bytes 3145732
  0.0 1.3 %copy-start.1 = (bf16[1024,512]{1,0:T(8,128)(2,1)S(1)}, bf16[1024,512]{1,0:T(8,128)(2,1)}, u32[]{:S(2)}) copy-start(bf16[1024,512]{1,0:T(8,128)(2,1)} %k_ref.5) | copy-start | bytes 3145732
  1.3 1.0 %copy-start.3 = (bf16[1024,256]{1,0:T(8,128)(2,1)S(1)}, bf16[1024,256]{1,0:T(8,128)(2,1)}, u32[]{:S(2)}) copy-start(bf16[1024,256]{1,0:T(8,128)(2,1)} %v_ref.5) | copy-start | bytes 1572868
  2.7 5.5 %collective-permute-start = (f32[256,128]{1,0:T(8,128)S(1)}, f32[256,128]{1,0:T(8,128)S(1)}, u32[]{:S(2)}, u32[]{:S(2)}) collective-permute-start(f32[256,128]{1,0:T(8,128)S(1)} %summary.1), channel_id=1, source_target_pairs={{0,8},{8,0},{16,24},{24,16},{32,40},{40,32},{48,56},{56,48},{64,72... | collective-permute-start | bytes 393224 | tf_op jit(solution)/shard_map/ppermute | solution.py:181
  8.2 6.0 %collective-permute-start.1 = (f32[256,128]{1,0:T(8,128)S(1)}, f32[256,128]{1,0:T(8,128)S(1)}, u32[]{:S(2)}, u32[]{:S(2)}) collective-permute-start(f32[256,128]{1,0:T(8,128)S(1)} %add.12), channel_id=1, source_target_pairs={{0,16},{8,24},{16,0},{24,8},{32,48},{40,56},{48,32},{56,40},{64,80... | collective-permute-start | bytes 393224 | tf_op jit(solution)/shard_map/ppermute | solution.py:181
  14.2 22.2 %copy-start.2 = (s32[10,4,1024]{2,1,0:T(4,128)S(1)}, s32[10,4,1024]{2,1,0:T(4,128)}, u32[]{:S(2)}) copy-start(s32[10,4,1024]{2,1,0:T(4,128)} %li_ref.7) | copy-start | bytes 491524
  14.2 12.5 %collective-permute-start.2 = (f32[256,128]{1,0:T(8,128)S(1)}, f32[256,128]{1,0:T(8,128)S(1)}, u32[]{:S(2)}, u32[]{:S(2)}) collective-permute-start(f32[256,128]{1,0:T(8,128)S(1)} %add.13), channel_id=1, source_target_pairs={{0,48},{8,56},{16,32},{24,40},{32,16},{40,24},{48,0},{56,8},{64,11... | collective-permute-start | bytes 393224 | tf_op jit(solution)/shard_map/ppermute | solution.py:181
  26.7 14.3 %collective-permute-start.3 = (f32[256,128]{1,0:T(8,128)S(1)}, f32[256,128]{1,0:T(8,128)S(1)}, u32[]{:S(2)}, u32[]{:S(2)}) collective-permute-start(f32[256,128]{1,0:T(8,128)S(1)} %add.14), channel_id=1, source_target_pairs={{0,64},{8,72},{16,80},{24,88},{32,96},{40,104},{48,112},{56,120},{... | collective-permute-start | bytes 393224 | tf_op jit(solution)/shard_map/ppermute | solution.py:181
  30.2 10.8 %collective-permute-start.4 = (f32[256,128]{1,0:T(8,128)S(1)}, f32[256,128]{1,0:T(8,128)S(1)}, u32[]{:S(2)}, u32[]{:S(2)}) collective-permute-start(f32[256,128]{1,0:T(8,128)S(1)} %add.14), channel_id=1, source_target_pairs={{0,128},{8,136},{16,144},{24,152},{32,160},{40,168},{48,176},{56,1... | collective-permute-start | bytes 393224 | tf_op jit(solution)/shard_map/ppermute | solution.py:181
  35.1 6.0 %collective-permute-start.5 = (f32[256,128]{1,0:T(8,128)S(1)}, f32[256,128]{1,0:T(8,128)S(1)}, u32[]{:S(2)}, u32[]{:S(2)}) collective-permute-start(f32[256,128]{1,0:T(8,128)S(1)} %add.14), channel_id=1, source_target_pairs={{0,192},{8,200},{16,208},{24,216},{32,224},{40,232},{48,240},{56,2... | collective-permute-start | bytes 393224 | tf_op jit(solution)/shard_map/ppermute | solution.py:181
  41.7 6.3 %copy-start.4 = (bf16[256]{0:T(256)(128)(2,1)S(1)}, bf16[256]{0:T(256)(128)(2,1)}, u32[]{:S(2)}) copy-start(bf16[256]{0:T(256)(128)(2,1)} %param.8) | copy-start | bytes 1540
  41.7 1.3 %collective-permute-start.6 = (f32[8,128]{1,0:T(8,128)S(1)}, f32[8,128]{1,0:T(8,128)S(1)}, u32[]{:S(2)}, u32[]{:S(2)}) collective-permute-start(f32[8,128]{1,0:T(8,128)S(1)} %get-tuple-element.8), channel_id=1, source_target_pairs={{0,1},{1,0},{2,3},{3,2},{4,5},{5,4},{6,7},{7,6},{8,9},{9,8},{10,11... | collective-permute-start | bytes 12296 | tf_op jit(solution)/shard_map/ppermute | solution.py:225
  43.0 5.1 %collective-permute-start.7 = (f32[8,128]{1,0:T(8,128)S(1)}, f32[8,128]{1,0:T(8,128)S(1)}, u32[]{:S(2)}, u32[]{:S(2)}) collective-permute-start(f32[8,128]{1,0:T(8,128)S(1)} %add.15.s0), channel_id=1, source_target_pairs={{0,2},{1,3},{2,4},{3,5},{4,6},{5,7},{6,0},{7,1},{8,10},{9,11},{10,... | collective-permute-start | bytes 12296 | tf_op jit(solution)/shard_map/ppermute | solution.py:227
  44.5 3.6 %collective-permute-start.8 = (f32[8,128]{1,0:T(8,128)S(1)}, f32[8,128]{1,0:T(8,128)S(1)}, u32[]{:S(2)}, u32[]{:S(2)}) collective-permute-start(f32[8,128]{1,0:T(8,128)S(1)} %add.15.s0), channel_id=1, source_target_pairs={{0,6},{1,7},{2,0},{3,1},{4,2},{5,3},{6,4},{7,5},{8,14},{9,15},{10,... | collective-permute-start | bytes 12296 | tf_op jit(solution)/shard_map/ppermute | solution.py:227
  46.2 5.1 %collective-permute-start.9 = (f32[8,128]{1,0:T(8,128)S(1)}, f32[8,128]{1,0:T(8,128)S(1)}, u32[]{:S(2)}, u32[]{:S(2)}) collective-permute-start(f32[8,128]{1,0:T(8,128)S(1)} %add.15.s0), channel_id=1, source_target_pairs={{0,4},{1,5},{2,6},{3,7},{4,0},{5,1},{6,2},{7,3},{8,12},{9,13},{10,... | collective-permute-start | bytes 12296 | tf_op jit(solution)/shard_map/ppermute | solution.py:227

commit v2 on v1

v2 whole, which is shorter than its diff:
```python
import functools

import jax
import jax.numpy as jnp
from jax import lax
from jax.experimental import pallas as pl
from jax.experimental.pallas import tpu as pltpu
from jax.sharding import PartitionSpec as P

H = 32
DK = 128
DV = 64
STRETCH = 64
HEADS = 4
TOK = 1024
BLK = 256
Z = 8
VMEM_LIMIT = 32 * 1024 * 1024
CHUNKS = 1
PER = HEADS // CHUNKS

NT = (((1,), (1,)), ((), ()))
NN = (((1,), (0,)), ((), ()))


def dot(a, b, dims):
    return lax.dot_general(a, b, dims, preferred_element_type=jnp.float32)


def weight_scale(level):
    span = STRETCH if level == 0 else STRETCH * 2 ** (level - 1)
    return float(span) ** (-0.5) / 256.0


def weight_row(li_ref, level, head, start, size):
    row = li_ref[level, head : head + 1, start : start + size]
    return row.astype(jnp.float32) * weight_scale(level)


def summary_kernel(k_hbm, v_hbm, *refs):
    outs, (k_ref, vt_ref, v_ref, sems) = refs[:CHUNKS], refs[CHUNKS:]
    copies = []
    for b in range(TOK // BLK):
        rows = pl.ds(b * BLK, BLK)
        pair = (
            pltpu.make_async_copy(v_hbm.at[rows], v_ref.at[rows], sems.at[0, b]),
            pltpu.make_async_copy(k_hbm.at[rows], k_ref.at[rows], sems.at[1, b]),
        )
        for copy in pair:
            copy.start()
        copies.append(pair)
    totals = [None] * HEADS
    for b in range(TOK // BLK):
        for copy in copies[b]:
            copy.wait()
        r0 = b * BLK
        vt = v_ref[r0 : r0 + BLK, :].T
        vt_ref[:, r0 : r0 + BLK] = vt
        for h in range(HEADS):
            part = dot(
                vt[h * DV : (h + 1) * DV, :], k_ref[r0 : r0 + BLK, h * DK : (h + 1) * DK], NN
            )
            totals[h] = part if b == 0 else totals[h] + part
    for h in range(HEADS):
        at = (h % PER) * DV
        outs[h // PER][at : at + DV, :] = totals[h]


def local_kernel(first_head, heads, q_ref, k_ref, vt_ref, li_ref, m_ref):
    lane = lax.broadcasted_iota(jnp.int32, (1, BLK), 1)
    t_stretch = lane // STRETCH
    row = lax.broadcasted_iota(jnp.int32, (BLK, BLK), 0)
    col = lax.broadcasted_iota(jnp.int32, (BLK, BLK), 1)
    causal = (row // STRETCH == col // STRETCH) & (row <= col)
    zero = jnp.zeros((), jnp.bfloat16)
    for h in range(heads):
        wh = first_head + h
        before = None
        first_half = None
        for b in range(TOK // BLK):
            r0 = b * BLK
            q = q_ref[r0 : r0 + BLK, h * DK : (h + 1) * DK]
            k = k_ref[r0 : r0 + BLK, h * DK : (h + 1) * DK]
            vt = vt_ref[h * DV : (h + 1) * DV, r0 : r0 + BLK]
            sums = dot(
                jnp.concatenate(
                    [
                        jnp.where(t_stretch == 0, vt, zero),
                        jnp.where(t_stretch == 2, vt, zero),
                        jnp.where(t_stretch < 2, vt, zero),
                        vt,
                    ],
                    axis=0,
                ),
                k,
                NN,
            )
            total = sums[3 * DV :]
            rows = [k, sums[: 3 * DV].astype(jnp.bfloat16)]
            if b % 2 == 1:
                rows.append(before.astype(jnp.bfloat16))
            if b >= 2:
                rows.append(first_half.astype(jnp.bfloat16))
            prod = dot(jnp.concatenate(rows, axis=0), q, NT)
            low = jnp.where(causal, prod[:BLK], 0.0).astype(jnp.bfloat16)
            mix = dot(vt, low, NN) * weight_row(li_ref, 0, wh, r0, BLK)
            part = [prod[BLK + i * DV : BLK + (i + 1) * DV] for i in range(len(rows) + 1)]
            near = jnp.where(
                t_stretch == 1, part[0], jnp.where(t_stretch == 3, part[1], 0.0)
            )
            mix = mix + near * weight_row(li_ref, 1, wh, r0, BLK)
            mix = mix + jnp.where(t_stretch >= 2, part[2], 0.0) * weight_row(
                li_ref, 2, wh, r0, BLK
            )
            at = 3
            if b % 2 == 1:
                mix = mix + part[at] * weight_row(li_ref, 3, wh, r0, BLK)
                at += 1
            if b >= 2:
                mix = mix + part[at] * weight_row(li_ref, 4, wh, r0, BLK)
            m_ref[h * DV : (h + 1) * DV, r0 : r0 + BLK] = mix
            if b == 1:
                first_half = before + total
            before = total


def far_mix(h, rank, bits, states, q_ref, li_ref):
    at = (h % PER) * DV
    rows = jnp.concatenate(
        [s[h // PER][at : at + DV, :].astype(jnp.bfloat16) for s in states], axis=0
    )
    prod = dot(rows, q_ref[:, h * DK : (h + 1) * DK], NT)
    mix = None
    for i, bit in enumerate(bits):
        has = (rank >> bit) & 1
        w = jnp.where(has == 1, weight_row(li_ref, 5 + bit, h, 0, TOK), 0.0)
        term = prod[i * DV : (i + 1) * DV] * w
        mix = term if mix is None else mix + term
    return mix


def grouped(refs, n):
    return [refs[i * CHUNKS : (i + 1) * CHUNKS] for i in range(n)]


def far_kernel(bits, q_ref, li_ref, *refs):
    n = len(bits) * CHUNKS
    states, m_in, m_ref = grouped(refs[:n], len(bits)), refs[n:-1], refs[-1]
    rank = lax.axis_index("ctx")
    per = HEADS // len(m_in)
    for h in range(HEADS):
        at = (h % per) * DV
        mix = far_mix(h, rank, bits, states, q_ref, li_ref)
        m_ref[h * DV : (h + 1) * DV, :] = m_in[h // per][at : at + DV, :] + mix


def last_kernel(q_ref, li_ref, *refs):
    (m_in, m_ref, ss_ref) = refs[2 * CHUNKS :]
    states = [[refs[c][...] + refs[CHUNKS + c][...] for c in range(CHUNKS)]]
    rank = lax.axis_index("ctx")
    squares = None
    for h in range(HEADS):
        mix = m_in[h * DV : (h + 1) * DV, :] + far_mix(h, rank, (4,), states, q_ref, li_ref)
        m_ref[h * DV : (h + 1) * DV, :] = mix
        sq = jnp.sum(mix * mix, axis=0, keepdims=True)
        squares = sq if squares is None else squares + sq
    for i in range(TOK // 128):
        ss_ref[i : i + 1, :] = squares[:, i * 128 : (i + 1) * 128]


def turn_kernel(m_ref, g_ref, t_ref):
    gain = g_ref[...].astype(jnp.float32)
    for i in range(TOK // 128):
        t_ref[i * 128 : (i + 1) * 128, :] = m_ref[:, i * 128 : (i + 1) * 128].T * gain


def norm_kernel(t_ref, s0, s1, s2, s3, out_hbm, o_ref, sems):
    total = (s0[...] + s1[...]) + (s2[...] + s3[...])
    inv = lax.rsqrt(total / (H * DV) + 1e-06).T
    copies = []
    for i in range(TOK // 128):
        rows = slice(i * 128, (i + 1) * 128)
        o_ref[rows, :] = (t_ref[rows, :] * inv[:, i : i + 1]).astype(jnp.bfloat16)
        rows = pl.ds(i * 128, 128)
        copies.append(pltpu.make_async_copy(o_ref.at[rows], out_hbm.at[rows], sems.at[i]))
        copies[-1].start()
    for copy in copies:
        copy.wait()


WHOLE = pl.BlockSpec(memory_space=pltpu.VMEM)
HBM = pl.BlockSpec(memory_space=pltpu.HBM)


def call(
    kernel,
    outs,
    n_in,
    name,
    flops=0,
    moved=0,
    in_specs=None,
    out_specs=None,
    scratch=(),
    grid=(),
    vmem=VMEM_LIMIT,
):
    return pl.pallas_call(
        kernel,
        grid=grid,
        out_shape=outs,
        in_specs=in_specs or [WHOLE] * n_in,
        out_specs=out_specs or jax.tree.map(lambda _: WHOLE, outs),
        scratch_shapes=scratch,
        compiler_params=pltpu.CompilerParams(vmem_limit_bytes=vmem),
        cost_estimate=pl.CostEstimate(flops=flops, bytes_accessed=moved, transcendentals=0),
        name=name,
    )


def f32(*shape):
    return jax.ShapeDtypeStruct(shape, jnp.float32)


def in_hbm(x):
    return pltpu.with_memory_space_constraint(x, pltpu.HBM)


def bf16(*shape):
    return jax.ShapeDtypeStruct(shape, jnp.bfloat16)


def on_device(queries, keys, values, norm_gain, level_index):
    ctx = lax.axis_size("ctx")
    state = f32(PER * DV, DK)
    mixed = f32(HEADS * DV, TOK)

    def over_ctx(chunks, move):
        pairs = []
        for r in range(ctx):
            to = move(r // Z, r % Z)
            if to is not None:
                pairs.append((r, to[0] * Z + to[1]))
        return [lax.ppermute(x, "ctx", pairs) for x in chunks]

    def add(a, b):
        return [x + y for x, y in zip(a, b)]

    *own, keys_here, values_turned = call(
        summary_kernel,
        [state] * CHUNKS + [bf16(TOK, HEADS * DK), bf16(HEADS * DV, TOK)],
        2,
        "summary",
        268_000_000,
        3_200_000,
        in_specs=[HBM, HBM],
        scratch=[
            pltpu.VMEM((TOK, HEADS * DV), jnp.bfloat16),
            pltpu.SemaphoreType.DMA((2, TOK // BLK)),
        ],
    )(in_hbm(keys), in_hbm(values))

    half = HEADS // 2
    parts = []
    for p in range(2):
        specs = [
            pl.BlockSpec((TOK, half * DK), lambda i, p=p: (0, p)),
            pl.BlockSpec((TOK, half * DK), lambda i, p=p: (0, p)),
            pl.BlockSpec((half * DV, TOK), lambda i, p=p: (p, 0)),
            pl.BlockSpec(level_index.shape, lambda i: (0, 0, 0)),
        ]
        parts.append(
            call(
                functools.partial(local_kernel, p * half, half),
                f32(half * DV, TOK),
                4,
                "local%d" % p,
                1_000_000_000,
                2_000_000,
                in_specs=specs,
                out_specs=pl.BlockSpec((half * DV, TOK), lambda i: (0, 0)),
                grid=(1,),
            )(queries, keys_here, values_turned, level_index)
        )

    l0 = over_ctx(own, lambda y, z: (y, z ^ 1))
    l0[-1], parts[0] = lax.optimization_barrier((l0[-1], parts[0]))
    pair = add(own, l0)
    l1 = over_ctx(pair, lambda y, z: (y, z ^ 3))
    l1[-1], parts[1] = lax.optimization_barrier((l1[-1], parts[1]))
    quad = add(pair, l1)
    hop = (6, 7, 4, 5, 2, 3, 0, 1)
    l2 = over_ctx(quad, lambda y, z: (y, hop[z]))
    group = add(quad, l2)
    l3 = over_ctx(group, lambda y, z: (y ^ 1, z))
    up = [over_ctx(group, lambda y, z, k=k: (y ^ k, z)) for k in (3, 2)]
    near = call(
        functools.partial(far_kernel, (0, 1, 2, 3)),
        mixed,
        4 + 4 * CHUNKS,
        "far0123",
        268_000_000,
        3_000_000,
    )(queries, level_index, *l0, *l1, *l2, *l3, *parts)
    flat, squares = call(
        last_kernel, (mixed, f32(8, 128)), 3 + 2 * CHUNKS, "last", 67_000_000, 3_000_000
    )(queries, level_index, *up[0], *up[1], near)

    turned = call(turn_kernel, f32(TOK, HEADS * DV), 2, "turn", 1_000_000, 2_000_000)(
        flat, norm_gain.reshape(1, HEADS * DV)
    )
    def over_head(x, move):
        pairs = [(i, (i // 2, i % 2)) for i in range(8)]
        return lax.ppermute(
            x, "head", [(i, to[0] * 2 + to[1]) for i, to in ((i, move(*xc)) for i, xc in pairs)]
        )

    squares = squares + over_head(squares, lambda x, c: (x, 1 - c))
    one = over_head(squares, lambda x, c: (x ^ (1 if c == 0 else 3), c))
    two = over_head(squares, lambda x, c: (x ^ 2, c))
    three = over_head(one, lambda x, c: (x, 1 - c))
    others = (one, two, three)
    return call(
        norm_kernel,
        bf16(TOK, HEADS * DV),
        5,
        "norm",
        1_000_000,
        1_500_000,
        out_specs=HBM,
        scratch=[pltpu.VMEM((TOK, HEADS * DV), jnp.bfloat16), pltpu.SemaphoreType.DMA((8,))],
    )(turned, squares, *others)


def solution(mesh):
    in_specs = (
        P("ctx", "head"),
        P("ctx", "head"),
        P("ctx", "head"),
        P("head"),
        P(None, "head", "ctx"),
    )
    out_specs = P("ctx", "head")
    return jax.shard_map(
        on_device, mesh=mesh, in_specs=in_specs, out_specs=out_specs, check_vma=False
    )
```

time: 52.6 us -> 46.4 us (0.88)
  the two profiles are of different devices: /device:TPU:64 before, /device:TPU:1 now
where the time goes in v2:
time: 46.4 us; the launch traced here: 46.3 us
  starting transfers between devices  24.8 us (53%)
  waiting for transfers between devices  12.7 us (27%)
  Pallas kernels  8.72 us (19%)
    ppermute x6, starting transfers between devices, over_ctx(): return [lax.ppermute(x, 'ctx', pairs) for x in chunks]  14.5 us
    ppermute x4, starting transfers between devices, over_head(): lax.ppermute(x, 'head', [(i, to[0] * 2 + to[1]) for i, to in ((i, move(*x...  10.3 us
    ppermute x6, waiting for transfers between devices, over_ctx(): return [lax.ppermute(x, 'ctx', pairs) for x in chunks]  9.57 us
    pallas_call x2, Pallas kernels, on_device(): call(functools.partial(local_kernel, p * half, half), f32(half * DV, TOK)...  4.06 us
    ppermute x4, waiting for transfers between devices, over_head(): lax.ppermute(x, 'head', [(i, to[0] * 2 + to[1]) for i, to in ((i, move(*x...  3.13 us
    pallas_call x1, Pallas kernels, on_device(): call(summary_kernel, [state] * CHUNKS + [bf16(TOK, HEADS * DK), bf16(HEAD...  2.02 us
    pallas_call x1, Pallas kernels, on_device(): call(norm_kernel, bf16(TOK, HEADS * DV), 5, 'norm', 1000000, 1500000, out...  1.09 us
  transfers between devices with their start and end apart: 10, of which 8 were waited for; matrix products, arithmetic and copies ran while one was open for 0% of the time, Pallas kernels for 11%

profile of v2, /device:TPU:1, one launch (start us, length us, event | category | flops | bytes accessed | tf_op | source)
XLA Modules:
  0.0 46.3 jit_solution(7980569888589411779)
XLA Ops:
  0.0 0.0 copy-start.1
  0.0 2.0 %summary.1 = (f32[256,128]{1,0:T(8,128)S(1)}, bf16[1024,512]{1,0:T(8,128)(2,1)S(1)}, bf16[256,1024]{1,0:T(8,128)(2,1)S(1)}) custom-call(bf16[1024,512]{1,0:T(8,128)(2,1)} %k_hbm.1, bf16[1024,256]{1,0:T(8,128)(2,1)} %v_hbm.1), custom_call_target="tpu_custom_call" | custom-call | flops 268000000 | bytes 3200000 | tf_op jit(solution)/shard_map/summary/pallas_call | solution.py:249
  2.0 2.6 %collective-permute-start = (f32[256,128]{1,0:T(8,128)S(1)}, f32[256,128]{1,0:T(8,128)S(1)}, u32[]{:S(2)}, u32[]{:S(2)}) collective-permute-start(f32[256,128]{1,0:T(8,128)S(1)} %get-tuple-element.14), channel_id=1, source_target_pairs={{0,8},{8,0},{16,24},{24,16},{32,40},{40,32},{48,56},{56,48},{64,72... | collective-permute-start | bytes 393224 | tf_op jit(solution)/shard_map/ppermute | solution.py:244
  4.6 0.0 copy-done.1
  4.6 0.0 copy-done
  4.6 2.0 %local0.1.refs_4_ = f32[128,1024]{1,0:T(8,128)S(1)} custom-call(bf16[1024,512]{1,0:T(8,128)(2,1)S(1)} %copy-done, bf16[1024,512]{1,0:T(8,128)(2,1)S(1)} %get-tuple-element.15.k_ref, bf16[256,1024]{1,0:T(8,128)(2,1)S(1)} %get-tuple-element.16.vt_ref, s32[10,4,1024]{2,1,0:T(4,128)S(1)} %copy-done.1), custom_call_target="tpu_custom_call" | custom-call | flops 1000000000 | bytes 2000000 | tf_op jit(solution)/shard_map/local0/pallas_call | solution.py:273
  6.6 0.3 collective-permute-done.refs_0_
  7.0 4.8 %collective-permute-start.1 = (f32[256,128]{1,0:T(8,128)S(1)}, f32[256,128]{1,0:T(8,128)S(1)}, u32[]{:S(2)}, u32[]{:S(2)}) collective-permute-start(f32[256,128]{1,0:T(8,128)S(1)} %add.12), channel_id=1, source_target_pairs={{0,24},{8,16},{16,8},{24,0},{32,56},{40,48},{48,40},{56,32},{64,88... | collective-permute-start | bytes 393224 | tf_op jit(solution)/shard_map/ppermute | solution.py:244
  11.8 2.0 %local1.1.refs_5_ = f32[128,1024]{1,0:T(8,128)S(1)} custom-call(bf16[1024,512]{1,0:T(8,128)(2,1)S(1)} %copy-done, bf16[1024,512]{1,0:T(8,128)(2,1)S(1)} %get-tuple-element.15.k_ref, bf16[256,1024]{1,0:T(8,128)(2,1)S(1)} %get-tuple-element.16.vt_ref, s32[10,4,1024]{2,1,0:T(4,128)S(1)} %copy-done.1), custom_call_target="tpu_custom_call" | custom-call | flops 1000000000 | bytes 2000000 | tf_op jit(solution)/shard_map/local1/pallas_call | solution.py:273
  13.8 0.4 collective-permute-done.1.refs_1_
  14.3 3.1 %collective-permute-start.2 = (f32[256,128]{1,0:T(8,128)S(1)}, f32[256,128]{1,0:T(8,128)S(1)}, u32[]{:S(2)}, u32[]{:S(2)}) collective-permute-start(f32[256,128]{1,0:T(8,128)S(1)} %add.13), channel_id=1, source_target_pairs={{0,48},{8,56},{16,32},{24,40},{32,16},{40,24},{48,0},{56,8},{64,11... | collective-permute-start | bytes 393224 | tf_op jit(solution)/shard_map/ppermute | solution.py:244
  17.4 4.4 %collective-permute-done.2.refs_2_ = f32[256,128]{1,0:T(8,128)S(1)} collective-permute-done((f32[256,128]{1,0:T(8,128)S(1)}, f32[256,128]{1,0:T(8,128)S(1)}, u32[]{:S(2)}, u32[]{:S(2)}) %collective-permute-start.2) | collective-permute-done | bytes 131104 | tf_op jit(solution)/shard_map/ppermute | solution.py:244
  21.8 1.4 %collective-permute-start.5 = (f32[256,128]{1,0:T(8,128)S(1)}, f32[256,128]{1,0:T(8,128)S(1)}, u32[]{:S(2)}, u32[]{:S(2)}) collective-permute-start(f32[256,128]{1,0:T(8,128)S(1)} %add.14), channel_id=1, source_target_pairs={{0,64},{8,72},{16,80},{24,88},{32,96},{40,104},{48,112},{56,120},{... | collective-permute-start | bytes 393224 | tf_op jit(solution)/shard_map/ppermute | solution.py:244
  23.2 2.6 %collective-permute-start.4 = (f32[256,128]{1,0:T(8,128)S(1)}, f32[256,128]{1,0:T(8,128)S(1)}, u32[]{:S(2)}, u32[]{:S(2)}) collective-permute-start(f32[256,128]{1,0:T(8,128)S(1)} %add.14), channel_id=1, source_target_pairs={{0,128},{8,136},{16,144},{24,152},{32,160},{40,168},{48,176},{56,1... | collective-permute-start | bytes 393224 | tf_op jit(solution)/shard_map/ppermute | solution.py:244
  25.8 0.0 collective-permute-start.3
  25.8 0.0 collective-permute-done.5.refs_3_
  25.8 0.7 %far0123.1.refs_2_ = f32[256,1024]{1,0:T(8,128)S(1)} custom-call(bf16[1024,512]{1,0:T(8,128)(2,1)S(1)} %copy-done, s32[10,4,1024]{2,1,0:T(4,128)S(1)} %copy-done.1, f32[256,128]{1,0:T(8,128)S(1)} %collective-permute-done.refs_0_, f32[256,128]{1,0:T(8,128)S(1)} %collective-permute-done.1.refs_1_, f32[256,128]{1,0:T(8,128)S(1)} %collective-permute-done.2.refs_2_, ...), custom_call_target="tpu_custom_call" | custom-call | flops 268000000 | bytes 3000000 | tf_op jit(solution)/shard_map/far0123/pallas_call | solution.py:297
  26.5 3.0 %collective-permute-done.4.refs_1_ = f32[256,128]{1,0:T(8,128)S(1)} collective-permute-done((f32[256,128]{1,0:T(8,128)S(1)}, f32[256,128]{1,0:T(8,128)S(1)}, u32[]{:S(2)}, u32[]{:S(2)}) %collective-permute-start.4) | collective-permute-done | bytes 131104 | tf_op jit(solution)/shard_map/ppermute | solution.py:244
  29.6 1.4 %collective-permute-done.3.refs_0_ = f32[256,128]{1,0:T(8,128)S(1)} collective-permute-done((f32[256,128]{1,0:T(8,128)S(1)}, f32[256,128]{1,0:T(8,128)S(1)}, u32[]{:S(2)}, u32[]{:S(2)}) %collective-permute-start.3) | collective-permute-done | bytes 131104 | tf_op jit(solution)/shard_map/ppermute | solution.py:244
  31.0 0.5 %last.1 = (f32[256,1024]{1,0:T(8,128)S(1)}, f32[8,128]{1,0:T(8,128)S(1)}) custom-call(bf16[1024,512]{1,0:T(8,128)(2,1)S(1)} %copy-done, s32[10,4,1024]{2,1,0:T(4,128)S(1)} %copy-done.1, f32[256,128]{1,0:T(8,128)S(1)} %collective-permute-done.3.refs_0_, f32[256,128]{1,0:T(8,128)S(1)} %collective-permute-done.4.refs_1_, f32[256,1024]{1,0:T(8,128)S(1)} %far0123.1.refs_2_), custom_call_target="tpu_custom_call" | custom-call | flops 67000000 | bytes 3000000 | tf_op jit(solution)/shard_map/last/pallas_call | solution.py:305
  31.5 0.0 copy-start.2
  31.5 6.4 %collective-permute-start.6 = (f32[8,128]{1,0:T(8,128)S(1)}, f32[8,128]{1,0:T(8,128)S(1)}, u32[]{:S(2)}, u32[]{:S(2)}) collective-permute-start(f32[8,128]{1,0:T(8,128)S(1)} %get-tuple-element.22), channel_id=1, source_target_pairs={{0,1},{1,0},{2,3},{3,2},{4,5},{5,4},{6,7},{7,6},{8,9},{9,8},{10,11... | collective-permute-start | bytes 12296 | tf_op jit(solution)/shard_map/ppermute | solution.py:314
  37.8 0.8 %collective-permute-done.6 = f32[8,128]{1,0:T(8,128)S(1)} collective-permute-done((f32[8,128]{1,0:T(8,128)S(1)}, f32[8,128]{1,0:T(8,128)S(1)}, u32[]{:S(2)}, u32[]{:S(2)}) %collective-permute-start.6) | collective-permute-done | bytes 4128 | tf_op jit(solution)/shard_map/ppermute | solution.py:314
  38.7 2.5 %collective-permute-start.7 = (f32[8,128]{1,0:T(8,128)S(1)}, f32[8,128]{1,0:T(8,128)S(1)}, u32[]{:S(2)}, u32[]{:S(2)}) collective-permute-start(f32[8,128]{1,0:T(8,128)S(1)} %add.15.s0), channel_id=1, source_target_pairs={{0,2},{1,7},{2,0},{3,5},{4,6},{5,3},{6,4},{7,1},{8,10},{9,15},{10,... | collective-permute-start | bytes 12296 | tf_op jit(solution)/shard_map/ppermute | solution.py:314
  41.1 0.5 %collective-permute-start.8 = (f32[8,128]{1,0:T(8,128)S(1)}, f32[8,128]{1,0:T(8,128)S(1)}, u32[]{:S(2)}, u32[]{:S(2)}) collective-permute-start(f32[8,128]{1,0:T(8,128)S(1)} %add.15.s0), channel_id=1, source_target_pairs={{0,4},{1,5},{2,6},{3,7},{4,0},{5,1},{6,2},{7,3},{8,12},{9,13},{10,... | collective-permute-start | bytes 12296 | tf_op jit(solution)/shard_map/ppermute | solution.py:314
  41.7 0.7 %collective-permute-done.7.s1 = f32[8,128]{1,0:T(8,128)S(1)} collective-permute-done((f32[8,128]{1,0:T(8,128)S(1)}, f32[8,128]{1,0:T(8,128)S(1)}, u32[]{:S(2)}, u32[]{:S(2)}) %collective-permute-start.7) | collective-permute-done | bytes 4128 | tf_op jit(solution)/shard_map/ppermute | solution.py:314
  42.3 0.9 %collective-permute-start.9 = (f32[8,128]{1,0:T(8,128)S(1)}, f32[8,128]{1,0:T(8,128)S(1)}, u32[]{:S(2)}, u32[]{:S(2)}) collective-permute-start(f32[8,128]{1,0:T(8,128)S(1)} %collective-permute-done.7.s1), channel_id=1, source_target_pairs={{0,1},{1,0},{2,3},{3,2},{4,5},{5,4},{6,7},{7,6},{8,9},{9,8},{10,11... | collective-permute-start | bytes 12296 | tf_op jit(solution)/shard_map/ppermute | solution.py:314
  43.2 0.0 copy-done.2
  43.2 0.3 turn.1.t_ref
  43.6 1.6 %collective-permute-done.8.s2 = f32[8,128]{1,0:T(8,128)S(1)} collective-permute-done((f32[8,128]{1,0:T(8,128)S(1)}, f32[8,128]{1,0:T(8,128)S(1)}, u32[]{:S(2)}, u32[]{:S(2)}) %collective-permute-start.8) | collective-permute-done | bytes 4128 | tf_op jit(solution)/shard_map/ppermute | solution.py:314
  45.2 0.0 collective-permute-done.9.s3
  45.2 1.1 %norm.1 = bf16[1024,256]{1,0:T(8,128)(2,1)} custom-call(f32[1024,256]{1,0:T(8,128)S(1)} %turn.1.t_ref, f32[8,128]{1,0:T(8,128)S(1)} %add.15.s0, f32[8,128]{1,0:T(8,128)S(1)} %collective-permute-done.7.s1, f32[8,128]{1,0:T(8,128)S(1)} %collective-permute-done.8.s2, f32[8,128]{1,0:T(8,128)S(1)} %collective-permute-done.9.s3), custom_call_target="tpu_custom_call" | custom-call | flops 1000000 | bytes 1500000 | tf_op jit(solution)/shard_map/norm/pallas_call | solution.py:323
  (6 shorter events, 0.1 us)
Async XLA Ops:
  0.0 4.6 %copy-start.1 = (s32[10,4,1024]{2,1,0:T(4,128)S(1)}, s32[10,4,1024]{2,1,0:T(4,128)}, u32[]{:S(2)}) copy-start(s32[10,4,1024]{2,1,0:T(4,128)} %li_ref.7) | copy-start | bytes 491524
  0.0 4.6 %copy-start = (bf16[1024,512]{1,0:T(8,128)(2,1)S(1)}, bf16[1024,512]{1,0:T(8,128)(2,1)}, u32[]{:S(2)}) copy-start(bf16[1024,512]{1,0:T(8,128)(2,1)} %q_ref.7) | copy-start | bytes 3145732
  2.0 4.9 %collective-permute-start = (f32[256,128]{1,0:T(8,128)S(1)}, f32[256,128]{1,0:T(8,128)S(1)}, u32[]{:S(2)}, u32[]{:S(2)}) collective-permute-start(f32[256,128]{1,0:T(8,128)S(1)} %get-tuple-element.14), channel_id=1, source_target_pairs={{0,8},{8,0},{16,24},{24,16},{32,40},{40,32},{48,56},{56,48},{64,72... | collective-permute-start | bytes 393224 | tf_op jit(solution)/shard_map/ppermute | solution.py:244
  7.0 7.3 %collective-permute-start.1 = (f32[256,128]{1,0:T(8,128)S(1)}, f32[256,128]{1,0:T(8,128)S(1)}, u32[]{:S(2)}, u32[]{:S(2)}) collective-permute-start(f32[256,128]{1,0:T(8,128)S(1)} %add.12), channel_id=1, source_target_pairs={{0,24},{8,16},{16,8},{24,0},{32,56},{40,48},{48,40},{56,32},{64,88... | collective-permute-start | bytes 393224 | tf_op jit(solution)/shard_map/ppermute | solution.py:244
  14.3 7.5 %collective-permute-start.2 = (f32[256,128]{1,0:T(8,128)S(1)}, f32[256,128]{1,0:T(8,128)S(1)}, u32[]{:S(2)}, u32[]{:S(2)}) collective-permute-start(f32[256,128]{1,0:T(8,128)S(1)} %add.13), channel_id=1, source_target_pairs={{0,48},{8,56},{16,32},{24,40},{32,16},{40,24},{48,0},{56,8},{64,11... | collective-permute-start | bytes 393224 | tf_op jit(solution)/shard_map/ppermute | solution.py:244
  21.8 4.0 %collective-permute-start.5 = (f32[256,128]{1,0:T(8,128)S(1)}, f32[256,128]{1,0:T(8,128)S(1)}, u32[]{:S(2)}, u32[]{:S(2)}) collective-permute-start(f32[256,128]{1,0:T(8,128)S(1)} %add.14), channel_id=1, source_target_pairs={{0,64},{8,72},{16,80},{24,88},{32,96},{40,104},{48,112},{56,120},{... | collective-permute-start | bytes 393224 | tf_op jit(solution)/shard_map/ppermute | solution.py:244
  23.2 6.4 %collective-permute-start.4 = (f32[256,128]{1,0:T(8,128)S(1)}, f32[256,128]{1,0:T(8,128)S(1)}, u32[]{:S(2)}, u32[]{:S(2)}) collective-permute-start(f32[256,128]{1,0:T(8,128)S(1)} %add.14), channel_id=1, source_target_pairs={{0,128},{8,136},{16,144},{24,152},{32,160},{40,168},{48,176},{56,1... | collective-permute-start | bytes 393224 | tf_op jit(solution)/shard_map/ppermute | solution.py:244
  25.8 5.2 %collective-permute-start.3 = (f32[256,128]{1,0:T(8,128)S(1)}, f32[256,128]{1,0:T(8,128)S(1)}, u32[]{:S(2)}, u32[]{:S(2)}) collective-permute-start(f32[256,128]{1,0:T(8,128)S(1)} %add.14), channel_id=1, source_target_pairs={{0,192},{8,200},{16,208},{24,216},{32,224},{40,232},{48,240},{56,2... | collective-permute-start | bytes 393224 | tf_op jit(solution)/shard_map/ppermute | solution.py:244
  31.5 11.8 %copy-start.2 = (bf16[256]{0:T(256)(128)(2,1)S(1)}, bf16[256]{0:T(256)(128)(2,1)}, u32[]{:S(2)}) copy-start(bf16[256]{0:T(256)(128)(2,1)} %param.8) | copy-start | bytes 1540
  31.5 7.2 %collective-permute-start.6 = (f32[8,128]{1,0:T(8,128)S(1)}, f32[8,128]{1,0:T(8,128)S(1)}, u32[]{:S(2)}, u32[]{:S(2)}) collective-permute-start(f32[8,128]{1,0:T(8,128)S(1)} %get-tuple-element.22), channel_id=1, source_target_pairs={{0,1},{1,0},{2,3},{3,2},{4,5},{5,4},{6,7},{7,6},{8,9},{9,8},{10,11... | collective-permute-start | bytes 12296 | tf_op jit(solution)/shard_map/ppermute | solution.py:314
  38.7 3.7 %collective-permute-start.7 = (f32[8,128]{1,0:T(8,128)S(1)}, f32[8,128]{1,0:T(8,128)S(1)}, u32[]{:S(2)}, u32[]{:S(2)}) collective-permute-start(f32[8,128]{1,0:T(8,128)S(1)} %add.15.s0), channel_id=1, source_target_pairs={{0,2},{1,7},{2,0},{3,5},{4,6},{5,3},{6,4},{7,1},{8,10},{9,15},{10,... | collective-permute-start | bytes 12296 | tf_op jit(solution)/shard_map/ppermute | solution.py:314
  41.1 4.1 %collective-permute-start.8 = (f32[8,128]{1,0:T(8,128)S(1)}, f32[8,128]{1,0:T(8,128)S(1)}, u32[]{:S(2)}, u32[]{:S(2)}) collective-permute-start(f32[8,128]{1,0:T(8,128)S(1)} %add.15.s0), channel_id=1, source_target_pairs={{0,4},{1,5},{2,6},{3,7},{4,0},{5,1},{6,2},{7,3},{8,12},{9,13},{10,... | collective-permute-start | bytes 12296 | tf_op jit(solution)/shard_map/ppermute | solution.py:314
  42.3 2.9 %collective-permute-start.9 = (f32[8,128]{1,0:T(8,128)S(1)}, f32[8,128]{1,0:T(8,128)S(1)}, u32[]{:S(2)}, u32[]{:S(2)}) collective-permute-start(f32[8,128]{1,0:T(8,128)S(1)} %collective-permute-done.7.s1), channel_id=1, source_target_pairs={{0,1},{1,0},{2,3},{3,2},{4,5},{5,4},{6,7},{7,6},{8,9},{9,8},{10,11... | collective-permute-start | bytes 12296 | tf_op jit(solution)/shard_map/ppermute | solution.py:314

commit v3 on v2

--- a/solution.py
+++ b/solution.py
@@ -73,12 +73,12 @@
     col = lax.broadcasted_iota(jnp.int32, (BLK, BLK), 1)
     causal = (row // STRETCH == col // STRETCH) & (row <= col)
     zero = jnp.zeros((), jnp.bfloat16)
-    for h in range(heads):
-        wh = first_head + h
-        before = None
-        first_half = None
-        for b in range(TOK // BLK):
-            r0 = b * BLK
+    before = [None] * heads
+    first_half = [None] * heads
+    for b in range(TOK // BLK):
+        r0 = b * BLK
+        for h in range(heads):
+            wh = first_head + h
             q = q_ref[r0 : r0 + BLK, h * DK : (h + 1) * DK]
             k = k_ref[r0 : r0 + BLK, h * DK : (h + 1) * DK]
             vt = vt_ref[h * DV : (h + 1) * DV, r0 : r0 + BLK]
@@ -98,9 +98,9 @@
             total = sums[3 * DV :]
             rows = [k, sums[: 3 * DV].astype(jnp.bfloat16)]
             if b % 2 == 1:
-                rows.append(before.astype(jnp.bfloat16))
+                rows.append(before[h].astype(jnp.bfloat16))
             if b >= 2:
-                rows.append(first_half.astype(jnp.bfloat16))
+                rows.append(first_half[h].astype(jnp.bfloat16))
             prod = dot(jnp.concatenate(rows, axis=0), q, NT)
             low = jnp.where(causal, prod[:BLK], 0.0).astype(jnp.bfloat16)
             mix = dot(vt, low, NN) * weight_row(li_ref, 0, wh, r0, BLK)
@@ -120,8 +120,8 @@
                 mix = mix + part[at] * weight_row(li_ref, 4, wh, r0, BLK)
             m_ref[h * DV : (h + 1) * DV, r0 : r0 + BLK] = mix
             if b == 1:
-                first_half = before + total
-            before = total
+                first_half[h] = before[h] + total
+            before[h] = total
 
 
 def far_mix(h, rank, bits, states, q_ref, li_ref):
@@ -155,12 +155,13 @@
 
 
 def last_kernel(q_ref, li_ref, *refs):
-    (m_in, m_ref, ss_ref) = refs[2 * CHUNKS :]
-    states = [[refs[c][...] + refs[CHUNKS + c][...] for c in range(CHUNKS)]]
+    l3, up3, up2 = grouped(refs[: 3 * CHUNKS], 3)
+    m_in, m_ref, ss_ref = refs[3 * CHUNKS :]
+    states = [l3, [a[...] + b[...] for a, b in zip(up3, up2)]]
     rank = lax.axis_index("ctx")
     squares = None
     for h in range(HEADS):
-        mix = m_in[h * DV : (h + 1) * DV, :] + far_mix(h, rank, (4,), states, q_ref, li_ref)
+        mix = m_in[h * DV : (h + 1) * DV, :] + far_mix(h, rank, (3, 4), states, q_ref, li_ref)
         m_ref[h * DV : (h + 1) * DV, :] = mix
         sq = jnp.sum(mix * mix, axis=0, keepdims=True)
         squares = sq if squares is None else squares + sq
@@ -168,19 +169,17 @@
         ss_ref[i : i + 1, :] = squares[:, i * 128 : (i + 1) * 128]
 
 
-def turn_kernel(m_ref, g_ref, t_ref):
-    gain = g_ref[...].astype(jnp.float32)
-    for i in range(TOK // 128):
-        t_ref[i * 128 : (i + 1) * 128, :] = m_ref[:, i * 128 : (i + 1) * 128].T * gain
-
-
-def norm_kernel(t_ref, s0, s1, s2, s3, out_hbm, o_ref, sems):
+def gain_kernel(m_ref, g_ref, t_ref):
+    t_ref[...] = m_ref[...] * g_ref[...].astype(jnp.float32).T
+
+
+def norm_kernel(m_ref, s0, s1, s2, s3, out_hbm, o_ref, sems):
     total = (s0[...] + s1[...]) + (s2[...] + s3[...])
-    inv = lax.rsqrt(total / (H * DV) + 1e-06).T
+    inv = lax.rsqrt(total / (H * DV) + 1e-06)
     copies = []
     for i in range(TOK // 128):
-        rows = slice(i * 128, (i + 1) * 128)
-        o_ref[rows, :] = (t_ref[rows, :] * inv[:, i : i + 1]).astype(jnp.bfloat16)
+        x = (m_ref[:, i * 128 : (i + 1) * 128] * inv[i : i + 1, :]).astype(jnp.bfloat16)
+        o_ref[i * 128 : (i + 1) * 128, :] = x.T
         rows = pl.ds(i * 128, 128)
         copies.append(pltpu.make_async_copy(o_ref.at[rows], out_hbm.at[rows], sems.at[i]))
         copies[-1].start()
@@ -263,12 +262,6 @@
     half = HEADS // 2
     parts = []
     for p in range(2):
-        specs = [
-            pl.BlockSpec((TOK, half * DK), lambda i, p=p: (0, p)),
-            pl.BlockSpec((TOK, half * DK), lambda i, p=p: (0, p)),
-            pl.BlockSpec((half * DV, TOK), lambda i, p=p: (p, 0)),
-            pl.BlockSpec(level_index.shape, lambda i: (0, 0, 0)),
-        ]
         parts.append(
             call(
                 functools.partial(local_kernel, p * half, half),
@@ -277,7 +270,12 @@
                 "local%d" % p,
                 1_000_000_000,
                 2_000_000,
-                in_specs=specs,
+                in_specs=[
+                    pl.BlockSpec((TOK, half * DK), lambda i, p=p: (0, p)),
+                    pl.BlockSpec((TOK, half * DK), lambda i, p=p: (0, p)),
+                    pl.BlockSpec((half * DV, TOK), lambda i, p=p: (p, 0)),
+                    pl.BlockSpec(level_index.shape, lambda i: (0, 0, 0)),
+                ],
                 out_specs=pl.BlockSpec((half * DV, TOK), lambda i: (0, 0)),
                 grid=(1,),
             )(queries, keys_here, values_turned, level_index)
@@ -289,24 +287,24 @@
     l1 = over_ctx(pair, lambda y, z: (y, z ^ 3))
     l1[-1], parts[1] = lax.optimization_barrier((l1[-1], parts[1]))
     quad = add(pair, l1)
-    hop = (6, 7, 4, 5, 2, 3, 0, 1)
+    hop = (7, 6, 5, 4, 3, 2, 1, 0)
     l2 = over_ctx(quad, lambda y, z: (y, hop[z]))
     group = add(quad, l2)
     l3 = over_ctx(group, lambda y, z: (y ^ 1, z))
     up = [over_ctx(group, lambda y, z, k=k: (y ^ k, z)) for k in (3, 2)]
     near = call(
-        functools.partial(far_kernel, (0, 1, 2, 3)),
+        functools.partial(far_kernel, (0, 1, 2)),
         mixed,
-        4 + 4 * CHUNKS,
-        "far0123",
+        4 + 3 * CHUNKS,
+        "far012",
         268_000_000,
         3_000_000,
-    )(queries, level_index, *l0, *l1, *l2, *l3, *parts)
+    )(queries, level_index, *l0, *l1, *l2, *parts)
     flat, squares = call(
-        last_kernel, (mixed, f32(8, 128)), 3 + 2 * CHUNKS, "last", 67_000_000, 3_000_000
-    )(queries, level_index, *up[0], *up[1], near)
-
-    turned = call(turn_kernel, f32(TOK, HEADS * DV), 2, "turn", 1_000_000, 2_000_000)(
+        last_kernel, (mixed, f32(8, 128)), 3 + 3 * CHUNKS, "last", 67_000_000, 3_000_000
+    )(queries, level_index, *l3, *up[0], *up[1], near)
+
+    scaled = call(gain_kernel, mixed, 2, "gain", 1_000_000, 2_000_000)(
         flat, norm_gain.reshape(1, HEADS * DV)
     )
     def over_head(x, move):
@@ -316,10 +314,7 @@
         )
 
     squares = squares + over_head(squares, lambda x, c: (x, 1 - c))
-    one = over_head(squares, lambda x, c: (x ^ (1 if c == 0 else 3), c))
-    two = over_head(squares, lambda x, c: (x ^ 2, c))
-    three = over_head(one, lambda x, c: (x, 1 - c))
-    others = (one, two, three)
+    others = [over_head(squares, lambda x, c, k=k: (x ^ k, 1 - c)) for k in (1, 3, 2)]
     return call(
         norm_kernel,
         bf16(TOK, HEADS * DV),
@@ -329,7 +324,7 @@
         1_500_000,
         out_specs=HBM,
         scratch=[pltpu.VMEM((TOK, HEADS * DV), jnp.bfloat16), pltpu.SemaphoreType.DMA((8,))],
-    )(turned, squares, *others)
+    )(scaled, squares, *others)
 
 
 def solution(mesh):

time: 46.4 us -> 45.3 us (0.976)
  waiting for transfers between devices: 12.7 us -> 11.8 us
    ppermute x6, waiting for transfers between devices: 9.57 us -> 7.93 us  [over_ctx(): return [lax.ppermute(x, 'ctx', pairs) for x in chunks]]
    ppermute x4, waiting for transfers between devices: 3.13 us -> 3.88 us  [over_head(): lax.ppermute(x, 'head', [(i, to[0] * 2 + to[1]) for i, to in ((i, move(*x...]
where the time goes in v3:
time: 45.3 us; the launch traced here: 45.2 us
  starting transfers between devices  24.7 us (55%)
  waiting for transfers between devices  11.8 us (26%)
  Pallas kernels  8.58 us (19%)
    ppermute x6, starting transfers between devices, over_ctx(): return [lax.ppermute(x, 'ctx', pairs) for x in chunks]  14.7 us
    ppermute x4, starting transfers between devices, over_head(): lax.ppermute(x, 'head', [(i, to[0] * 2 + to[1]) for i, to in ((i, move(*x...  9.96 us
    ppermute x6, waiting for transfers between devices, over_ctx(): return [lax.ppermute(x, 'ctx', pairs) for x in chunks]  7.93 us
    pallas_call x2, Pallas kernels, on_device(): call(functools.partial(local_kernel, p * half, half), f32(half * DV, TOK)...  4.3 us
    ppermute x4, waiting for transfers between devices, over_head(): lax.ppermute(x, 'head', [(i, to[0] * 2 + to[1]) for i, to in ((i, move(*x...  3.88 us
    pallas_call x1, Pallas kernels, on_device(): call(summary_kernel, [state] * CHUNKS + [bf16(TOK, HEADS * DK), bf16(HEAD...  2.02 us
    pallas_call x1, Pallas kernels, on_device(): call(norm_kernel, bf16(TOK, HEADS * DV), 5, 'norm', 1000000, 1500000, out...  0.93 us
  transfers between devices with their start and end apart: 10, of which 8 were waited for; matrix products, arithmetic and copies ran while one was open for 0% of the time, Pallas kernels for 11%

profile of v3, /device:TPU:1, one launch (start us, length us, event | category | flops | bytes accessed | tf_op | source)
XLA Modules:
  0.0 45.2 jit_solution(17316382177319577188)
XLA Ops:
  0.0 0.0 copy-start.1
  0.0 2.0 %summary.1 = (f32[256,128]{1,0:T(8,128)S(1)}, bf16[1024,512]{1,0:T(8,128)(2,1)S(1)}, bf16[256,1024]{1,0:T(8,128)(2,1)S(1)}) custom-call(bf16[1024,512]{1,0:T(8,128)(2,1)} %k_hbm.1, bf16[1024,256]{1,0:T(8,128)(2,1)} %v_hbm.1), custom_call_target="tpu_custom_call" | custom-call | flops 268000000 | bytes 3200000 | tf_op jit(solution)/shard_map/summary/pallas_call | solution.py:248
  2.0 2.6 %collective-permute-start = (f32[256,128]{1,0:T(8,128)S(1)}, f32[256,128]{1,0:T(8,128)S(1)}, u32[]{:S(2)}, u32[]{:S(2)}) collective-permute-start(f32[256,128]{1,0:T(8,128)S(1)} %get-tuple-element.14), channel_id=1, source_target_pairs={{0,8},{8,0},{16,24},{24,16},{32,40},{40,32},{48,56},{56,48},{64,72... | collective-permute-start | bytes 393224 | tf_op jit(solution)/shard_map/ppermute | solution.py:243
  4.6 0.0 copy-done.1
  4.6 0.0 copy-done
  4.6 2.2 %local0.1.refs_3_ = f32[128,1024]{1,0:T(8,128)S(1)} custom-call(bf16[1024,512]{1,0:T(8,128)(2,1)S(1)} %copy-done, bf16[1024,512]{1,0:T(8,128)(2,1)S(1)} %get-tuple-element.15.k_ref, bf16[256,1024]{1,0:T(8,128)(2,1)S(1)} %get-tuple-element.16.vt_ref, s32[10,4,1024]{2,1,0:T(4,128)S(1)} %copy-done.1), custom_call_target="tpu_custom_call" | custom-call | flops 1000000000 | bytes 2000000 | tf_op jit(solution)/shard_map/local0/pallas_call | solution.py:266
  6.8 0.2 collective-permute-done.refs_0_
  7.0 4.8 %collective-permute-start.1 = (f32[256,128]{1,0:T(8,128)S(1)}, f32[256,128]{1,0:T(8,128)S(1)}, u32[]{:S(2)}, u32[]{:S(2)}) collective-permute-start(f32[256,128]{1,0:T(8,128)S(1)} %add.12), channel_id=1, source_target_pairs={{0,24},{8,16},{16,8},{24,0},{32,56},{40,48},{48,40},{56,32},{64,88... | collective-permute-start | bytes 393224 | tf_op jit(solution)/shard_map/ppermute | solution.py:243
  11.8 2.2 %local1.1.refs_4_ = f32[128,1024]{1,0:T(8,128)S(1)} custom-call(bf16[1024,512]{1,0:T(8,128)(2,1)S(1)} %copy-done, bf16[1024,512]{1,0:T(8,128)(2,1)S(1)} %get-tuple-element.15.k_ref, bf16[256,1024]{1,0:T(8,128)(2,1)S(1)} %get-tuple-element.16.vt_ref, s32[10,4,1024]{2,1,0:T(4,128)S(1)} %copy-done.1), custom_call_target="tpu_custom_call" | custom-call | flops 1000000000 | bytes 2000000 | tf_op jit(solution)/shard_map/local1/pallas_call | solution.py:266
  13.9 0.3 collective-permute-done.1.refs_1_
  14.3 4.6 %collective-permute-start.2 = (f32[256,128]{1,0:T(8,128)S(1)}, f32[256,128]{1,0:T(8,128)S(1)}, u32[]{:S(2)}, u32[]{:S(2)}) collective-permute-start(f32[256,128]{1,0:T(8,128)S(1)} %add.13), channel_id=1, source_target_pairs={{0,56},{8,48},{16,40},{24,32},{32,24},{40,16},{48,8},{56,0},{64,12... | collective-permute-start | bytes 393224 | tf_op jit(solution)/shard_map/ppermute | solution.py:243
  18.8 3.8 %collective-permute-done.2.refs_2_ = f32[256,128]{1,0:T(8,128)S(1)} collective-permute-done((f32[256,128]{1,0:T(8,128)S(1)}, f32[256,128]{1,0:T(8,128)S(1)}, u32[]{:S(2)}, u32[]{:S(2)}) %collective-permute-start.2) | collective-permute-done | bytes 131104 | tf_op jit(solution)/shard_map/ppermute | solution.py:243
  22.6 2.0 %collective-permute-start.5 = (f32[256,128]{1,0:T(8,128)S(1)}, f32[256,128]{1,0:T(8,128)S(1)}, u32[]{:S(2)}, u32[]{:S(2)}) collective-permute-start(f32[256,128]{1,0:T(8,128)S(1)} %add.14), channel_id=1, source_target_pairs={{0,128},{8,136},{16,144},{24,152},{32,160},{40,168},{48,176},{56,1... | collective-permute-start | bytes 393224 | tf_op jit(solution)/shard_map/ppermute | solution.py:243
  24.6 0.8 %collective-permute-start.4 = (f32[256,128]{1,0:T(8,128)S(1)}, f32[256,128]{1,0:T(8,128)S(1)}, u32[]{:S(2)}, u32[]{:S(2)}) collective-permute-start(f32[256,128]{1,0:T(8,128)S(1)} %add.14), channel_id=1, source_target_pairs={{0,192},{8,200},{16,208},{24,216},{32,224},{40,232},{48,240},{56,2... | collective-permute-start | bytes 393224 | tf_op jit(solution)/shard_map/ppermute | solution.py:243
  25.4 0.0 collective-permute-start.3
  25.4 0.6 %far012.1.refs_3_ = f32[256,1024]{1,0:T(8,128)S(1)} custom-call(bf16[1024,512]{1,0:T(8,128)(2,1)S(1)} %copy-done, s32[10,4,1024]{2,1,0:T(4,128)S(1)} %copy-done.1, f32[256,128]{1,0:T(8,128)S(1)} %collective-permute-done.refs_0_, f32[256,128]{1,0:T(8,128)S(1)} %collective-permute-done.1.refs_1_, f32[256,128]{1,0:T(8,128)S(1)} %collective-permute-done.2.refs_2_, ...), custom_call_target="tpu_custom_call" | custom-call | flops 268000000 | bytes 3000000 | tf_op jit(solution)/shard_map/far012/pallas_call | solution.py:295
  26.0 2.0 %collective-permute-done.5.refs_2_ = f32[256,128]{1,0:T(8,128)S(1)} collective-permute-done((f32[256,128]{1,0:T(8,128)S(1)}, f32[256,128]{1,0:T(8,128)S(1)}, u32[]{:S(2)}, u32[]{:S(2)}) %collective-permute-start.5) | collective-permute-done | bytes 131104 | tf_op jit(solution)/shard_map/ppermute | solution.py:243
  28.0 1.6 %collective-permute-done.4.refs_1_ = f32[256,128]{1,0:T(8,128)S(1)} collective-permute-done((f32[256,128]{1,0:T(8,128)S(1)}, f32[256,128]{1,0:T(8,128)S(1)}, u32[]{:S(2)}, u32[]{:S(2)}) %collective-permute-start.4) | collective-permute-done | bytes 131104 | tf_op jit(solution)/shard_map/ppermute | solution.py:243
  29.6 0.0 collective-permute-done.3.refs_0_
  29.6 0.5 %last.1 = (f32[256,1024]{1,0:T(8,128)S(1)}, f32[8,128]{1,0:T(8,128)S(1)}) custom-call(bf16[1024,512]{1,0:T(8,128)(2,1)S(1)} %copy-done, s32[10,4,1024]{2,1,0:T(4,128)S(1)} %copy-done.1, f32[256,128]{1,0:T(8,128)S(1)} %collective-permute-done.3.refs_0_, f32[256,128]{1,0:T(8,128)S(1)} %collective-permute-done.4.refs_1_, ...), custom_call_target="tpu_custom_call" | custom-call | flops 67000000 | bytes 3000000 | tf_op jit(solution)/shard_map/last/pallas_call | solution.py:303
  30.1 0.0 copy-start.2
  30.2 6.1 %collective-permute-start.6 = (f32[8,128]{1,0:T(8,128)S(1)}, f32[8,128]{1,0:T(8,128)S(1)}, u32[]{:S(2)}, u32[]{:S(2)}) collective-permute-start(f32[8,128]{1,0:T(8,128)S(1)} %get-tuple-element.22), channel_id=1, source_target_pairs={{0,1},{1,0},{2,3},{3,2},{4,5},{5,4},{6,7},{7,6},{8,9},{9,8},{10,11... | collective-permute-start | bytes 12296 | tf_op jit(solution)/shard_map/ppermute | solution.py:312
  36.2 0.8 %collective-permute-done.6 = f32[8,128]{1,0:T(8,128)S(1)} collective-permute-done((f32[8,128]{1,0:T(8,128)S(1)}, f32[8,128]{1,0:T(8,128)S(1)}, u32[]{:S(2)}, u32[]{:S(2)}) %collective-permute-start.6) | collective-permute-done | bytes 4128 | tf_op jit(solution)/shard_map/ppermute | solution.py:312
  37.1 3.0 %collective-permute-start.9 = (f32[8,128]{1,0:T(8,128)S(1)}, f32[8,128]{1,0:T(8,128)S(1)}, u32[]{:S(2)}, u32[]{:S(2)}) collective-permute-start(f32[8,128]{1,0:T(8,128)S(1)} %add.15.s0), channel_id=1, source_target_pairs={{0,5},{1,4},{2,7},{3,6},{4,1},{5,0},{6,3},{7,2},{8,13},{9,12},{10,... | collective-permute-start | bytes 12296 | tf_op jit(solution)/shard_map/ppermute | solution.py:312
  40.0 0.9 %collective-permute-start.8 = (f32[8,128]{1,0:T(8,128)S(1)}, f32[8,128]{1,0:T(8,128)S(1)}, u32[]{:S(2)}, u32[]{:S(2)}) collective-permute-start(f32[8,128]{1,0:T(8,128)S(1)} %add.15.s0), channel_id=1, source_target_pairs={{0,7},{1,6},{2,5},{3,4},{4,3},{5,2},{6,1},{7,0},{8,15},{9,14},{10,... | collective-permute-start | bytes 12296 | tf_op jit(solution)/shard_map/ppermute | solution.py:312
  40.9 0.0 collective-permute-start.7
  40.9 0.0 copy-done.2
  41.0 0.3 gain.1.m_ref
  41.2 0.4 collective-permute-done.9.s3
  41.6 2.7 %collective-permute-done.8.s2 = f32[8,128]{1,0:T(8,128)S(1)} collective-permute-done((f32[8,128]{1,0:T(8,128)S(1)}, f32[8,128]{1,0:T(8,128)S(1)}, u32[]{:S(2)}, u32[]{:S(2)}) %collective-permute-start.8) | collective-permute-done | bytes 4128 | tf_op jit(solution)/shard_map/ppermute | solution.py:312
  44.3 0.0 collective-permute-done.7.s1
  44.3 0.9 %norm.1 = bf16[1024,256]{1,0:T(8,128)(2,1)} custom-call(f32[256,1024]{1,0:T(8,128)S(1)} %gain.1.m_ref, f32[8,128]{1,0:T(8,128)S(1)} %add.15.s0, f32[8,128]{1,0:T(8,128)S(1)} %collective-permute-done.7.s1, f32[8,128]{1,0:T(8,128)S(1)} %collective-permute-done.8.s2, f32[8,128]{1,0:T(8,128)S(1)} %collective-permute-done.9.s3), custom_call_target="tpu_custom_call" | custom-call | flops 1000000 | bytes 1500000 | tf_op jit(solution)/shard_map/norm/pallas_call | solution.py:318
  (6 shorter events, 0.1 us)
Async XLA Ops:
  0.0 4.6 %copy-start.1 = (s32[10,4,1024]{2,1,0:T(4,128)S(1)}, s32[10,4,1024]{2,1,0:T(4,128)}, u32[]{:S(2)}) copy-start(s32[10,4,1024]{2,1,0:T(4,128)} %li_ref.7) | copy-start | bytes 491524
  0.0 4.6 %copy-start = (bf16[1024,512]{1,0:T(8,128)(2,1)S(1)}, bf16[1024,512]{1,0:T(8,128)(2,1)}, u32[]{:S(2)}) copy-start(bf16[1024,512]{1,0:T(8,128)(2,1)} %q_ref.7) | copy-start | bytes 3145732
  2.0 4.9 %collective-permute-start = (f32[256,128]{1,0:T(8,128)S(1)}, f32[256,128]{1,0:T(8,128)S(1)}, u32[]{:S(2)}, u32[]{:S(2)}) collective-permute-start(f32[256,128]{1,0:T(8,128)S(1)} %get-tuple-element.14), channel_id=1, source_target_pairs={{0,8},{8,0},{16,24},{24,16},{32,40},{40,32},{48,56},{56,48},{64,72... | collective-permute-start | bytes 393224 | tf_op jit(solution)/shard_map/ppermute | solution.py:243
  7.0 7.3 %collective-permute-start.1 = (f32[256,128]{1,0:T(8,128)S(1)}, f32[256,128]{1,0:T(8,128)S(1)}, u32[]{:S(2)}, u32[]{:S(2)}) collective-permute-start(f32[256,128]{1,0:T(8,128)S(1)} %add.12), channel_id=1, source_target_pairs={{0,24},{8,16},{16,8},{24,0},{32,56},{40,48},{48,40},{56,32},{64,88... | collective-permute-start | bytes 393224 | tf_op jit(solution)/shard_map/ppermute | solution.py:243
  14.3 8.3 %collective-permute-start.2 = (f32[256,128]{1,0:T(8,128)S(1)}, f32[256,128]{1,0:T(8,128)S(1)}, u32[]{:S(2)}, u32[]{:S(2)}) collective-permute-start(f32[256,128]{1,0:T(8,128)S(1)} %add.13), channel_id=1, source_target_pairs={{0,56},{8,48},{16,40},{24,32},{32,24},{40,16},{48,8},{56,0},{64,12... | collective-permute-start | bytes 393224 | tf_op jit(solution)/shard_map/ppermute | solution.py:243
  22.6 5.4 %collective-permute-start.5 = (f32[256,128]{1,0:T(8,128)S(1)}, f32[256,128]{1,0:T(8,128)S(1)}, u32[]{:S(2)}, u32[]{:S(2)}) collective-permute-start(f32[256,128]{1,0:T(8,128)S(1)} %add.14), channel_id=1, source_target_pairs={{0,128},{8,136},{16,144},{24,152},{32,160},{40,168},{48,176},{56,1... | collective-permute-start | bytes 393224 | tf_op jit(solution)/shard_map/ppermute | solution.py:243
  24.6 5.0 %collective-permute-start.4 = (f32[256,128]{1,0:T(8,128)S(1)}, f32[256,128]{1,0:T(8,128)S(1)}, u32[]{:S(2)}, u32[]{:S(2)}) collective-permute-start(f32[256,128]{1,0:T(8,128)S(1)} %add.14), channel_id=1, source_target_pairs={{0,192},{8,200},{16,208},{24,216},{32,224},{40,232},{48,240},{56,2... | collective-permute-start | bytes 393224 | tf_op jit(solution)/shard_map/ppermute | solution.py:243
  25.4 4.3 %collective-permute-start.3 = (f32[256,128]{1,0:T(8,128)S(1)}, f32[256,128]{1,0:T(8,128)S(1)}, u32[]{:S(2)}, u32[]{:S(2)}) collective-permute-start(f32[256,128]{1,0:T(8,128)S(1)} %add.14), channel_id=1, source_target_pairs={{0,64},{8,72},{16,80},{24,88},{32,96},{40,104},{48,112},{56,120},{... | collective-permute-start | bytes 393224 | tf_op jit(solution)/shard_map/ppermute | solution.py:243
  30.1 10.8 %copy-start.2 = (bf16[256]{0:T(256)(128)(2,1)S(1)}, bf16[256]{0:T(256)(128)(2,1)}, u32[]{:S(2)}) copy-start(bf16[256]{0:T(256)(128)(2,1)} %param.8) | copy-start | bytes 1540
  30.2 6.9 %collective-permute-start.6 = (f32[8,128]{1,0:T(8,128)S(1)}, f32[8,128]{1,0:T(8,128)S(1)}, u32[]{:S(2)}, u32[]{:S(2)}) collective-permute-start(f32[8,128]{1,0:T(8,128)S(1)} %get-tuple-element.22), channel_id=1, source_target_pairs={{0,1},{1,0},{2,3},{3,2},{4,5},{5,4},{6,7},{7,6},{8,9},{9,8},{10,11... | collective-permute-start | bytes 12296 | tf_op jit(solution)/shard_map/ppermute | solution.py:312
  37.1 4.5 %collective-permute-start.9 = (f32[8,128]{1,0:T(8,128)S(1)}, f32[8,128]{1,0:T(8,128)S(1)}, u32[]{:S(2)}, u32[]{:S(2)}) collective-permute-start(f32[8,128]{1,0:T(8,128)S(1)} %add.15.s0), channel_id=1, source_target_pairs={{0,5},{1,4},{2,7},{3,6},{4,1},{5,0},{6,3},{7,2},{8,13},{9,12},{10,... | collective-permute-start | bytes 12296 | tf_op jit(solution)/shard_map/ppermute | solution.py:312
  40.0 4.2 %collective-permute-start.8 = (f32[8,128]{1,0:T(8,128)S(1)}, f32[8,128]{1,0:T(8,128)S(1)}, u32[]{:S(2)}, u32[]{:S(2)}) collective-permute-start(f32[8,128]{1,0:T(8,128)S(1)} %add.15.s0), channel_id=1, source_target_pairs={{0,7},{1,6},{2,5},{3,4},{4,3},{5,2},{6,1},{7,0},{8,15},{9,14},{10,... | collective-permute-start | bytes 12296 | tf_op jit(solution)/shard_map/ppermute | solution.py:312
  40.9 3.3 %collective-permute-start.7 = (f32[8,128]{1,0:T(8,128)S(1)}, f32[8,128]{1,0:T(8,128)S(1)}, u32[]{:S(2)}, u32[]{:S(2)}) collective-permute-start(f32[8,128]{1,0:T(8,128)S(1)} %add.15.s0), channel_id=1, source_target_pairs={{0,3},{1,2},{2,1},{3,0},{4,7},{5,6},{6,5},{7,4},{8,11},{9,10},{10,... | collective-permute-start | bytes 12296 | tf_op jit(solution)/shard_map/ppermute | solution.py:312

commit v4 on v3

--- a/solution.py
+++ b/solution.py
@@ -14,6 +14,7 @@
 HEADS = 4
 TOK = 1024
 BLK = 256
+SUM_BLK = 512
 Z = 8
 VMEM_LIMIT = 32 * 1024 * 1024
 CHUNKS = 1
@@ -40,8 +41,8 @@
 def summary_kernel(k_hbm, v_hbm, *refs):
     outs, (k_ref, vt_ref, v_ref, sems) = refs[:CHUNKS], refs[CHUNKS:]
     copies = []
-    for b in range(TOK // BLK):
-        rows = pl.ds(b * BLK, BLK)
+    for b in range(TOK // SUM_BLK):
+        rows = pl.ds(b * SUM_BLK, SUM_BLK)
         pair = (
             pltpu.make_async_copy(v_hbm.at[rows], v_ref.at[rows], sems.at[0, b]),
             pltpu.make_async_copy(k_hbm.at[rows], k_ref.at[rows], sems.at[1, b]),
@@ -50,15 +51,15 @@
             copy.start()
         copies.append(pair)
     totals = [None] * HEADS
-    for b in range(TOK // BLK):
+    for b in range(TOK // SUM_BLK):
         for copy in copies[b]:
             copy.wait()
-        r0 = b * BLK
-        vt = v_ref[r0 : r0 + BLK, :].T
-        vt_ref[:, r0 : r0 + BLK] = vt
+        r0 = b * SUM_BLK
+        vt = v_ref[r0 : r0 + SUM_BLK, :].T
+        vt_ref[:, r0 : r0 + SUM_BLK] = vt
         for h in range(HEADS):
             part = dot(
-                vt[h * DV : (h + 1) * DV, :], k_ref[r0 : r0 + BLK, h * DK : (h + 1) * DK], NN
+                vt[h * DV : (h + 1) * DV, :], k_ref[r0 : r0 + SUM_BLK, h * DK : (h + 1) * DK], NN
             )
             totals[h] = part if b == 0 else totals[h] + part
     for h in range(HEADS):
@@ -255,7 +256,7 @@
         in_specs=[HBM, HBM],
         scratch=[
             pltpu.VMEM((TOK, HEADS * DV), jnp.bfloat16),
-            pltpu.SemaphoreType.DMA((2, TOK // BLK)),
+            pltpu.SemaphoreType.DMA((2, TOK // SUM_BLK)),
         ],
     )(in_hbm(keys), in_hbm(values))
 
@@ -287,7 +288,7 @@
     l1 = over_ctx(pair, lambda y, z: (y, z ^ 3))
     l1[-1], parts[1] = lax.optimization_barrier((l1[-1], parts[1]))
     quad = add(pair, l1)
-    hop = (7, 6, 5, 4, 3, 2, 1, 0)
+    hop = (7, 6, 5, 4, 2, 3, 0, 1)
     l2 = over_ctx(quad, lambda y, z: (y, hop[z]))
     group = add(quad, l2)
     l3 = over_ctx(group, lambda y, z: (y ^ 1, z))
@@ -314,7 +315,10 @@
         )
 
     squares = squares + over_head(squares, lambda x, c: (x, 1 - c))
-    others = [over_head(squares, lambda x, c, k=k: (x ^ k, 1 - c)) for k in (1, 3, 2)]
+    one = over_head(squares, lambda x, c: (x ^ (1 if c == 0 else 3), 1 - c))
+    two = over_head(squares, lambda x, c: (x ^ 2, c))
+    three = over_head(one, lambda x, c: (x, 1 - c))
+    others = (one, two, three)
     return call(
         norm_kernel,
         bf16(TOK, HEADS * DV),

time: 45.3 us -> 44 us (0.971)
  waiting for transfers between devices: 11.8 us -> 9.97 us
  starting transfers between devices: 24.7 us -> 25.4 us
    ppermute x4, waiting for transfers between devices: 3.88 us -> 2.86 us  [over_head(): lax.ppermute(x, 'head', [(i, to[0] * 2 + to[1]) for i, to in ((i, move(*x...]
    ppermute x6, starting transfers between devices: 14.7 us -> 15.7 us  [over_ctx(): return [lax.ppermute(x, 'ctx', pairs) for x in chunks]]
    ppermute x6, waiting for transfers between devices: 7.93 us -> 7.11 us  [over_ctx(): return [lax.ppermute(x, 'ctx', pairs) for x in chunks]]
  transfers between devices with their start and end apart: 10 -> 10, of which waited for: 8 -> 8; matrix products, arithmetic and copies ran while one was open for 0% -> 0% of each run, Pallas kernels for 11% -> 12%
where the time goes in v4:
time: 44 us; the launch traced here: 43.9 us
  starting transfers between devices  25.4 us (58%)
  waiting for transfers between devices  9.97 us (23%)
  Pallas kernels  8.4 us (19%)
    ppermute x6, starting transfers between devices, over_ctx(): return [lax.ppermute(x, 'ctx', pairs) for x in chunks]  15.7 us
    ppermute x4, starting transfers between devices, over_head(): lax.ppermute(x, 'head', [(i, to[0] * 2 + to[1]) for i, to in ((i, move(*x...  9.7 us
    ppermute x6, waiting for transfers between devices, over_ctx(): return [lax.ppermute(x, 'ctx', pairs) for x in chunks]  7.11 us
    pallas_call x2, Pallas kernels, on_device(): call(functools.partial(local_kernel, p * half, half), f32(half * DV, TOK)...  4.3 us
    ppermute x4, waiting for transfers between devices, over_head(): lax.ppermute(x, 'head', [(i, to[0] * 2 + to[1]) for i, to in ((i, move(*x...  2.86 us
    pallas_call x1, Pallas kernels, on_device(): call(summary_kernel, [state] * CHUNKS + [bf16(TOK, HEADS * DK), bf16(HEAD...  1.83 us
    pallas_call x1, Pallas kernels, on_device(): call(norm_kernel, bf16(TOK, HEADS * DV), 5, 'norm', 1000000, 1500000, out...  0.93 us
  transfers between devices with their start and end apart: 10, of which 8 were waited for; matrix products, arithmetic and copies ran while one was open for 0% of the time, Pallas kernels for 12%

profile of v4, /device:TPU:1, one launch (start us, length us, event | category | flops | bytes accessed | tf_op | source)
XLA Modules:
  0.0 43.9 jit_solution(13932253991822210076)
XLA Ops:
  0.0 0.0 copy-start.1
  0.0 1.8 %summary.1 = (f32[256,128]{1,0:T(8,128)S(1)}, bf16[1024,512]{1,0:T(8,128)(2,1)S(1)}, bf16[256,1024]{1,0:T(8,128)(2,1)S(1)}) custom-call(bf16[1024,512]{1,0:T(8,128)(2,1)} %k_hbm.1, bf16[1024,256]{1,0:T(8,128)(2,1)} %v_hbm.1), custom_call_target="tpu_custom_call" | custom-call | flops 268000000 | bytes 3200000 | tf_op jit(solution)/shard_map/summary/pallas_call | solution.py:249
  1.8 2.6 %collective-permute-start = (f32[256,128]{1,0:T(8,128)S(1)}, f32[256,128]{1,0:T(8,128)S(1)}, u32[]{:S(2)}, u32[]{:S(2)}) collective-permute-start(f32[256,128]{1,0:T(8,128)S(1)} %get-tuple-element.14), channel_id=1, source_target_pairs={{0,8},{8,0},{16,24},{24,16},{32,40},{40,32},{48,56},{56,48},{64,72... | collective-permute-start | bytes 393224 | tf_op jit(solution)/shard_map/ppermute | solution.py:244
  4.4 0.0 copy-done.1
  4.4 0.0 copy-done
  4.4 2.2 %local0.1.refs_3_ = f32[128,1024]{1,0:T(8,128)S(1)} custom-call(bf16[1024,512]{1,0:T(8,128)(2,1)S(1)} %copy-done, bf16[1024,512]{1,0:T(8,128)(2,1)S(1)} %get-tuple-element.15.k_ref, bf16[256,1024]{1,0:T(8,128)(2,1)S(1)} %get-tuple-element.16.vt_ref, s32[10,4,1024]{2,1,0:T(4,128)S(1)} %copy-done.1), custom_call_target="tpu_custom_call" | custom-call | flops 1000000000 | bytes 2000000 | tf_op jit(solution)/shard_map/local0/pallas_call | solution.py:267
  6.6 0.2 collective-permute-done.refs_0_
  6.8 4.8 %collective-permute-start.1 = (f32[256,128]{1,0:T(8,128)S(1)}, f32[256,128]{1,0:T(8,128)S(1)}, u32[]{:S(2)}, u32[]{:S(2)}) collective-permute-start(f32[256,128]{1,0:T(8,128)S(1)} %add.12), channel_id=1, source_target_pairs={{0,24},{8,16},{16,8},{24,0},{32,56},{40,48},{48,40},{56,32},{64,88... | collective-permute-start | bytes 393224 | tf_op jit(solution)/shard_map/ppermute | solution.py:244
  11.6 2.2 %local1.1.refs_4_ = f32[128,1024]{1,0:T(8,128)S(1)} custom-call(bf16[1024,512]{1,0:T(8,128)(2,1)S(1)} %copy-done, bf16[1024,512]{1,0:T(8,128)(2,1)S(1)} %get-tuple-element.15.k_ref, bf16[256,1024]{1,0:T(8,128)(2,1)S(1)} %get-tuple-element.16.vt_ref, s32[10,4,1024]{2,1,0:T(4,128)S(1)} %copy-done.1), custom_call_target="tpu_custom_call" | custom-call | flops 1000000000 | bytes 2000000 | tf_op jit(solution)/shard_map/local1/pallas_call | solution.py:267
  13.7 0.3 collective-permute-done.1.refs_1_
  14.1 4.6 %collective-permute-start.2 = (f32[256,128]{1,0:T(8,128)S(1)}, f32[256,128]{1,0:T(8,128)S(1)}, u32[]{:S(2)}, u32[]{:S(2)}) collective-permute-start(f32[256,128]{1,0:T(8,128)S(1)} %add.13), channel_id=1, source_target_pairs={{0,56},{8,48},{16,40},{24,32},{32,16},{40,24},{48,0},{56,8},{64,12... | collective-permute-start | bytes 393224 | tf_op jit(solution)/shard_map/ppermute | solution.py:244
  18.6 3.0 %collective-permute-done.2.refs_2_ = f32[256,128]{1,0:T(8,128)S(1)} collective-permute-done((f32[256,128]{1,0:T(8,128)S(1)}, f32[256,128]{1,0:T(8,128)S(1)}, u32[]{:S(2)}, u32[]{:S(2)}) %collective-permute-start.2) | collective-permute-done | bytes 131104 | tf_op jit(solution)/shard_map/ppermute | solution.py:244
  21.6 3.0 %collective-permute-start.5 = (f32[256,128]{1,0:T(8,128)S(1)}, f32[256,128]{1,0:T(8,128)S(1)}, u32[]{:S(2)}, u32[]{:S(2)}) collective-permute-start(f32[256,128]{1,0:T(8,128)S(1)} %add.14), channel_id=1, source_target_pairs={{0,128},{8,136},{16,144},{24,152},{32,160},{40,168},{48,176},{56,1... | collective-permute-start | bytes 393224 | tf_op jit(solution)/shard_map/ppermute | solution.py:244
  24.6 0.8 %collective-permute-start.4 = (f32[256,128]{1,0:T(8,128)S(1)}, f32[256,128]{1,0:T(8,128)S(1)}, u32[]{:S(2)}, u32[]{:S(2)}) collective-permute-start(f32[256,128]{1,0:T(8,128)S(1)} %add.14), channel_id=1, source_target_pairs={{0,192},{8,200},{16,208},{24,216},{32,224},{40,232},{48,240},{56,2... | collective-permute-start | bytes 393224 | tf_op jit(solution)/shard_map/ppermute | solution.py:244
  25.4 0.0 collective-permute-start.3
  25.4 0.6 %far012.1.refs_3_ = f32[256,1024]{1,0:T(8,128)S(1)} custom-call(bf16[1024,512]{1,0:T(8,128)(2,1)S(1)} %copy-done, s32[10,4,1024]{2,1,0:T(4,128)S(1)} %copy-done.1, f32[256,128]{1,0:T(8,128)S(1)} %collective-permute-done.refs_0_, f32[256,128]{1,0:T(8,128)S(1)} %collective-permute-done.1.refs_1_, f32[256,128]{1,0:T(8,128)S(1)} %collective-permute-done.2.refs_2_, ...), custom_call_target="tpu_custom_call" | custom-call | flops 268000000 | bytes 3000000 | tf_op jit(solution)/shard_map/far012/pallas_call | solution.py:296
  26.0 1.0 %collective-permute-done.5.refs_2_ = f32[256,128]{1,0:T(8,128)S(1)} collective-permute-done((f32[256,128]{1,0:T(8,128)S(1)}, f32[256,128]{1,0:T(8,128)S(1)}, u32[]{:S(2)}, u32[]{:S(2)}) %collective-permute-start.5) | collective-permute-done | bytes 131104 | tf_op jit(solution)/shard_map/ppermute | solution.py:244
  27.0 2.6 %collective-permute-done.4.refs_1_ = f32[256,128]{1,0:T(8,128)S(1)} collective-permute-done((f32[256,128]{1,0:T(8,128)S(1)}, f32[256,128]{1,0:T(8,128)S(1)}, u32[]{:S(2)}, u32[]{:S(2)}) %collective-permute-start.4) | collective-permute-done | bytes 131104 | tf_op jit(solution)/shard_map/ppermute | solution.py:244
  29.6 0.0 collective-permute-done.3.refs_0_
  29.6 0.5 %last.1 = (f32[256,1024]{1,0:T(8,128)S(1)}, f32[8,128]{1,0:T(8,128)S(1)}) custom-call(bf16[1024,512]{1,0:T(8,128)(2,1)S(1)} %copy-done, s32[10,4,1024]{2,1,0:T(4,128)S(1)} %copy-done.1, f32[256,128]{1,0:T(8,128)S(1)} %collective-permute-done.3.refs_0_, f32[256,128]{1,0:T(8,128)S(1)} %collective-permute-done.4.refs_1_, ...), custom_call_target="tpu_custom_call" | custom-call | flops 67000000 | bytes 3000000 | tf_op jit(solution)/shard_map/last/pallas_call | solution.py:304
  30.1 0.0 copy-start.2
  30.1 5.3 %collective-permute-start.6 = (f32[8,128]{1,0:T(8,128)S(1)}, f32[8,128]{1,0:T(8,128)S(1)}, u32[]{:S(2)}, u32[]{:S(2)}) collective-permute-start(f32[8,128]{1,0:T(8,128)S(1)} %get-tuple-element.22), channel_id=1, source_target_pairs={{0,1},{1,0},{2,3},{3,2},{4,5},{5,4},{6,7},{7,6},{8,9},{9,8},{10,11... | collective-permute-start | bytes 12296 | tf_op jit(solution)/shard_map/ppermute | solution.py:313
  35.5 0.8 %collective-permute-done.6 = f32[8,128]{1,0:T(8,128)S(1)} collective-permute-done((f32[8,128]{1,0:T(8,128)S(1)}, f32[8,128]{1,0:T(8,128)S(1)}, u32[]{:S(2)}, u32[]{:S(2)}) %collective-permute-start.6) | collective-permute-done | bytes 4128 | tf_op jit(solution)/shard_map/ppermute | solution.py:313
  36.3 2.7 %collective-permute-start.7 = (f32[8,128]{1,0:T(8,128)S(1)}, f32[8,128]{1,0:T(8,128)S(1)}, u32[]{:S(2)}, u32[]{:S(2)}) collective-permute-start(f32[8,128]{1,0:T(8,128)S(1)} %add.15.s0), channel_id=1, source_target_pairs={{0,3},{1,6},{2,1},{3,4},{4,7},{5,2},{6,5},{7,0},{8,11},{9,14},{10,... | collective-permute-start | bytes 12296 | tf_op jit(solution)/shard_map/ppermute | solution.py:313
  39.0 0.5 %collective-permute-start.8 = (f32[8,128]{1,0:T(8,128)S(1)}, f32[8,128]{1,0:T(8,128)S(1)}, u32[]{:S(2)}, u32[]{:S(2)}) collective-permute-start(f32[8,128]{1,0:T(8,128)S(1)} %add.15.s0), channel_id=1, source_target_pairs={{0,4},{1,5},{2,6},{3,7},{4,0},{5,1},{6,2},{7,3},{8,12},{9,13},{10,... | collective-permute-start | bytes 12296 | tf_op jit(solution)/shard_map/ppermute | solution.py:313
  39.5 0.2 collective-permute-done.7.s1
  39.8 1.1 %collective-permute-start.9 = (f32[8,128]{1,0:T(8,128)S(1)}, f32[8,128]{1,0:T(8,128)S(1)}, u32[]{:S(2)}, u32[]{:S(2)}) collective-permute-start(f32[8,128]{1,0:T(8,128)S(1)} %collective-permute-done.7.s1), channel_id=1, source_target_pairs={{0,1},{1,0},{2,3},{3,2},{4,5},{5,4},{6,7},{7,6},{8,9},{9,8},{10,11... | collective-permute-start | bytes 12296 | tf_op jit(solution)/shard_map/ppermute | solution.py:313
  40.9 0.0 copy-done.2
  40.9 0.3 gain.1.m_ref
  41.2 1.8 %collective-permute-done.8.s2 = f32[8,128]{1,0:T(8,128)S(1)} collective-permute-done((f32[8,128]{1,0:T(8,128)S(1)}, f32[8,128]{1,0:T(8,128)S(1)}, u32[]{:S(2)}, u32[]{:S(2)}) %collective-permute-start.8) | collective-permute-done | bytes 4128 | tf_op jit(solution)/shard_map/ppermute | solution.py:313
  43.0 0.0 collective-permute-done.9.s3
  43.0 0.9 %norm.1 = bf16[1024,256]{1,0:T(8,128)(2,1)} custom-call(f32[256,1024]{1,0:T(8,128)S(1)} %gain.1.m_ref, f32[8,128]{1,0:T(8,128)S(1)} %add.15.s0, f32[8,128]{1,0:T(8,128)S(1)} %collective-permute-done.7.s1, f32[8,128]{1,0:T(8,128)S(1)} %collective-permute-done.8.s2, f32[8,128]{1,0:T(8,128)S(1)} %collective-permute-done.9.s3), custom_call_target="tpu_custom_call" | custom-call | flops 1000000 | bytes 1500000 | tf_op jit(solution)/shard_map/norm/pallas_call | solution.py:322
  (6 shorter events, 0.1 us)
Async XLA Ops:
  0.0 4.4 %copy-start.1 = (s32[10,4,1024]{2,1,0:T(4,128)S(1)}, s32[10,4,1024]{2,1,0:T(4,128)}, u32[]{:S(2)}) copy-start(s32[10,4,1024]{2,1,0:T(4,128)} %li_ref.7) | copy-start | bytes 491524
  0.0 4.4 %copy-start = (bf16[1024,512]{1,0:T(8,128)(2,1)S(1)}, bf16[1024,512]{1,0:T(8,128)(2,1)}, u32[]{:S(2)}) copy-start(bf16[1024,512]{1,0:T(8,128)(2,1)} %q_ref.7) | copy-start | bytes 3145732
  1.8 4.9 %collective-permute-start = (f32[256,128]{1,0:T(8,128)S(1)}, f32[256,128]{1,0:T(8,128)S(1)}, u32[]{:S(2)}, u32[]{:S(2)}) collective-permute-start(f32[256,128]{1,0:T(8,128)S(1)} %get-tuple-element.14), channel_id=1, source_target_pairs={{0,8},{8,0},{16,24},{24,16},{32,40},{40,32},{48,56},{56,48},{64,72... | collective-permute-start | bytes 393224 | tf_op jit(solution)/shard_map/ppermute | solution.py:244
  6.8 7.3 %collective-permute-start.1 = (f32[256,128]{1,0:T(8,128)S(1)}, f32[256,128]{1,0:T(8,128)S(1)}, u32[]{:S(2)}, u32[]{:S(2)}) collective-permute-start(f32[256,128]{1,0:T(8,128)S(1)} %add.12), channel_id=1, source_target_pairs={{0,24},{8,16},{16,8},{24,0},{32,56},{40,48},{48,40},{56,32},{64,88... | collective-permute-start | bytes 393224 | tf_op jit(solution)/shard_map/ppermute | solution.py:244
  14.1 7.5 %collective-permute-start.2 = (f32[256,128]{1,0:T(8,128)S(1)}, f32[256,128]{1,0:T(8,128)S(1)}, u32[]{:S(2)}, u32[]{:S(2)}) collective-permute-start(f32[256,128]{1,0:T(8,128)S(1)} %add.13), channel_id=1, source_target_pairs={{0,56},{8,48},{16,40},{24,32},{32,16},{40,24},{48,0},{56,8},{64,12... | collective-permute-start | bytes 393224 | tf_op jit(solution)/shard_map/ppermute | solution.py:244
  21.6 5.4 %collective-permute-start.5 = (f32[256,128]{1,0:T(8,128)S(1)}, f32[256,128]{1,0:T(8,128)S(1)}, u32[]{:S(2)}, u32[]{:S(2)}) collective-permute-start(f32[256,128]{1,0:T(8,128)S(1)} %add.14), channel_id=1, source_target_pairs={{0,128},{8,136},{16,144},{24,152},{32,160},{40,168},{48,176},{56,1... | collective-permute-start | bytes 393224 | tf_op jit(solution)/shard_map/ppermute | solution.py:244
  24.6 5.0 %collective-permute-start.4 = (f32[256,128]{1,0:T(8,128)S(1)}, f32[256,128]{1,0:T(8,128)S(1)}, u32[]{:S(2)}, u32[]{:S(2)}) collective-permute-start(f32[256,128]{1,0:T(8,128)S(1)} %add.14), channel_id=1, source_target_pairs={{0,192},{8,200},{16,208},{24,216},{32,224},{40,232},{48,240},{56,2... | collective-permute-start | bytes 393224 | tf_op jit(solution)/shard_map/ppermute | solution.py:244
  25.4 4.3 %collective-permute-start.3 = (f32[256,128]{1,0:T(8,128)S(1)}, f32[256,128]{1,0:T(8,128)S(1)}, u32[]{:S(2)}, u32[]{:S(2)}) collective-permute-start(f32[256,128]{1,0:T(8,128)S(1)} %add.14), channel_id=1, source_target_pairs={{0,64},{8,72},{16,80},{24,88},{32,96},{40,104},{48,112},{56,120},{... | collective-permute-start | bytes 393224 | tf_op jit(solution)/shard_map/ppermute | solution.py:244
  30.1 10.8 %copy-start.2 = (bf16[256]{0:T(256)(128)(2,1)S(1)}, bf16[256]{0:T(256)(128)(2,1)}, u32[]{:S(2)}) copy-start(bf16[256]{0:T(256)(128)(2,1)} %param.8) | copy-start | bytes 1540
  30.1 6.2 %collective-permute-start.6 = (f32[8,128]{1,0:T(8,128)S(1)}, f32[8,128]{1,0:T(8,128)S(1)}, u32[]{:S(2)}, u32[]{:S(2)}) collective-permute-start(f32[8,128]{1,0:T(8,128)S(1)} %get-tuple-element.22), channel_id=1, source_target_pairs={{0,1},{1,0},{2,3},{3,2},{4,5},{5,4},{6,7},{7,6},{8,9},{9,8},{10,11... | collective-permute-start | bytes 12296 | tf_op jit(solution)/shard_map/ppermute | solution.py:313
  36.3 3.5 %collective-permute-start.7 = (f32[8,128]{1,0:T(8,128)S(1)}, f32[8,128]{1,0:T(8,128)S(1)}, u32[]{:S(2)}, u32[]{:S(2)}) collective-permute-start(f32[8,128]{1,0:T(8,128)S(1)} %add.15.s0), channel_id=1, source_target_pairs={{0,3},{1,6},{2,1},{3,4},{4,7},{5,2},{6,5},{7,0},{8,11},{9,14},{10,... | collective-permute-start | bytes 12296 | tf_op jit(solution)/shard_map/ppermute | solution.py:313
  39.0 4.0 %collective-permute-start.8 = (f32[8,128]{1,0:T(8,128)S(1)}, f32[8,128]{1,0:T(8,128)S(1)}, u32[]{:S(2)}, u32[]{:S(2)}) collective-permute-start(f32[8,128]{1,0:T(8,128)S(1)} %add.15.s0), channel_id=1, source_target_pairs={{0,4},{1,5},{2,6},{3,7},{4,0},{5,1},{6,2},{7,3},{8,12},{9,13},{10,... | collective-permute-start | bytes 12296 | tf_op jit(solution)/shard_map/ppermute | solution.py:313
  39.8 3.2 %collective-permute-start.9 = (f32[8,128]{1,0:T(8,128)S(1)}, f32[8,128]{1,0:T(8,128)S(1)}, u32[]{:S(2)}, u32[]{:S(2)}) collective-permute-start(f32[8,128]{1,0:T(8,128)S(1)} %collective-permute-done.7.s1), channel_id=1, source_target_pairs={{0,1},{1,0},{2,3},{3,2},{4,5},{5,4},{6,7},{7,6},{8,9},{9,8},{10,11... | collective-permute-start | bytes 12296 | tf_op jit(solution)/shard_map/ppermute | solution.py:313

commit v5 on v4

--- a/solution.py
+++ b/solution.py
@@ -235,13 +235,14 @@
     state = f32(PER * DV, DK)
     mixed = f32(HEADS * DV, TOK)
 
-    def over_ctx(chunks, move):
+    def over_ctx(chunks, move, other=None):
+        moves = (move, other or move)
         pairs = []
         for r in range(ctx):
-            to = move(r // Z, r % Z)
-            if to is not None:
-                pairs.append((r, to[0] * Z + to[1]))
-        return [lax.ppermute(x, "ctx", pairs) for x in chunks]
+            for h in range(8):
+                y, z = moves[h % 2](r // Z, r % Z)
+                pairs.append((r * 8 + h, (y * Z + z) * 8 + h))
+        return [lax.ppermute(x, ("ctx", "head"), pairs) for x in chunks]
 
     def add(a, b):
         return [x + y for x, y in zip(a, b)]
@@ -289,7 +290,7 @@
     l1[-1], parts[1] = lax.optimization_barrier((l1[-1], parts[1]))
     quad = add(pair, l1)
     hop = (7, 6, 5, 4, 2, 3, 0, 1)
-    l2 = over_ctx(quad, lambda y, z: (y, hop[z]))
+    l2 = over_ctx(quad, lambda y, z: (y, hop[z]), lambda y, z: (y, 7 - z))
     group = add(quad, l2)
     l3 = over_ctx(group, lambda y, z: (y ^ 1, z))
     up = [over_ctx(group, lambda y, z, k=k: (y ^ k, z)) for k in (3, 2)]

time: 44 us -> 43.9 us (level)
  starting transfers between devices: 25.4 us -> 24.5 us
  waiting for transfers between devices: 9.97 us -> 10.8 us
    ppermute x6, starting transfers between devices: 15.7 us -> 14.7 us  [over_ctx(): return [lax.ppermute(x, ('ctx', 'head'), pairs) for x in chunks]]
    ppermute x6, waiting for transfers between devices: 7.11 us -> 7.92 us  [over_ctx(): return [lax.ppermute(x, ('ctx', 'head'), pairs) for x in chunks]]
where the time goes in v5:
time: 43.9 us; the launch traced here: 43.8 us
  starting transfers between devices  24.5 us (56%)
  waiting for transfers between devices  10.8 us (25%)
  Pallas kernels  8.4 us (19%)
    ppermute x6, starting transfers between devices, over_ctx(): return [lax.ppermute(x, ('ctx', 'head'), pairs) for x in chunks]  14.7 us
    ppermute x4, starting transfers between devices, over_head(): lax.ppermute(x, 'head', [(i, to[0] * 2 + to[1]) for i, to in ((i, move(*x...  9.78 us
    ppermute x6, waiting for transfers between devices, over_ctx(): return [lax.ppermute(x, ('ctx', 'head'), pairs) for x in chunks]  7.92 us
    pallas_call x2, Pallas kernels, on_device(): call(functools.partial(local_kernel, p * half, half), f32(half * DV, TOK)...  4.3 us
    ppermute x4, waiting for transfers between devices, over_head(): lax.ppermute(x, 'head', [(i, to[0] * 2 + to[1]) for i, to in ((i, move(*x...  2.86 us
    pallas_call x1, Pallas kernels, on_device(): call(summary_kernel, [state] * CHUNKS + [bf16(TOK, HEADS * DK), bf16(HEAD...  1.83 us
    pallas_call x1, Pallas kernels, on_device(): call(norm_kernel, bf16(TOK, HEADS * DV), 5, 'norm', 1000000, 1500000, out...  0.93 us
  transfers between devices with their start and end apart: 10, of which 8 were waited for; matrix products, arithmetic and copies ran while one was open for 0% of the time, Pallas kernels for 12%

profile of v5, /device:TPU:1, one launch (start us, length us, event | category | flops | bytes accessed | tf_op | source)
XLA Modules:
  0.0 43.8 jit_solution(13198392047507659988)
XLA Ops:
  0.0 0.0 copy-start.1
  0.0 1.8 %summary.1 = (f32[256,128]{1,0:T(8,128)S(1)}, bf16[1024,512]{1,0:T(8,128)(2,1)S(1)}, bf16[256,1024]{1,0:T(8,128)(2,1)S(1)}) custom-call(bf16[1024,512]{1,0:T(8,128)(2,1)} %k_hbm.1, bf16[1024,256]{1,0:T(8,128)(2,1)} %v_hbm.1), custom_call_target="tpu_custom_call" | custom-call | flops 268000000 | bytes 3200000 | tf_op jit(solution)/shard_map/summary/pallas_call | solution.py:250
  1.8 2.6 %collective-permute-start = (f32[256,128]{1,0:T(8,128)S(1)}, f32[256,128]{1,0:T(8,128)S(1)}, u32[]{:S(2)}, u32[]{:S(2)}) collective-permute-start(f32[256,128]{1,0:T(8,128)S(1)} %get-tuple-element.14), channel_id=1, source_target_pairs={{0,8},{1,9},{2,10},{3,11},{4,12},{5,13},{6,14},{7,15},{8,0},{9,1},... | collective-permute-start | bytes 393224 | tf_op jit(solution)/shard_map/ppermute | solution.py:245
  4.4 0.0 copy-done.1
  4.4 0.0 copy-done
  4.4 2.2 %local0.1.refs_3_ = f32[128,1024]{1,0:T(8,128)S(1)} custom-call(bf16[1024,512]{1,0:T(8,128)(2,1)S(1)} %copy-done, bf16[1024,512]{1,0:T(8,128)(2,1)S(1)} %get-tuple-element.15.k_ref, bf16[256,1024]{1,0:T(8,128)(2,1)S(1)} %get-tuple-element.16.vt_ref, s32[10,4,1024]{2,1,0:T(4,128)S(1)} %copy-done.1), custom_call_target="tpu_custom_call" | custom-call | flops 1000000000 | bytes 2000000 | tf_op jit(solution)/shard_map/local0/pallas_call | solution.py:268
  6.6 0.2 collective-permute-done.refs_0_
  6.8 4.8 %collective-permute-start.1 = (f32[256,128]{1,0:T(8,128)S(1)}, f32[256,128]{1,0:T(8,128)S(1)}, u32[]{:S(2)}, u32[]{:S(2)}) collective-permute-start(f32[256,128]{1,0:T(8,128)S(1)} %add.12), channel_id=1, source_target_pairs={{0,24},{1,25},{2,26},{3,27},{4,28},{5,29},{6,30},{7,31},{8,16},{9,... | collective-permute-start | bytes 393224 | tf_op jit(solution)/shard_map/ppermute | solution.py:245
  11.6 2.2 %local1.1.refs_4_ = f32[128,1024]{1,0:T(8,128)S(1)} custom-call(bf16[1024,512]{1,0:T(8,128)(2,1)S(1)} %copy-done, bf16[1024,512]{1,0:T(8,128)(2,1)S(1)} %get-tuple-element.15.k_ref, bf16[256,1024]{1,0:T(8,128)(2,1)S(1)} %get-tuple-element.16.vt_ref, s32[10,4,1024]{2,1,0:T(4,128)S(1)} %copy-done.1), custom_call_target="tpu_custom_call" | custom-call | flops 1000000000 | bytes 2000000 | tf_op jit(solution)/shard_map/local1/pallas_call | solution.py:268
  13.7 0.3 collective-permute-done.1.refs_1_
  14.1 4.6 %collective-permute-start.2 = (f32[256,128]{1,0:T(8,128)S(1)}, f32[256,128]{1,0:T(8,128)S(1)}, u32[]{:S(2)}, u32[]{:S(2)}) collective-permute-start(f32[256,128]{1,0:T(8,128)S(1)} %add.13), channel_id=1, source_target_pairs={{0,56},{1,57},{2,58},{3,59},{4,60},{5,61},{6,62},{7,63},{8,48},{9,... | collective-permute-start | bytes 393224 | tf_op jit(solution)/shard_map/ppermute | solution.py:245
  18.6 3.8 %collective-permute-done.2.refs_2_ = f32[256,128]{1,0:T(8,128)S(1)} collective-permute-done((f32[256,128]{1,0:T(8,128)S(1)}, f32[256,128]{1,0:T(8,128)S(1)}, u32[]{:S(2)}, u32[]{:S(2)}) %collective-permute-start.2) | collective-permute-done | bytes 131104 | tf_op jit(solution)/shard_map/ppermute | solution.py:245
  22.4 2.0 %collective-permute-start.5 = (f32[256,128]{1,0:T(8,128)S(1)}, f32[256,128]{1,0:T(8,128)S(1)}, u32[]{:S(2)}, u32[]{:S(2)}) collective-permute-start(f32[256,128]{1,0:T(8,128)S(1)} %add.14), channel_id=1, source_target_pairs={{0,128},{1,129},{2,130},{3,131},{4,132},{5,133},{6,134},{7,135},{8... | collective-permute-start | bytes 393224 | tf_op jit(solution)/shard_map/ppermute | solution.py:245
  24.4 0.8 %collective-permute-start.4 = (f32[256,128]{1,0:T(8,128)S(1)}, f32[256,128]{1,0:T(8,128)S(1)}, u32[]{:S(2)}, u32[]{:S(2)}) collective-permute-start(f32[256,128]{1,0:T(8,128)S(1)} %add.14), channel_id=1, source_target_pairs={{0,192},{1,193},{2,194},{3,195},{4,196},{5,197},{6,198},{7,199},{8... | collective-permute-start | bytes 393224 | tf_op jit(solution)/shard_map/ppermute | solution.py:245
  25.2 0.0 collective-permute-start.3
  25.2 0.6 %far012.1.refs_3_ = f32[256,1024]{1,0:T(8,128)S(1)} custom-call(bf16[1024,512]{1,0:T(8,128)(2,1)S(1)} %copy-done, s32[10,4,1024]{2,1,0:T(4,128)S(1)} %copy-done.1, f32[256,128]{1,0:T(8,128)S(1)} %collective-permute-done.refs_0_, f32[256,128]{1,0:T(8,128)S(1)} %collective-permute-done.1.refs_1_, f32[256,128]{1,0:T(8,128)S(1)} %collective-permute-done.2.refs_2_, ...), custom_call_target="tpu_custom_call" | custom-call | flops 268000000 | bytes 3000000 | tf_op jit(solution)/shard_map/far012/pallas_call | solution.py:297
  25.8 2.0 %collective-permute-done.5.refs_2_ = f32[256,128]{1,0:T(8,128)S(1)} collective-permute-done((f32[256,128]{1,0:T(8,128)S(1)}, f32[256,128]{1,0:T(8,128)S(1)}, u32[]{:S(2)}, u32[]{:S(2)}) %collective-permute-start.5) | collective-permute-done | bytes 131104 | tf_op jit(solution)/shard_map/ppermute | solution.py:245
  27.8 1.6 %collective-permute-done.4.refs_1_ = f32[256,128]{1,0:T(8,128)S(1)} collective-permute-done((f32[256,128]{1,0:T(8,128)S(1)}, f32[256,128]{1,0:T(8,128)S(1)}, u32[]{:S(2)}, u32[]{:S(2)}) %collective-permute-start.4) | collective-permute-done | bytes 131104 | tf_op jit(solution)/shard_map/ppermute | solution.py:245
  29.4 0.0 collective-permute-done.3.refs_0_
  29.4 0.5 %last.1 = (f32[256,1024]{1,0:T(8,128)S(1)}, f32[8,128]{1,0:T(8,128)S(1)}) custom-call(bf16[1024,512]{1,0:T(8,128)(2,1)S(1)} %copy-done, s32[10,4,1024]{2,1,0:T(4,128)S(1)} %copy-done.1, f32[256,128]{1,0:T(8,128)S(1)} %collective-permute-done.3.refs_0_, f32[256,128]{1,0:T(8,128)S(1)} %collective-permute-done.4.refs_1_, ...), custom_call_target="tpu_custom_call" | custom-call | flops 67000000 | bytes 3000000 | tf_op jit(solution)/shard_map/last/pallas_call | solution.py:305
  29.9 0.0 copy-start.2
  30.0 5.4 %collective-permute-start.6 = (f32[8,128]{1,0:T(8,128)S(1)}, f32[8,128]{1,0:T(8,128)S(1)}, u32[]{:S(2)}, u32[]{:S(2)}) collective-permute-start(f32[8,128]{1,0:T(8,128)S(1)} %get-tuple-element.22), channel_id=1, source_target_pairs={{0,1},{1,0},{2,3},{3,2},{4,5},{5,4},{6,7},{7,6},{8,9},{9,8},{10,11... | collective-permute-start | bytes 12296 | tf_op jit(solution)/shard_map/ppermute | solution.py:314
  35.4 0.8 %collective-permute-done.6 = f32[8,128]{1,0:T(8,128)S(1)} collective-permute-done((f32[8,128]{1,0:T(8,128)S(1)}, f32[8,128]{1,0:T(8,128)S(1)}, u32[]{:S(2)}, u32[]{:S(2)}) %collective-permute-start.6) | collective-permute-done | bytes 4128 | tf_op jit(solution)/shard_map/ppermute | solution.py:314
  36.2 2.7 %collective-permute-start.7 = (f32[8,128]{1,0:T(8,128)S(1)}, f32[8,128]{1,0:T(8,128)S(1)}, u32[]{:S(2)}, u32[]{:S(2)}) collective-permute-start(f32[8,128]{1,0:T(8,128)S(1)} %add.15.s0), channel_id=1, source_target_pairs={{0,3},{1,6},{2,1},{3,4},{4,7},{5,2},{6,5},{7,0},{8,11},{9,14},{10,... | collective-permute-start | bytes 12296 | tf_op jit(solution)/shard_map/ppermute | solution.py:314
  38.9 0.5 %collective-permute-start.8 = (f32[8,128]{1,0:T(8,128)S(1)}, f32[8,128]{1,0:T(8,128)S(1)}, u32[]{:S(2)}, u32[]{:S(2)}) collective-permute-start(f32[8,128]{1,0:T(8,128)S(1)} %add.15.s0), channel_id=1, source_target_pairs={{0,4},{1,5},{2,6},{3,7},{4,0},{5,1},{6,2},{7,3},{8,12},{9,13},{10,... | collective-permute-start | bytes 12296 | tf_op jit(solution)/shard_map/ppermute | solution.py:314
  39.4 0.2 collective-permute-done.7.s1
  39.7 1.1 %collective-permute-start.9 = (f32[8,128]{1,0:T(8,128)S(1)}, f32[8,128]{1,0:T(8,128)S(1)}, u32[]{:S(2)}, u32[]{:S(2)}) collective-permute-start(f32[8,128]{1,0:T(8,128)S(1)} %collective-permute-done.7.s1), channel_id=1, source_target_pairs={{0,1},{1,0},{2,3},{3,2},{4,5},{5,4},{6,7},{7,6},{8,9},{9,8},{10,11... | collective-permute-start | bytes 12296 | tf_op jit(solution)/shard_map/ppermute | solution.py:314
  40.8 0.0 copy-done.2
  40.8 0.3 gain.1.m_ref
  41.1 1.8 %collective-permute-done.8.s2 = f32[8,128]{1,0:T(8,128)S(1)} collective-permute-done((f32[8,128]{1,0:T(8,128)S(1)}, f32[8,128]{1,0:T(8,128)S(1)}, u32[]{:S(2)}, u32[]{:S(2)}) %collective-permute-start.8) | collective-permute-done | bytes 4128 | tf_op jit(solution)/shard_map/ppermute | solution.py:314
  42.9 0.0 collective-permute-done.9.s3
  42.9 0.9 %norm.1 = bf16[1024,256]{1,0:T(8,128)(2,1)} custom-call(f32[256,1024]{1,0:T(8,128)S(1)} %gain.1.m_ref, f32[8,128]{1,0:T(8,128)S(1)} %add.15.s0, f32[8,128]{1,0:T(8,128)S(1)} %collective-permute-done.7.s1, f32[8,128]{1,0:T(8,128)S(1)} %collective-permute-done.8.s2, f32[8,128]{1,0:T(8,128)S(1)} %collective-permute-done.9.s3), custom_call_target="tpu_custom_call" | custom-call | flops 1000000 | bytes 1500000 | tf_op jit(solution)/shard_map/norm/pallas_call | solution.py:323
  (6 shorter events, 0.1 us)
Async XLA Ops:
  0.0 4.4 %copy-start.1 = (s32[10,4,1024]{2,1,0:T(4,128)S(1)}, s32[10,4,1024]{2,1,0:T(4,128)}, u32[]{:S(2)}) copy-start(s32[10,4,1024]{2,1,0:T(4,128)} %li_ref.7) | copy-start | bytes 491524
  0.0 4.4 %copy-start = (bf16[1024,512]{1,0:T(8,128)(2,1)S(1)}, bf16[1024,512]{1,0:T(8,128)(2,1)}, u32[]{:S(2)}) copy-start(bf16[1024,512]{1,0:T(8,128)(2,1)} %q_ref.7) | copy-start | bytes 3145732
  1.8 4.9 %collective-permute-start = (f32[256,128]{1,0:T(8,128)S(1)}, f32[256,128]{1,0:T(8,128)S(1)}, u32[]{:S(2)}, u32[]{:S(2)}) collective-permute-start(f32[256,128]{1,0:T(8,128)S(1)} %get-tuple-element.14), channel_id=1, source_target_pairs={{0,8},{1,9},{2,10},{3,11},{4,12},{5,13},{6,14},{7,15},{8,0},{9,1},... | collective-permute-start | bytes 393224 | tf_op jit(solution)/shard_map/ppermute | solution.py:245
  6.8 7.3 %collective-permute-start.1 = (f32[256,128]{1,0:T(8,128)S(1)}, f32[256,128]{1,0:T(8,128)S(1)}, u32[]{:S(2)}, u32[]{:S(2)}) collective-permute-start(f32[256,128]{1,0:T(8,128)S(1)} %add.12), channel_id=1, source_target_pairs={{0,24},{1,25},{2,26},{3,27},{4,28},{5,29},{6,30},{7,31},{8,16},{9,... | collective-permute-start | bytes 393224 | tf_op jit(solution)/shard_map/ppermute | solution.py:245
  14.1 8.3 %collective-permute-start.2 = (f32[256,128]{1,0:T(8,128)S(1)}, f32[256,128]{1,0:T(8,128)S(1)}, u32[]{:S(2)}, u32[]{:S(2)}) collective-permute-start(f32[256,128]{1,0:T(8,128)S(1)} %add.13), channel_id=1, source_target_pairs={{0,56},{1,57},{2,58},{3,59},{4,60},{5,61},{6,62},{7,63},{8,48},{9,... | collective-permute-start | bytes 393224 | tf_op jit(solution)/shard_map/ppermute | solution.py:245
  22.4 5.4 %collective-permute-start.5 = (f32[256,128]{1,0:T(8,128)S(1)}, f32[256,128]{1,0:T(8,128)S(1)}, u32[]{:S(2)}, u32[]{:S(2)}) collective-permute-start(f32[256,128]{1,0:T(8,128)S(1)} %add.14), channel_id=1, source_target_pairs={{0,128},{1,129},{2,130},{3,131},{4,132},{5,133},{6,134},{7,135},{8... | collective-permute-start | bytes 393224 | tf_op jit(solution)/shard_map/ppermute | solution.py:245
  24.4 5.0 %collective-permute-start.4 = (f32[256,128]{1,0:T(8,128)S(1)}, f32[256,128]{1,0:T(8,128)S(1)}, u32[]{:S(2)}, u32[]{:S(2)}) collective-permute-start(f32[256,128]{1,0:T(8,128)S(1)} %add.14), channel_id=1, source_target_pairs={{0,192},{1,193},{2,194},{3,195},{4,196},{5,197},{6,198},{7,199},{8... | collective-permute-start | bytes 393224 | tf_op jit(solution)/shard_map/ppermute | solution.py:245
  25.2 4.3 %collective-permute-start.3 = (f32[256,128]{1,0:T(8,128)S(1)}, f32[256,128]{1,0:T(8,128)S(1)}, u32[]{:S(2)}, u32[]{:S(2)}) collective-permute-start(f32[256,128]{1,0:T(8,128)S(1)} %add.14), channel_id=1, source_target_pairs={{0,64},{1,65},{2,66},{3,67},{4,68},{5,69},{6,70},{7,71},{8,72},{9,... | collective-permute-start | bytes 393224 | tf_op jit(solution)/shard_map/ppermute | solution.py:245
  29.9 10.9 %copy-start.2 = (bf16[256]{0:T(256)(128)(2,1)S(1)}, bf16[256]{0:T(256)(128)(2,1)}, u32[]{:S(2)}) copy-start(bf16[256]{0:T(256)(128)(2,1)} %param.8) | copy-start | bytes 1540
  30.0 6.2 %collective-permute-start.6 = (f32[8,128]{1,0:T(8,128)S(1)}, f32[8,128]{1,0:T(8,128)S(1)}, u32[]{:S(2)}, u32[]{:S(2)}) collective-permute-start(f32[8,128]{1,0:T(8,128)S(1)} %get-tuple-element.22), channel_id=1, source_target_pairs={{0,1},{1,0},{2,3},{3,2},{4,5},{5,4},{6,7},{7,6},{8,9},{9,8},{10,11... | collective-permute-start | bytes 12296 | tf_op jit(solution)/shard_map/ppermute | solution.py:314
  36.2 3.5 %collective-permute-start.7 = (f32[8,128]{1,0:T(8,128)S(1)}, f32[8,128]{1,0:T(8,128)S(1)}, u32[]{:S(2)}, u32[]{:S(2)}) collective-permute-start(f32[8,128]{1,0:T(8,128)S(1)} %add.15.s0), channel_id=1, source_target_pairs={{0,3},{1,6},{2,1},{3,4},{4,7},{5,2},{6,5},{7,0},{8,11},{9,14},{10,... | collective-permute-start | bytes 12296 | tf_op jit(solution)/shard_map/ppermute | solution.py:314
  38.9 4.0 %collective-permute-start.8 = (f32[8,128]{1,0:T(8,128)S(1)}, f32[8,128]{1,0:T(8,128)S(1)}, u32[]{:S(2)}, u32[]{:S(2)}) collective-permute-start(f32[8,128]{1,0:T(8,128)S(1)} %add.15.s0), channel_id=1, source_target_pairs={{0,4},{1,5},{2,6},{3,7},{4,0},{5,1},{6,2},{7,3},{8,12},{9,13},{10,... | collective-permute-start | bytes 12296 | tf_op jit(solution)/shard_map/ppermute | solution.py:314
  39.7 3.2 %collective-permute-start.9 = (f32[8,128]{1,0:T(8,128)S(1)}, f32[8,128]{1,0:T(8,128)S(1)}, u32[]{:S(2)}, u32[]{:S(2)}) collective-permute-start(f32[8,128]{1,0:T(8,128)S(1)} %collective-permute-done.7.s1), channel_id=1, source_target_pairs={{0,1},{1,0},{2,3},{3,2},{4,5},{5,4},{6,7},{7,6},{8,9},{9,8},{10,11... | collective-permute-start | bytes 12296 | tf_op jit(solution)/shard_map/ppermute | solution.py:314

commit v6 on v5

--- a/solution.py
+++ b/solution.py
@@ -293,7 +293,8 @@
     l2 = over_ctx(quad, lambda y, z: (y, hop[z]), lambda y, z: (y, 7 - z))
     group = add(quad, l2)
     l3 = over_ctx(group, lambda y, z: (y ^ 1, z))
-    up = [over_ctx(group, lambda y, z, k=k: (y ^ k, z)) for k in (3, 2)]
+    far = (2, 3, 1, 0)
+    up = [over_ctx(group, lambda y, z: (y ^ 3, z)), over_ctx(group, lambda y, z: (far[y], z))]
     near = call(
         functools.partial(far_kernel, (0, 1, 2)),
         mixed,

time: 43.9 us -> 43.9 us (level)
  no operation moved by 1% of the time
where the time goes in v6:
time: 43.9 us; the launch traced here: 43.8 us
  starting transfers between devices  24.4 us (56%)
  waiting for transfers between devices  10.8 us (25%)
  Pallas kernels  8.4 us (19%)
    ppermute x6, starting transfers between devices, over_ctx(): return [lax.ppermute(x, ('ctx', 'head'), pairs) for x in chunks]  14.7 us
    ppermute x4, starting transfers between devices, over_head(): lax.ppermute(x, 'head', [(i, to[0] * 2 + to[1]) for i, to in ((i, move(*x...  9.78 us
    ppermute x6, waiting for transfers between devices, over_ctx(): return [lax.ppermute(x, ('ctx', 'head'), pairs) for x in chunks]  7.94 us
    pallas_call x2, Pallas kernels, on_device(): call(functools.partial(local_kernel, p * half, half), f32(half * DV, TOK)...  4.3 us
    ppermute x4, waiting for transfers between devices, over_head(): lax.ppermute(x, 'head', [(i, to[0] * 2 + to[1]) for i, to in ((i, move(*x...  2.86 us
    pallas_call x1, Pallas kernels, on_device(): call(summary_kernel, [state] * CHUNKS + [bf16(TOK, HEADS * DK), bf16(HEAD...  1.83 us
    pallas_call x1, Pallas kernels, on_device(): call(norm_kernel, bf16(TOK, HEADS * DV), 5, 'norm', 1000000, 1500000, out...  0.93 us
  transfers between devices with their start and end apart: 10, of which 8 were waited for; matrix products, arithmetic and copies ran while one was open for 0% of the time, Pallas kernels for 12%

profile of v6, /device:TPU:1, one launch (start us, length us, event | category | flops | bytes accessed | tf_op | source)
XLA Modules:
  0.0 43.8 jit_solution(15598334760740986722)
XLA Ops:
  0.0 0.0 copy-start.1
  0.0 1.8 %summary.1 = (f32[256,128]{1,0:T(8,128)S(1)}, bf16[1024,512]{1,0:T(8,128)(2,1)S(1)}, bf16[256,1024]{1,0:T(8,128)(2,1)S(1)}) custom-call(bf16[1024,512]{1,0:T(8,128)(2,1)} %k_hbm.1, bf16[1024,256]{1,0:T(8,128)(2,1)} %v_hbm.1), custom_call_target="tpu_custom_call" | custom-call | flops 268000000 | bytes 3200000 | tf_op jit(solution)/shard_map/summary/pallas_call | solution.py:250
  1.8 2.6 %collective-permute-start = (f32[256,128]{1,0:T(8,128)S(1)}, f32[256,128]{1,0:T(8,128)S(1)}, u32[]{:S(2)}, u32[]{:S(2)}) collective-permute-start(f32[256,128]{1,0:T(8,128)S(1)} %get-tuple-element.14), channel_id=1, source_target_pairs={{0,8},{1,9},{2,10},{3,11},{4,12},{5,13},{6,14},{7,15},{8,0},{9,1},... | collective-permute-start | bytes 393224 | tf_op jit(solution)/shard_map/ppermute | solution.py:245
  4.4 0.0 copy-done.1
  4.4 0.0 copy-done
  4.4 2.2 %local0.1.refs_3_ = f32[128,1024]{1,0:T(8,128)S(1)} custom-call(bf16[1024,512]{1,0:T(8,128)(2,1)S(1)} %copy-done, bf16[1024,512]{1,0:T(8,128)(2,1)S(1)} %get-tuple-element.15.k_ref, bf16[256,1024]{1,0:T(8,128)(2,1)S(1)} %get-tuple-element.16.vt_ref, s32[10,4,1024]{2,1,0:T(4,128)S(1)} %copy-done.1), custom_call_target="tpu_custom_call" | custom-call | flops 1000000000 | bytes 2000000 | tf_op jit(solution)/shard_map/local0/pallas_call | solution.py:268
  6.6 0.2 collective-permute-done.refs_0_
  6.8 4.8 %collective-permute-start.1 = (f32[256,128]{1,0:T(8,128)S(1)}, f32[256,128]{1,0:T(8,128)S(1)}, u32[]{:S(2)}, u32[]{:S(2)}) collective-permute-start(f32[256,128]{1,0:T(8,128)S(1)} %add.12), channel_id=1, source_target_pairs={{0,24},{1,25},{2,26},{3,27},{4,28},{5,29},{6,30},{7,31},{8,16},{9,... | collective-permute-start | bytes 393224 | tf_op jit(solution)/shard_map/ppermute | solution.py:245
  11.6 2.2 %local1.1.refs_4_ = f32[128,1024]{1,0:T(8,128)S(1)} custom-call(bf16[1024,512]{1,0:T(8,128)(2,1)S(1)} %copy-done, bf16[1024,512]{1,0:T(8,128)(2,1)S(1)} %get-tuple-element.15.k_ref, bf16[256,1024]{1,0:T(8,128)(2,1)S(1)} %get-tuple-element.16.vt_ref, s32[10,4,1024]{2,1,0:T(4,128)S(1)} %copy-done.1), custom_call_target="tpu_custom_call" | custom-call | flops 1000000000 | bytes 2000000 | tf_op jit(solution)/shard_map/local1/pallas_call | solution.py:268
  13.7 0.3 collective-permute-done.1.refs_1_
  14.1 4.6 %collective-permute-start.2 = (f32[256,128]{1,0:T(8,128)S(1)}, f32[256,128]{1,0:T(8,128)S(1)}, u32[]{:S(2)}, u32[]{:S(2)}) collective-permute-start(f32[256,128]{1,0:T(8,128)S(1)} %add.13), channel_id=1, source_target_pairs={{0,56},{1,57},{2,58},{3,59},{4,60},{5,61},{6,62},{7,63},{8,48},{9,... | collective-permute-start | bytes 393224 | tf_op jit(solution)/shard_map/ppermute | solution.py:245
  18.6 3.8 %collective-permute-done.2.refs_2_ = f32[256,128]{1,0:T(8,128)S(1)} collective-permute-done((f32[256,128]{1,0:T(8,128)S(1)}, f32[256,128]{1,0:T(8,128)S(1)}, u32[]{:S(2)}, u32[]{:S(2)}) %collective-permute-start.2) | collective-permute-done | bytes 131104 | tf_op jit(solution)/shard_map/ppermute | solution.py:245
  22.4 2.0 %collective-permute-start.5 = (f32[256,128]{1,0:T(8,128)S(1)}, f32[256,128]{1,0:T(8,128)S(1)}, u32[]{:S(2)}, u32[]{:S(2)}) collective-permute-start(f32[256,128]{1,0:T(8,128)S(1)} %add.14), channel_id=1, source_target_pairs={{0,128},{1,129},{2,130},{3,131},{4,132},{5,133},{6,134},{7,135},{8... | collective-permute-start | bytes 393224 | tf_op jit(solution)/shard_map/ppermute | solution.py:245
  24.4 0.8 %collective-permute-start.4 = (f32[256,128]{1,0:T(8,128)S(1)}, f32[256,128]{1,0:T(8,128)S(1)}, u32[]{:S(2)}, u32[]{:S(2)}) collective-permute-start(f32[256,128]{1,0:T(8,128)S(1)} %add.14), channel_id=1, source_target_pairs={{0,192},{1,193},{2,194},{3,195},{4,196},{5,197},{6,198},{7,199},{8... | collective-permute-start | bytes 393224 | tf_op jit(solution)/shard_map/ppermute | solution.py:245
  25.2 0.0 collective-permute-start.3
  25.2 0.6 %far012.1.refs_3_ = f32[256,1024]{1,0:T(8,128)S(1)} custom-call(bf16[1024,512]{1,0:T(8,128)(2,1)S(1)} %copy-done, s32[10,4,1024]{2,1,0:T(4,128)S(1)} %copy-done.1, f32[256,128]{1,0:T(8,128)S(1)} %collective-permute-done.refs_0_, f32[256,128]{1,0:T(8,128)S(1)} %collective-permute-done.1.refs_1_, f32[256,128]{1,0:T(8,128)S(1)} %collective-permute-done.2.refs_2_, ...), custom_call_target="tpu_custom_call" | custom-call | flops 268000000 | bytes 3000000 | tf_op jit(solution)/shard_map/far012/pallas_call | solution.py:298
  25.8 1.8 %collective-permute-done.5.refs_2_ = f32[256,128]{1,0:T(8,128)S(1)} collective-permute-done((f32[256,128]{1,0:T(8,128)S(1)}, f32[256,128]{1,0:T(8,128)S(1)}, u32[]{:S(2)}, u32[]{:S(2)}) %collective-permute-start.5) | collective-permute-done | bytes 131104 | tf_op jit(solution)/shard_map/ppermute | solution.py:245
  27.5 1.9 %collective-permute-done.4.refs_1_ = f32[256,128]{1,0:T(8,128)S(1)} collective-permute-done((f32[256,128]{1,0:T(8,128)S(1)}, f32[256,128]{1,0:T(8,128)S(1)}, u32[]{:S(2)}, u32[]{:S(2)}) %collective-permute-start.4) | collective-permute-done | bytes 131104 | tf_op jit(solution)/shard_map/ppermute | solution.py:245
  29.4 0.0 collective-permute-done.3.refs_0_
  29.4 0.5 %last.1 = (f32[256,1024]{1,0:T(8,128)S(1)}, f32[8,128]{1,0:T(8,128)S(1)}) custom-call(bf16[1024,512]{1,0:T(8,128)(2,1)S(1)} %copy-done, s32[10,4,1024]{2,1,0:T(4,128)S(1)} %copy-done.1, f32[256,128]{1,0:T(8,128)S(1)} %collective-permute-done.3.refs_0_, f32[256,128]{1,0:T(8,128)S(1)} %collective-permute-done.4.refs_1_, ...), custom_call_target="tpu_custom_call" | custom-call | flops 67000000 | bytes 3000000 | tf_op jit(solution)/shard_map/last/pallas_call | solution.py:306
  29.9 0.0 copy-start.2
  29.9 5.4 %collective-permute-start.6 = (f32[8,128]{1,0:T(8,128)S(1)}, f32[8,128]{1,0:T(8,128)S(1)}, u32[]{:S(2)}, u32[]{:S(2)}) collective-permute-start(f32[8,128]{1,0:T(8,128)S(1)} %get-tuple-element.22), channel_id=1, source_target_pairs={{0,1},{1,0},{2,3},{3,2},{4,5},{5,4},{6,7},{7,6},{8,9},{9,8},{10,11... | collective-permute-start | bytes 12296 | tf_op jit(solution)/shard_map/ppermute | solution.py:315
  35.4 0.8 %collective-permute-done.6 = f32[8,128]{1,0:T(8,128)S(1)} collective-permute-done((f32[8,128]{1,0:T(8,128)S(1)}, f32[8,128]{1,0:T(8,128)S(1)}, u32[]{:S(2)}, u32[]{:S(2)}) %collective-permute-start.6) | collective-permute-done | bytes 4128 | tf_op jit(solution)/shard_map/ppermute | solution.py:315
  36.2 2.7 %collective-permute-start.7 = (f32[8,128]{1,0:T(8,128)S(1)}, f32[8,128]{1,0:T(8,128)S(1)}, u32[]{:S(2)}, u32[]{:S(2)}) collective-permute-start(f32[8,128]{1,0:T(8,128)S(1)} %add.15.s0), channel_id=1, source_target_pairs={{0,3},{1,6},{2,1},{3,4},{4,7},{5,2},{6,5},{7,0},{8,11},{9,14},{10,... | collective-permute-start | bytes 12296 | tf_op jit(solution)/shard_map/ppermute | solution.py:315
  38.9 0.5 %collective-permute-start.8 = (f32[8,128]{1,0:T(8,128)S(1)}, f32[8,128]{1,0:T(8,128)S(1)}, u32[]{:S(2)}, u32[]{:S(2)}) collective-permute-start(f32[8,128]{1,0:T(8,128)S(1)} %add.15.s0), channel_id=1, source_target_pairs={{0,4},{1,5},{2,6},{3,7},{4,0},{5,1},{6,2},{7,3},{8,12},{9,13},{10,... | collective-permute-start | bytes 12296 | tf_op jit(solution)/shard_map/ppermute | solution.py:315
  39.4 0.2 collective-permute-done.7.s1
  39.7 1.1 %collective-permute-start.9 = (f32[8,128]{1,0:T(8,128)S(1)}, f32[8,128]{1,0:T(8,128)S(1)}, u32[]{:S(2)}, u32[]{:S(2)}) collective-permute-start(f32[8,128]{1,0:T(8,128)S(1)} %collective-permute-done.7.s1), channel_id=1, source_target_pairs={{0,1},{1,0},{2,3},{3,2},{4,5},{5,4},{6,7},{7,6},{8,9},{9,8},{10,11... | collective-permute-start | bytes 12296 | tf_op jit(solution)/shard_map/ppermute | solution.py:315
  40.8 0.0 copy-done.2
  40.8 0.3 gain.1.m_ref
  41.1 1.8 %collective-permute-done.8.s2 = f32[8,128]{1,0:T(8,128)S(1)} collective-permute-done((f32[8,128]{1,0:T(8,128)S(1)}, f32[8,128]{1,0:T(8,128)S(1)}, u32[]{:S(2)}, u32[]{:S(2)}) %collective-permute-start.8) | collective-permute-done | bytes 4128 | tf_op jit(solution)/shard_map/ppermute | solution.py:315
  42.9 0.0 collective-permute-done.9.s3
  42.9 0.9 %norm.1 = bf16[1024,256]{1,0:T(8,128)(2,1)} custom-call(f32[256,1024]{1,0:T(8,128)S(1)} %gain.1.m_ref, f32[8,128]{1,0:T(8,128)S(1)} %add.15.s0, f32[8,128]{1,0:T(8,128)S(1)} %collective-permute-done.7.s1, f32[8,128]{1,0:T(8,128)S(1)} %collective-permute-done.8.s2, f32[8,128]{1,0:T(8,128)S(1)} %collective-permute-done.9.s3), custom_call_target="tpu_custom_call" | custom-call | flops 1000000 | bytes 1500000 | tf_op jit(solution)/shard_map/norm/pallas_call | solution.py:324
  (6 shorter events, 0.1 us)
Async XLA Ops:
  0.0 4.4 %copy-start.1 = (s32[10,4,1024]{2,1,0:T(4,128)S(1)}, s32[10,4,1024]{2,1,0:T(4,128)}, u32[]{:S(2)}) copy-start(s32[10,4,1024]{2,1,0:T(4,128)} %li_ref.7) | copy-start | bytes 491524
  0.0 4.4 %copy-start = (bf16[1024,512]{1,0:T(8,128)(2,1)S(1)}, bf16[1024,512]{1,0:T(8,128)(2,1)}, u32[]{:S(2)}) copy-start(bf16[1024,512]{1,0:T(8,128)(2,1)} %q_ref.7) | copy-start | bytes 3145732
  1.8 4.9 %collective-permute-start = (f32[256,128]{1,0:T(8,128)S(1)}, f32[256,128]{1,0:T(8,128)S(1)}, u32[]{:S(2)}, u32[]{:S(2)}) collective-permute-start(f32[256,128]{1,0:T(8,128)S(1)} %get-tuple-element.14), channel_id=1, source_target_pairs={{0,8},{1,9},{2,10},{3,11},{4,12},{5,13},{6,14},{7,15},{8,0},{9,1},... | collective-permute-start | bytes 393224 | tf_op jit(solution)/shard_map/ppermute | solution.py:245
  6.8 7.3 %collective-permute-start.1 = (f32[256,128]{1,0:T(8,128)S(1)}, f32[256,128]{1,0:T(8,128)S(1)}, u32[]{:S(2)}, u32[]{:S(2)}) collective-permute-start(f32[256,128]{1,0:T(8,128)S(1)} %add.12), channel_id=1, source_target_pairs={{0,24},{1,25},{2,26},{3,27},{4,28},{5,29},{6,30},{7,31},{8,16},{9,... | collective-permute-start | bytes 393224 | tf_op jit(solution)/shard_map/ppermute | solution.py:245
  14.1 8.3 %collective-permute-start.2 = (f32[256,128]{1,0:T(8,128)S(1)}, f32[256,128]{1,0:T(8,128)S(1)}, u32[]{:S(2)}, u32[]{:S(2)}) collective-permute-start(f32[256,128]{1,0:T(8,128)S(1)} %add.13), channel_id=1, source_target_pairs={{0,56},{1,57},{2,58},{3,59},{4,60},{5,61},{6,62},{7,63},{8,48},{9,... | collective-permute-start | bytes 393224 | tf_op jit(solution)/shard_map/ppermute | solution.py:245
  22.4 5.1 %collective-permute-start.5 = (f32[256,128]{1,0:T(8,128)S(1)}, f32[256,128]{1,0:T(8,128)S(1)}, u32[]{:S(2)}, u32[]{:S(2)}) collective-permute-start(f32[256,128]{1,0:T(8,128)S(1)} %add.14), channel_id=1, source_target_pairs={{0,128},{1,129},{2,130},{3,131},{4,132},{5,133},{6,134},{7,135},{8... | collective-permute-start | bytes 393224 | tf_op jit(solution)/shard_map/ppermute | solution.py:245
  24.4 5.0 %collective-permute-start.4 = (f32[256,128]{1,0:T(8,128)S(1)}, f32[256,128]{1,0:T(8,128)S(1)}, u32[]{:S(2)}, u32[]{:S(2)}) collective-permute-start(f32[256,128]{1,0:T(8,128)S(1)} %add.14), channel_id=1, source_target_pairs={{0,192},{1,193},{2,194},{3,195},{4,196},{5,197},{6,198},{7,199},{8... | collective-permute-start | bytes 393224 | tf_op jit(solution)/shard_map/ppermute | solution.py:245
  25.2 4.3 %collective-permute-start.3 = (f32[256,128]{1,0:T(8,128)S(1)}, f32[256,128]{1,0:T(8,128)S(1)}, u32[]{:S(2)}, u32[]{:S(2)}) collective-permute-start(f32[256,128]{1,0:T(8,128)S(1)} %add.14), channel_id=1, source_target_pairs={{0,64},{1,65},{2,66},{3,67},{4,68},{5,69},{6,70},{7,71},{8,72},{9,... | collective-permute-start | bytes 393224 | tf_op jit(solution)/shard_map/ppermute | solution.py:245
  29.9 10.9 %copy-start.2 = (bf16[256]{0:T(256)(128)(2,1)S(1)}, bf16[256]{0:T(256)(128)(2,1)}, u32[]{:S(2)}) copy-start(bf16[256]{0:T(256)(128)(2,1)} %param.8) | copy-start | bytes 1540
  29.9 6.2 %collective-permute-start.6 = (f32[8,128]{1,0:T(8,128)S(1)}, f32[8,128]{1,0:T(8,128)S(1)}, u32[]{:S(2)}, u32[]{:S(2)}) collective-permute-start(f32[8,128]{1,0:T(8,128)S(1)} %get-tuple-element.22), channel_id=1, source_target_pairs={{0,1},{1,0},{2,3},{3,2},{4,5},{5,4},{6,7},{7,6},{8,9},{9,8},{10,11... | collective-permute-start | bytes 12296 | tf_op jit(solution)/shard_map/ppermute | solution.py:315
  36.2 3.5 %collective-permute-start.7 = (f32[8,128]{1,0:T(8,128)S(1)}, f32[8,128]{1,0:T(8,128)S(1)}, u32[]{:S(2)}, u32[]{:S(2)}) collective-permute-start(f32[8,128]{1,0:T(8,128)S(1)} %add.15.s0), channel_id=1, source_target_pairs={{0,3},{1,6},{2,1},{3,4},{4,7},{5,2},{6,5},{7,0},{8,11},{9,14},{10,... | collective-permute-start | bytes 12296 | tf_op jit(solution)/shard_map/ppermute | solution.py:315
  38.9 4.0 %collective-permute-start.8 = (f32[8,128]{1,0:T(8,128)S(1)}, f32[8,128]{1,0:T(8,128)S(1)}, u32[]{:S(2)}, u32[]{:S(2)}) collective-permute-start(f32[8,128]{1,0:T(8,128)S(1)} %add.15.s0), channel_id=1, source_target_pairs={{0,4},{1,5},{2,6},{3,7},{4,0},{5,1},{6,2},{7,3},{8,12},{9,13},{10,... | collective-permute-start | bytes 12296 | tf_op jit(solution)/shard_map/ppermute | solution.py:315
  39.7 3.2 %collective-permute-start.9 = (f32[8,128]{1,0:T(8,128)S(1)}, f32[8,128]{1,0:T(8,128)S(1)}, u32[]{:S(2)}, u32[]{:S(2)}) collective-permute-start(f32[8,128]{1,0:T(8,128)S(1)} %collective-permute-done.7.s1), channel_id=1, source_target_pairs={{0,1},{1,0},{2,3},{3,2},{4,5},{5,4},{6,7},{7,6},{8,9},{9,8},{10,11... | collective-permute-start | bytes 12296 | tf_op jit(solution)/shard_map/ppermute | solution.py:315

commit v7 on v6

--- a/solution.py
+++ b/solution.py
@@ -289,7 +289,7 @@
     l1 = over_ctx(pair, lambda y, z: (y, z ^ 3))
     l1[-1], parts[1] = lax.optimization_barrier((l1[-1], parts[1]))
     quad = add(pair, l1)
-    hop = (7, 6, 5, 4, 2, 3, 0, 1)
+    hop = (7, 6, 4, 5, 2, 3, 0, 1)
     l2 = over_ctx(quad, lambda y, z: (y, hop[z]), lambda y, z: (y, 7 - z))
     group = add(quad, l2)
     l3 = over_ctx(group, lambda y, z: (y ^ 1, z))

time: 43.9 us -> 43.9 us (level)
  no operation moved by 1% of the time
where the time goes in v7:
time: 43.9 us; the launch traced here: 43.8 us
  starting transfers between devices  24.4 us (56%)
  waiting for transfers between devices  10.8 us (25%)
  Pallas kernels  8.4 us (19%)
    ppermute x6, starting transfers between devices, over_ctx(): return [lax.ppermute(x, ('ctx', 'head'), pairs) for x in chunks]  14.7 us
    ppermute x4, starting transfers between devices, over_head(): lax.ppermute(x, 'head', [(i, to[0] * 2 + to[1]) for i, to in ((i, move(*x...  9.78 us
    ppermute x6, waiting for transfers between devices, over_ctx(): return [lax.ppermute(x, ('ctx', 'head'), pairs) for x in chunks]  7.94 us
    pallas_call x2, Pallas kernels, on_device(): call(functools.partial(local_kernel, p * half, half), f32(half * DV, TOK)...  4.3 us
    ppermute x4, waiting for transfers between devices, over_head(): lax.ppermute(x, 'head', [(i, to[0] * 2 + to[1]) for i, to in ((i, move(*x...  2.87 us
    pallas_call x1, Pallas kernels, on_device(): call(summary_kernel, [state] * CHUNKS + [bf16(TOK, HEADS * DK), bf16(HEAD...  1.83 us
    pallas_call x1, Pallas kernels, on_device(): call(norm_kernel, bf16(TOK, HEADS * DV), 5, 'norm', 1000000, 1500000, out...  0.93 us
  transfers between devices with their start and end apart: 10, of which 8 were waited for; matrix products, arithmetic and copies ran while one was open for 0% of the time, Pallas kernels for 12%

profile of v7, /device:TPU:1, one launch (start us, length us, event | category | flops | bytes accessed | tf_op | source)
XLA Modules:
  0.0 43.8 jit_solution(17475225361428647793)
XLA Ops:
  0.0 0.0 copy-start.1
  0.0 1.8 %summary.1 = (f32[256,128]{1,0:T(8,128)S(1)}, bf16[1024,512]{1,0:T(8,128)(2,1)S(1)}, bf16[256,1024]{1,0:T(8,128)(2,1)S(1)}) custom-call(bf16[1024,512]{1,0:T(8,128)(2,1)} %k_hbm.1, bf16[1024,256]{1,0:T(8,128)(2,1)} %v_hbm.1), custom_call_target="tpu_custom_call" | custom-call | flops 268000000 | bytes 3200000 | tf_op jit(solution)/shard_map/summary/pallas_call | solution.py:250
  1.8 2.6 %collective-permute-start = (f32[256,128]{1,0:T(8,128)S(1)}, f32[256,128]{1,0:T(8,128)S(1)}, u32[]{:S(2)}, u32[]{:S(2)}) collective-permute-start(f32[256,128]{1,0:T(8,128)S(1)} %get-tuple-element.14), channel_id=1, source_target_pairs={{0,8},{1,9},{2,10},{3,11},{4,12},{5,13},{6,14},{7,15},{8,0},{9,1},... | collective-permute-start | bytes 393224 | tf_op jit(solution)/shard_map/ppermute | solution.py:245
  4.4 0.0 copy-done.1
  4.4 0.0 copy-done
  4.4 2.2 %local0.1.refs_3_ = f32[128,1024]{1,0:T(8,128)S(1)} custom-call(bf16[1024,512]{1,0:T(8,128)(2,1)S(1)} %copy-done, bf16[1024,512]{1,0:T(8,128)(2,1)S(1)} %get-tuple-element.15.k_ref, bf16[256,1024]{1,0:T(8,128)(2,1)S(1)} %get-tuple-element.16.vt_ref, s32[10,4,1024]{2,1,0:T(4,128)S(1)} %copy-done.1), custom_call_target="tpu_custom_call" | custom-call | flops 1000000000 | bytes 2000000 | tf_op jit(solution)/shard_map/local0/pallas_call | solution.py:268
  6.6 0.2 collective-permute-done.refs_0_
  6.8 4.8 %collective-permute-start.1 = (f32[256,128]{1,0:T(8,128)S(1)}, f32[256,128]{1,0:T(8,128)S(1)}, u32[]{:S(2)}, u32[]{:S(2)}) collective-permute-start(f32[256,128]{1,0:T(8,128)S(1)} %add.12), channel_id=1, source_target_pairs={{0,24},{1,25},{2,26},{3,27},{4,28},{5,29},{6,30},{7,31},{8,16},{9,... | collective-permute-start | bytes 393224 | tf_op jit(solution)/shard_map/ppermute | solution.py:245
  11.6 2.2 %local1.1.refs_4_ = f32[128,1024]{1,0:T(8,128)S(1)} custom-call(bf16[1024,512]{1,0:T(8,128)(2,1)S(1)} %copy-done, bf16[1024,512]{1,0:T(8,128)(2,1)S(1)} %get-tuple-element.15.k_ref, bf16[256,1024]{1,0:T(8,128)(2,1)S(1)} %get-tuple-element.16.vt_ref, s32[10,4,1024]{2,1,0:T(4,128)S(1)} %copy-done.1), custom_call_target="tpu_custom_call" | custom-call | flops 1000000000 | bytes 2000000 | tf_op jit(solution)/shard_map/local1/pallas_call | solution.py:268
  13.7 0.3 collective-permute-done.1.refs_1_
  14.1 4.6 %collective-permute-start.2 = (f32[256,128]{1,0:T(8,128)S(1)}, f32[256,128]{1,0:T(8,128)S(1)}, u32[]{:S(2)}, u32[]{:S(2)}) collective-permute-start(f32[256,128]{1,0:T(8,128)S(1)} %add.13), channel_id=1, source_target_pairs={{0,56},{1,57},{2,58},{3,59},{4,60},{5,61},{6,62},{7,63},{8,48},{9,... | collective-permute-start | bytes 393224 | tf_op jit(solution)/shard_map/ppermute | solution.py:245
  18.6 3.8 %collective-permute-done.2.refs_2_ = f32[256,128]{1,0:T(8,128)S(1)} collective-permute-done((f32[256,128]{1,0:T(8,128)S(1)}, f32[256,128]{1,0:T(8,128)S(1)}, u32[]{:S(2)}, u32[]{:S(2)}) %collective-permute-start.2) | collective-permute-done | bytes 131104 | tf_op jit(solution)/shard_map/ppermute | solution.py:245
  22.4 2.0 %collective-permute-start.5 = (f32[256,128]{1,0:T(8,128)S(1)}, f32[256,128]{1,0:T(8,128)S(1)}, u32[]{:S(2)}, u32[]{:S(2)}) collective-permute-start(f32[256,128]{1,0:T(8,128)S(1)} %add.14), channel_id=1, source_target_pairs={{0,128},{1,129},{2,130},{3,131},{4,132},{5,133},{6,134},{7,135},{8... | collective-permute-start | bytes 393224 | tf_op jit(solution)/shard_map/ppermute | solution.py:245
  24.4 0.8 %collective-permute-start.4 = (f32[256,128]{1,0:T(8,128)S(1)}, f32[256,128]{1,0:T(8,128)S(1)}, u32[]{:S(2)}, u32[]{:S(2)}) collective-permute-start(f32[256,128]{1,0:T(8,128)S(1)} %add.14), channel_id=1, source_target_pairs={{0,192},{1,193},{2,194},{3,195},{4,196},{5,197},{6,198},{7,199},{8... | collective-permute-start | bytes 393224 | tf_op jit(solution)/shard_map/ppermute | solution.py:245
  25.2 0.0 collective-permute-start.3
  25.2 0.6 %far012.1.refs_3_ = f32[256,1024]{1,0:T(8,128)S(1)} custom-call(bf16[1024,512]{1,0:T(8,128)(2,1)S(1)} %copy-done, s32[10,4,1024]{2,1,0:T(4,128)S(1)} %copy-done.1, f32[256,128]{1,0:T(8,128)S(1)} %collective-permute-done.refs_0_, f32[256,128]{1,0:T(8,128)S(1)} %collective-permute-done.1.refs_1_, f32[256,128]{1,0:T(8,128)S(1)} %collective-permute-done.2.refs_2_, ...), custom_call_target="tpu_custom_call" | custom-call | flops 268000000 | bytes 3000000 | tf_op jit(solution)/shard_map/far012/pallas_call | solution.py:298
  25.8 1.8 %collective-permute-done.5.refs_2_ = f32[256,128]{1,0:T(8,128)S(1)} collective-permute-done((f32[256,128]{1,0:T(8,128)S(1)}, f32[256,128]{1,0:T(8,128)S(1)}, u32[]{:S(2)}, u32[]{:S(2)}) %collective-permute-start.5) | collective-permute-done | bytes 131104 | tf_op jit(solution)/shard_map/ppermute | solution.py:245
  27.5 1.9 %collective-permute-done.4.refs_1_ = f32[256,128]{1,0:T(8,128)S(1)} collective-permute-done((f32[256,128]{1,0:T(8,128)S(1)}, f32[256,128]{1,0:T(8,128)S(1)}, u32[]{:S(2)}, u32[]{:S(2)}) %collective-permute-start.4) | collective-permute-done | bytes 131104 | tf_op jit(solution)/shard_map/ppermute | solution.py:245
  29.4 0.0 collective-permute-done.3.refs_0_
  29.4 0.5 %last.1 = (f32[256,1024]{1,0:T(8,128)S(1)}, f32[8,128]{1,0:T(8,128)S(1)}) custom-call(bf16[1024,512]{1,0:T(8,128)(2,1)S(1)} %copy-done, s32[10,4,1024]{2,1,0:T(4,128)S(1)} %copy-done.1, f32[256,128]{1,0:T(8,128)S(1)} %collective-permute-done.3.refs_0_, f32[256,128]{1,0:T(8,128)S(1)} %collective-permute-done.4.refs_1_, ...), custom_call_target="tpu_custom_call" | custom-call | flops 67000000 | bytes 3000000 | tf_op jit(solution)/shard_map/last/pallas_call | solution.py:306
  29.9 0.0 copy-start.2
  29.9 5.4 %collective-permute-start.6 = (f32[8,128]{1,0:T(8,128)S(1)}, f32[8,128]{1,0:T(8,128)S(1)}, u32[]{:S(2)}, u32[]{:S(2)}) collective-permute-start(f32[8,128]{1,0:T(8,128)S(1)} %get-tuple-element.22), channel_id=1, source_target_pairs={{0,1},{1,0},{2,3},{3,2},{4,5},{5,4},{6,7},{7,6},{8,9},{9,8},{10,11... | collective-permute-start | bytes 12296 | tf_op jit(solution)/shard_map/ppermute | solution.py:315
  35.4 0.8 %collective-permute-done.6 = f32[8,128]{1,0:T(8,128)S(1)} collective-permute-done((f32[8,128]{1,0:T(8,128)S(1)}, f32[8,128]{1,0:T(8,128)S(1)}, u32[]{:S(2)}, u32[]{:S(2)}) %collective-permute-start.6) | collective-permute-done | bytes 4128 | tf_op jit(solution)/shard_map/ppermute | solution.py:315
  36.2 2.7 %collective-permute-start.7 = (f32[8,128]{1,0:T(8,128)S(1)}, f32[8,128]{1,0:T(8,128)S(1)}, u32[]{:S(2)}, u32[]{:S(2)}) collective-permute-start(f32[8,128]{1,0:T(8,128)S(1)} %add.15.s0), channel_id=1, source_target_pairs={{0,3},{1,6},{2,1},{3,4},{4,7},{5,2},{6,5},{7,0},{8,11},{9,14},{10,... | collective-permute-start | bytes 12296 | tf_op jit(solution)/shard_map/ppermute | solution.py:315
  38.9 0.5 %collective-permute-start.8 = (f32[8,128]{1,0:T(8,128)S(1)}, f32[8,128]{1,0:T(8,128)S(1)}, u32[]{:S(2)}, u32[]{:S(2)}) collective-permute-start(f32[8,128]{1,0:T(8,128)S(1)} %add.15.s0), channel_id=1, source_target_pairs={{0,4},{1,5},{2,6},{3,7},{4,0},{5,1},{6,2},{7,3},{8,12},{9,13},{10,... | collective-permute-start | bytes 12296 | tf_op jit(solution)/shard_map/ppermute | solution.py:315
  39.4 0.2 collective-permute-done.7.s1
  39.7 1.1 %collective-permute-start.9 = (f32[8,128]{1,0:T(8,128)S(1)}, f32[8,128]{1,0:T(8,128)S(1)}, u32[]{:S(2)}, u32[]{:S(2)}) collective-permute-start(f32[8,128]{1,0:T(8,128)S(1)} %collective-permute-done.7.s1), channel_id=1, source_target_pairs={{0,1},{1,0},{2,3},{3,2},{4,5},{5,4},{6,7},{7,6},{8,9},{9,8},{10,11... | collective-permute-start | bytes 12296 | tf_op jit(solution)/shard_map/ppermute | solution.py:315
  40.8 0.0 copy-done.2
  40.8 0.3 gain.1.m_ref
  41.0 1.8 %collective-permute-done.8.s2 = f32[8,128]{1,0:T(8,128)S(1)} collective-permute-done((f32[8,128]{1,0:T(8,128)S(1)}, f32[8,128]{1,0:T(8,128)S(1)}, u32[]{:S(2)}, u32[]{:S(2)}) %collective-permute-start.8) | collective-permute-done | bytes 4128 | tf_op jit(solution)/shard_map/ppermute | solution.py:315
  42.9 0.0 collective-permute-done.9.s3
  42.9 0.9 %norm.1 = bf16[1024,256]{1,0:T(8,128)(2,1)} custom-call(f32[256,1024]{1,0:T(8,128)S(1)} %gain.1.m_ref, f32[8,128]{1,0:T(8,128)S(1)} %add.15.s0, f32[8,128]{1,0:T(8,128)S(1)} %collective-permute-done.7.s1, f32[8,128]{1,0:T(8,128)S(1)} %collective-permute-done.8.s2, f32[8,128]{1,0:T(8,128)S(1)} %collective-permute-done.9.s3), custom_call_target="tpu_custom_call" | custom-call | flops 1000000 | bytes 1500000 | tf_op jit(solution)/shard_map/norm/pallas_call | solution.py:324
  (6 shorter events, 0.1 us)
Async XLA Ops:
  0.0 4.4 %copy-start.1 = (s32[10,4,1024]{2,1,0:T(4,128)S(1)}, s32[10,4,1024]{2,1,0:T(4,128)}, u32[]{:S(2)}) copy-start(s32[10,4,1024]{2,1,0:T(4,128)} %li_ref.7) | copy-start | bytes 491524
  0.0 4.4 %copy-start = (bf16[1024,512]{1,0:T(8,128)(2,1)S(1)}, bf16[1024,512]{1,0:T(8,128)(2,1)}, u32[]{:S(2)}) copy-start(bf16[1024,512]{1,0:T(8,128)(2,1)} %q_ref.7) | copy-start | bytes 3145732
  1.8 4.9 %collective-permute-start = (f32[256,128]{1,0:T(8,128)S(1)}, f32[256,128]{1,0:T(8,128)S(1)}, u32[]{:S(2)}, u32[]{:S(2)}) collective-permute-start(f32[256,128]{1,0:T(8,128)S(1)} %get-tuple-element.14), channel_id=1, source_target_pairs={{0,8},{1,9},{2,10},{3,11},{4,12},{5,13},{6,14},{7,15},{8,0},{9,1},... | collective-permute-start | bytes 393224 | tf_op jit(solution)/shard_map/ppermute | solution.py:245
  6.8 7.3 %collective-permute-start.1 = (f32[256,128]{1,0:T(8,128)S(1)}, f32[256,128]{1,0:T(8,128)S(1)}, u32[]{:S(2)}, u32[]{:S(2)}) collective-permute-start(f32[256,128]{1,0:T(8,128)S(1)} %add.12), channel_id=1, source_target_pairs={{0,24},{1,25},{2,26},{3,27},{4,28},{5,29},{6,30},{7,31},{8,16},{9,... | collective-permute-start | bytes 393224 | tf_op jit(solution)/shard_map/ppermute | solution.py:245
  14.1 8.3 %collective-permute-start.2 = (f32[256,128]{1,0:T(8,128)S(1)}, f32[256,128]{1,0:T(8,128)S(1)}, u32[]{:S(2)}, u32[]{:S(2)}) collective-permute-start(f32[256,128]{1,0:T(8,128)S(1)} %add.13), channel_id=1, source_target_pairs={{0,56},{1,57},{2,58},{3,59},{4,60},{5,61},{6,62},{7,63},{8,48},{9,... | collective-permute-start | bytes 393224 | tf_op jit(solution)/shard_map/ppermute | solution.py:245
  22.4 5.1 %collective-permute-start.5 = (f32[256,128]{1,0:T(8,128)S(1)}, f32[256,128]{1,0:T(8,128)S(1)}, u32[]{:S(2)}, u32[]{:S(2)}) collective-permute-start(f32[256,128]{1,0:T(8,128)S(1)} %add.14), channel_id=1, source_target_pairs={{0,128},{1,129},{2,130},{3,131},{4,132},{5,133},{6,134},{7,135},{8... | collective-permute-start | bytes 393224 | tf_op jit(solution)/shard_map/ppermute | solution.py:245
  24.4 5.0 %collective-permute-start.4 = (f32[256,128]{1,0:T(8,128)S(1)}, f32[256,128]{1,0:T(8,128)S(1)}, u32[]{:S(2)}, u32[]{:S(2)}) collective-permute-start(f32[256,128]{1,0:T(8,128)S(1)} %add.14), channel_id=1, source_target_pairs={{0,192},{1,193},{2,194},{3,195},{4,196},{5,197},{6,198},{7,199},{8... | collective-permute-start | bytes 393224 | tf_op jit(solution)/shard_map/ppermute | solution.py:245
  25.2 4.3 %collective-permute-start.3 = (f32[256,128]{1,0:T(8,128)S(1)}, f32[256,128]{1,0:T(8,128)S(1)}, u32[]{:S(2)}, u32[]{:S(2)}) collective-permute-start(f32[256,128]{1,0:T(8,128)S(1)} %add.14), channel_id=1, source_target_pairs={{0,64},{1,65},{2,66},{3,67},{4,68},{5,69},{6,70},{7,71},{8,72},{9,... | collective-permute-start | bytes 393224 | tf_op jit(solution)/shard_map/ppermute | solution.py:245
  29.9 10.8 %copy-start.2 = (bf16[256]{0:T(256)(128)(2,1)S(1)}, bf16[256]{0:T(256)(128)(2,1)}, u32[]{:S(2)}) copy-start(bf16[256]{0:T(256)(128)(2,1)} %param.8) | copy-start | bytes 1540
  29.9 6.2 %collective-permute-start.6 = (f32[8,128]{1,0:T(8,128)S(1)}, f32[8,128]{1,0:T(8,128)S(1)}, u32[]{:S(2)}, u32[]{:S(2)}) collective-permute-start(f32[8,128]{1,0:T(8,128)S(1)} %get-tuple-element.22), channel_id=1, source_target_pairs={{0,1},{1,0},{2,3},{3,2},{4,5},{5,4},{6,7},{7,6},{8,9},{9,8},{10,11... | collective-permute-start | bytes 12296 | tf_op jit(solution)/shard_map/ppermute | solution.py:315
  36.2 3.5 %collective-permute-start.7 = (f32[8,128]{1,0:T(8,128)S(1)}, f32[8,128]{1,0:T(8,128)S(1)}, u32[]{:S(2)}, u32[]{:S(2)}) collective-permute-start(f32[8,128]{1,0:T(8,128)S(1)} %add.15.s0), channel_id=1, source_target_pairs={{0,3},{1,6},{2,1},{3,4},{4,7},{5,2},{6,5},{7,0},{8,11},{9,14},{10,... | collective-permute-start | bytes 12296 | tf_op jit(solution)/shard_map/ppermute | solution.py:315
  38.9 4.0 %collective-permute-start.8 = (f32[8,128]{1,0:T(8,128)S(1)}, f32[8,128]{1,0:T(8,128)S(1)}, u32[]{:S(2)}, u32[]{:S(2)}) collective-permute-start(f32[8,128]{1,0:T(8,128)S(1)} %add.15.s0), channel_id=1, source_target_pairs={{0,4},{1,5},{2,6},{3,7},{4,0},{5,1},{6,2},{7,3},{8,12},{9,13},{10,... | collective-permute-start | bytes 12296 | tf_op jit(solution)/shard_map/ppermute | solution.py:315
  39.7 3.2 %collective-permute-start.9 = (f32[8,128]{1,0:T(8,128)S(1)}, f32[8,128]{1,0:T(8,128)S(1)}, u32[]{:S(2)}, u32[]{:S(2)}) collective-permute-start(f32[8,128]{1,0:T(8,128)S(1)} %collective-permute-done.7.s1), channel_id=1, source_target_pairs={{0,1},{1,0},{2,3},{3,2},{4,5},{5,4},{6,7},{7,6},{8,9},{9,8},{10,11... | collective-permute-start | bytes 12296 | tf_op jit(solution)/shard_map/ppermute | solution.py:315
